TPU v7x, 32 devices: a whole 2x2x4 slice. The times are simulated.
32 devices in a mesh: req: 8 (over z, x), kv: 4 (over y, core).
Axes of the slice: x: 2, y: 2, z: 4, core: 2. Of those that a mesh axis runs over, the one named last changes fastest.
Arguments:
- hidden: bfloat16 [32, 5120], P('kv', 'req'), may hold values from -120 to 120
- gain: bfloat16 [5120], P('req'), may hold values from 0.5 to 1.5
- w_query: bfloat16 [5120, 5120], P('req', 'kv'), may hold values from -0.078125 to 0.078125
- w_key: bfloat16 [5120, 1024], P('req', 'kv'), may hold values from -0.078125 to 0.078125
- w_value: bfloat16 [5120, 1024], P('req', 'kv'), may hold values from -0.078125 to 0.078125
- b_query: bfloat16 [5120], P('kv'), may hold values from -3 to 3
- b_key: bfloat16 [1024], P('kv'), may hold values from -3 to 3
- b_value: bfloat16 [1024], P('kv'), may hold values from -3 to 3
- w_output: bfloat16 [5120, 5120], P('kv', 'req'), may hold values from -0.5 to 0.5
- key_cache: bfloat16 [32, 8, 4096, 128], P('req', 'kv'), may hold values from -160 to 160
- value_cache: bfloat16 [32, 8, 4096, 128], P('req', 'kv'), may hold values from -9 to 9
- sink_keys: bfloat16 [32, 8, 4, 128], P('req', 'kv'), may hold values from -6 to 6
- sink_values: bfloat16 [32, 8, 4, 128], P('req', 'kv'), may hold values from -9 to 9
- lengths: int32 [32], P('req'), may hold values from 4 to 8192, as said below
- sink_count: int32 [32], P('req'), may hold values from 0 to 4, as said below
- window: int32 [32], P('req'), may hold values from 1024 to 4096, as said below
Outputs:
- attn_out: bfloat16 [32, 5120], P('kv', 'req')
Inputs may be any that keep to these rules, and one draw needn't show every extreme that they name: `lengths`: exactly 2 requests have length 8192; the others are heavy-tailed below it. `sink_count`: some request keeps 4. Some request has window 4096.
All inputs are finite; a program needn't handle non-finite values.
Results may differ from a plain program's by a relative error of at most 0.012.
The roundings to bfloat16 on the way count: a program that leaves them out, or rounds other values in their place, can miss the bound.
Values may be sent and summed in bfloat16 or wider, within the bound.
No kernel may reach another device: no remote copies, remote signals or barrier semaphores. Data moves between devices by JAX's collectives and lax.ppermute only.
A program may use at most 64 MiB of HBM per device.

v0:
```python
import math

import jax
import jax.numpy as jnp
from jax import lax
from jax.sharding import PartitionSpec as P

D = 5120
CYCLE = 4096
SINKS = 4


def rotate(window_values, positions):
    half = window_values.shape[-1] // 2
    freq = jnp.power(
        1000000.0, -2.0 * jnp.arange(half, dtype=jnp.float32) / window_values.shape[-1]
    )
    angle = positions[..., None] * freq
    cosine = jnp.cos(angle)
    sine = jnp.sin(angle)
    first = window_values[..., :half]
    second = window_values[..., half:]
    return jnp.concatenate([first * cosine - second * sine, second * cosine + first * sine], -1)


def live_slots(size, lengths, sink_count, window):
    cycle = CYCLE
    slot = jnp.arange(size, dtype=jnp.int32)
    cache_length = lengths[:, None]
    place = slot[None, :] + cycle * ((cache_length - 1 - slot[None, :]) // cycle)
    floor_at = jnp.maximum(sink_count, lengths - window)[:, None]
    live = (slot[None, :] < cache_length) & (place >= floor_at)
    return live[:, None, None, :]


def on_device(
    hidden,
    gain,
    w_query,
    w_key,
    w_value,
    b_query,
    b_key,
    b_value,
    w_output,
    key_cache,
    value_cache,
    sink_keys,
    sink_values,
    lengths,
    sink_count,
    window,
):
    gathered = lax.all_gather(hidden, "kv", axis=0, tiled=True)
    xf = gathered.astype(jnp.float32)
    partial_value = jnp.sum(xf * xf, 1)
    scaled = (xf * gain.astype(jnp.float32)).astype(jnp.bfloat16)
    count_req = lengths.shape[0]
    own = partial_value[:count_req]
    totals = lax.psum(partial_value, "req")
    own = lax.dynamic_slice_in_dim(totals, lax.axis_index("req") * count_req, count_req)
    q_cols = w_query.shape[1]

    def make_term(weight):
        product = jnp.dot(scaled, weight, preferred_element_type=jnp.float32)
        return product

    q_wide = lax.psum_scatter(make_term(w_query), "req", scatter_dimension=0, tiled=True)
    k_sum = lax.psum_scatter(make_term(w_key), "req", scatter_dimension=0, tiled=True)
    v_sum = lax.psum_scatter(make_term(w_value), "req", scatter_dimension=0, tiled=True)
    inv_rms = lax.rsqrt(own / D + 1e-06)
    query_vector = inv_rms[:, None] * q_wide + b_query.astype(jnp.float32)
    fresh_key = inv_rms[:, None] * k_sum + b_key.astype(jnp.float32)
    value_f = inv_rms[:, None] * v_sum + b_value.astype(jnp.float32)
    heads_kv = key_cache.shape[1]
    head_size = key_cache.shape[3]
    group = q_cols // (heads_kv * head_size)
    positions = lengths.astype(jnp.float32)[:, None]
    q_rot = (
        rotate(query_vector.reshape(count_req, heads_kv * group, head_size), positions)
        .astype(jnp.bfloat16)
        .reshape(count_req, heads_kv, group, head_size)
    )
    k_rot = rotate(fresh_key.reshape(count_req, heads_kv, head_size), positions).astype(
        jnp.bfloat16
    )
    fresh_value = value_f.reshape(count_req, heads_kv, head_size).astype(jnp.bfloat16)
    score_scale = 1.0 / math.sqrt(head_size)
    sink_score = (
        jnp.einsum("rkgd,rksd->rkgs", q_rot, sink_keys, preferred_element_type=jnp.float32)
        * score_scale
    )
    s_self = (
        jnp.sum(q_rot.astype(jnp.float32) * k_rot.astype(jnp.float32)[:, :, None, :], -1)
        * score_scale
    )
    sink_live = (
        jnp.arange(SINKS, dtype=jnp.int32)[None, :] < jnp.minimum(sink_count, lengths)[:, None]
    )[:, None, None, :]
    top_start = jnp.maximum(jnp.max(jnp.where(sink_live, sink_score, -jnp.inf), -1), s_self)
    cycle = key_cache.shape[2]
    scores = (
        jnp.einsum("rkgd,rksd->rkgs", q_rot, key_cache, preferred_element_type=jnp.float32)
        * score_scale
    )
    scores = jnp.where(live_slots(cycle, lengths, sink_count, window), scores, -jnp.inf)
    top = jnp.maximum(top_start, jnp.max(scores, -1))
    e_sink_now = jnp.where(sink_live, jnp.exp(sink_score - top[..., None]), 0.0)
    e_self = jnp.exp(s_self - top)
    total = jnp.sum(e_sink_now, -1) + e_self
    numer = jnp.einsum(
        "rkgs,rksd->rkgd",
        e_sink_now.astype(jnp.bfloat16),
        sink_values,
        preferred_element_type=jnp.float32,
    )
    numer = (
        numer
        + e_self.astype(jnp.bfloat16).astype(jnp.float32)[..., None]
        * fresh_value.astype(jnp.float32)[:, :, None, :]
    )
    accumulate_total = total
    accumulate_numer = numer
    weights = jnp.where(scores > -jnp.inf, jnp.exp(scores - top[..., None]), 0.0)
    accumulate_numer = accumulate_numer + jnp.einsum(
        "rkgs,rksd->rkgd",
        weights.astype(jnp.bfloat16),
        value_cache,
        preferred_element_type=jnp.float32,
    )
    total = accumulate_total + jnp.sum(weights, -1)
    context = (accumulate_numer / total[..., None]).astype(jnp.bfloat16).reshape(count_req, q_cols)
    partial_out = jnp.dot(
        lax.all_gather(context, "req", axis=0, tiled=True),
        w_output,
        preferred_element_type=jnp.float32,
    )
    return lax.psum_scatter(partial_out, "kv", scatter_dimension=0, tiled=True).astype(jnp.bfloat16)


def solution(mesh):
    in_specs = (
        P("kv", "req"),
        P("req"),
        P("req", "kv"),
        P("req", "kv"),
        P("req", "kv"),
        P("kv"),
        P("kv"),
        P("kv"),
        P("kv", "req"),
        P("req", "kv", None, None),
        P("req", "kv", None, None),
        P("req", "kv", None, None),
        P("req", "kv", None, None),
        P("req"),
        P("req"),
        P("req"),
    )
    out_specs = P("kv", "req")
    return jax.shard_map(
        on_device, mesh=mesh, in_specs=in_specs, out_specs=out_specs, check_vma=False
    )
```

profile of v0, /device:TPU:0, one launch (start us, length us, event | category | flops | bytes accessed | tf_op | source)
XLA Modules:
  0.0 220.9 jit_solution(9797267069841844137)
XLA Ops:
  6.5 0.0 copy-start
  6.5 0.0 all-reduce.10.cloned.1.call-start
  6.5 0.8 convert_element_type.83
  7.3 6.4 %all_gather.6 = bf16[32,640]{1,0:T(8,128)(2,1)S(1)} all-gather(bf16[8,640]{1,0:T(8,128)(2,1)} %param.16), channel_id=1, replica_groups=mesh['req'=8,'kv'=4] {'kv'}, dimensions={0}, use_global_device_ids=true | all-gather | bytes 51200 | tf_op jit(solution)/shard_map/all_gather | solution.py:54
  13.8 0.6 fusion.11
  14.4 1.8 fusion.22
  16.1 1.8 fusion.20
  17.9 0.0 all-reduce.10.cloned.1.call-update
  17.9 0.0 all-reduce.8.cloned.1.call-start
  18.0 0.0 copy-done
  18.0 1.0 fusion.24
  19.0 0.0 all-reduce.8.cloned.1.call-update
  19.0 1.3 dynamic-slice.6
  20.3 1.3 dynamic-slice
  21.6 0.7 convert_element_type.88
  22.3 0.7 convert_element_type.93
  22.9 0.7 fusion.40
  23.7 0.1 iota_compare_fusion.1
  23.7 0.7 convert_element_type.85
  25.8 0.1 multiply_cosine_fusion
  25.9 0.8 fusion.19
  26.7 62.5 %all-reduce.10.cloned.1.call-done = (f32[32,256]{1,0:T(8,128)}, f32[32]{0:T(128)}, f32[32,256]{1,0:T(8,128)}) async-done(((f32[32,256]{1,0:T(8,128)}, f32[32]{0:T(128)}, f32[32,256]{1,0:T(8,128)}), (f32[32,256]{1,0:T(8,128)}, f32[32]{0:T(128)}, f32[32,256]{1,0:T(8,128)})) %all-reduce.10.cloned.1.call-update) | async-done | bytes 65680
  89.2 0.7 add_rsqrt_fusion
  89.9 0.8 fusion.35
  90.7 0.1 subtract_convert_fusion.1
  90.8 0.1 maximum_convert_fusion
  90.9 71.0 %all-reduce.8.cloned.1.call-done = f32[32,1280]{1,0:T(8,128)} async-done(((f32[32,1280]{1,0:T(8,128)}), f32[32,1280]{1,0:T(8,128)}) %all-reduce.8.cloned.1.call-update) | async-done | bytes 163856
  161.9 0.9 fusion.26
  162.8 0.0 slice-start
  162.8 0.1 subtract_convert_fusion
  162.9 0.0 copy-start.3
  162.9 0.2 multiply_reduce_fusion
  163.1 0.0 slice-start.1
  163.1 6.0 %fusion.41 = (f32[4,2,5]{2,1,0:T(2,128)S(1)}, f32[4,2,5,4096]{3,2,1,0:T(8,128)S(1)}) fusion(bf16[4,2,4096,128]{3,2,1,0:T(8,128)(2,1)} %param.25, bf16[4,2,5,64]{3,2,1,0:T(8,128)(2,1)S(1)} %copy.24, bf16[4,2,5,64]{3,2,1,0:T(8,128)(2,1)S(1)} %copy.23, pred[4,4096]{1,0:T(4,128)(4,1)S(1)} %fusion.19), kind=kOutput, calls=%fused_computation.76 | convolution fusion | flops 42455000 | bytes 9070752 | tf_op jit(solution)/shard_map/rkgd,rksd->rkgs/dot_general | solution.py:103
  169.1 0.2 fusion.9
  169.3 0.0 copy-done.2
  169.3 0.2 select_reduce_fusion
  169.5 0.1 fusion.27
  169.6 0.4 fusion.3
  170.0 0.0 copy-done.3
  170.1 0.2 convolution_add_fusion.1
  170.3 0.0 slice-done
  170.3 0.0 slice-done.1
  170.3 1.3 fusion.2
  171.6 30.5 %all-gather = bf16[8,4,1280]{2,1,0:T(4,128)(2,1)S(1)} all-gather(bf16[1,4,1280]{2,1,0:T(4,128)(2,1)S(1)} %reshape.226), channel_id=1, replica_groups=mesh['req'=8,'kv'=4] {'req'}, dimensions={0}, use_global_device_ids=true | all-gather | bytes 92160 | tf_op jit(solution)/shard_map/all_gather | solution.py:134
  202.2 0.4 fusion.42
  202.6 10.9 %all-reduce.3 = bf16[32,640]{1,0:T(8,128)(2,1)S(1)} all-reduce(f32[32,640]{1,0:T(8,128)S(1)} %fusion.42), channel_id=5, replica_groups=mesh['req'=8,'kv'=4] {'kv'}, use_global_device_ids=true, to_apply=%region_10.11.clone | all-reduce | flops 20480 | bytes 122880
  213.5 0.6 dynamic-slice_convert_fusion
  (16 shorter events, 0.2 us)
Async XLA Ops:
  6.5 11.4 %copy-start = (bf16[640,1280]{1,0:T(8,128)(2,1)S(1)}, bf16[640,1280]{1,0:T(8,128)(2,1)}, u32[]{:S(2)}) copy-start(bf16[640,1280]{1,0:T(8,128)(2,1)} %param.18) | copy-start | bytes 4915204
  6.5 82.7 %all-reduce.10.cloned.1.call-start = ((), (), s32[]{:S(2)}) async-start(), calls=%async_computation.1 | async-start | bytes 132096
  17.9 144.0 %all-reduce.8.cloned.1.call-start = ((), (), s32[]{:S(2)}) async-start(), calls=%async_computation | async-start | bytes 327680
  19.0 150.3 %copy-start.2 = (bf16[4,2,4,128]{3,2,1,0:T(4,128)(2,1)S(1)}, bf16[4,2,4,128]{3,2,1,0:T(4,128)(2,1)}, u32[]{:S(2)}) copy-start(bf16[4,2,4,128]{3,2,1,0:T(4,128)(2,1)} %param.27) | copy-start | bytes 24580
  162.8 7.5 %slice-start = ((s8[8388608]{0:T(1024)(128)(4,1)}), s8[4194304]{0:T(1024)(128)(4,1)S(1)}, s32[]{:S(2)}) async-start(s8[8388608]{0:T(1024)(128)(4,1)} %bitcast.13), calls=%async_computation.2 | async-start | bytes 8388608
  162.9 7.2 %copy-start.3 = (bf16[4,2,4,128]{3,2,1,0:T(4,128)(2,1)S(1)}, bf16[4,2,4,128]{3,2,1,0:T(4,128)(2,1)}, u32[]{:S(2)}) copy-start(bf16[4,2,4,128]{3,2,1,0:T(4,128)(2,1)} %param.28) | copy-start | bytes 24580
  163.1 7.2 %slice-start.1 = ((s8[8388608]{0:T(1024)(128)(4,1)}), s8[4194304]{0:T(1024)(128)(4,1)S(1)}, s32[]{:S(2)}) async-start(s8[8388608]{0:T(1024)(128)(4,1)} %bitcast.13), calls=%async_computation.3 | async-start | bytes 8388608
  169.1 33.1 %copy-start.1 = (bf16[1280,640]{1,0:T(8,128)(2,1)S(1)}, bf16[1280,640]{1,0:T(8,128)(2,1)}, u32[]{:S(2)}) copy-start(bf16[1280,640]{1,0:T(8,128)(2,1)} %param.24) | copy-start | bytes 4915204
Sparse Core Ops, SparseCore 0:
  18.0 71.1 all-reduce.9
  92.5 69.3 all-reduce.7
where the time goes:
time: 221 us
  waiting for transfers between devices  133 us (60%)
  blocking collectives  47.8 us (22%)
  between operations  14.9 us (7%)
  matrix products  12.6 us (6%)
  other arithmetic  8.74 us (4%)
  local copies, waits for them, and re-layouts  3.37 us (2%)
    unnamed x4, waiting for transfers between devices  133 us
    all_gather x1, blocking collectives, on_device(): lax.all_gather(context, 'req', axis=0, tiled=True)  30.5 us
    unnamed x1, blocking collectives  10.9 us
    all_gather x1, blocking collectives, on_device(): gathered = lax.all_gather(hidden, 'kv', axis=0, tiled=True)  6.41 us
    dot_general x1, matrix products, on_device(): jnp.einsum('rkgd,rksd->rkgs', q_rot, key_cache, preferred_element_type=jn...  5.96 us
    dot_general x3, matrix products, make_term(): product = jnp.dot(scaled, weight, preferred_element_type=jnp.float32)  4.5 us
  transfers between devices with their start and end apart: 2, of which 2 were waited for; matrix products, arithmetic and copies ran while one was open for 4% of the time, Pallas kernels for 0%

commit v1 on v0

v1 whole, which is shorter than its diff:
```python
import math

import jax
import jax.numpy as jnp
from jax import lax
from jax.experimental import pallas as pl
from jax.experimental.pallas import tpu as pltpu
from jax.sharding import PartitionSpec as P

D = 5120
SINKS = 4
EPS = 1e-06
BLOCK = 512
EXTRA = 128


def log2(n):
    bits = n.bit_length() - 1
    assert n == 1 << bits
    return bits


def stages(n):
    bits = log2(n)
    if bits == 0:
        return []
    result = [(2, 1)]
    left = bits - 1
    while left:
        take = 2 if left % 2 == 0 else 1
        left -= take
        result.append((1 << take, 2 << left))
    return result


def place_to_offset(place, n):
    bits = log2(n)
    if bits == 0:
        return place
    return ((place << 1) | (place >> (bits - 1))) & (n - 1)


def offset_to_place(offset, n):
    bits = log2(n)
    if bits == 0:
        return offset
    return (offset >> 1) | ((offset & 1) << (bits - 1))


def swap(x, axis, n, offset):
    return lax.ppermute(x, axis, [(i, i ^ offset) for i in range(n)])


def gather_blocks(x, axis, n):
    for radix, unit in reversed(stages(n)):
        x = jnp.concatenate([x] + [swap(x, axis, n, q * unit) for q in range(1, radix)], 0)
    return x


def row_order(size, rows_req, rows_kv, req, kv, to_kv):
    n_req, n_kv = size // rows_req, size // rows_kv
    shape = (size, size)
    req_row = lax.broadcasted_iota(jnp.int32, shape, 1 if to_kv else 0)
    kv_row = lax.broadcasted_iota(jnp.int32, shape, 0 if to_kv else 1)
    place = req_row >> log2(rows_req)
    owner = place_to_offset(place, n_req) ^ req
    request = (owner << log2(rows_req)) | (req_row & (rows_req - 1))
    kv_place = offset_to_place((request >> log2(rows_kv)) ^ kv, n_kv)
    kv_request = (kv_place << log2(rows_kv)) | (request & (rows_kv - 1))
    return (kv_request == kv_row).astype(jnp.bfloat16)


def project_kernel(rows_req, hidden, gain, w_query, w_key, w_value, keep, send):
    size = hidden.shape[0]
    rows_kv = size // lax.axis_size("kv")
    order = row_order(
        size, rows_req, rows_kv, lax.axis_index("req"), lax.axis_index("kv"), False
    )
    xf = jnp.dot(order, hidden[...], preferred_element_type=jnp.float32)
    scaled = (xf * gain[...].astype(jnp.float32)).astype(jnp.bfloat16)
    half = keep.shape[0]

    def put(start, block):
        width = block.shape[1]
        keep[:, start : start + width] = block[:half]
        send[:, start : start + width] = block[half:]

    at = 0
    for weight in (w_query, w_key, w_value):
        put(at, jnp.dot(scaled, weight[...], preferred_element_type=jnp.float32))
        at += weight.shape[1]
    squares = jnp.sum(xf * xf, 1, keepdims=True)
    put(at, jnp.broadcast_to(squares, (size, EXTRA)))


def attend_kernel(
    n_parts,
    lengths,
    sink_count,
    window,
    *refs,
):
    parts = refs[:n_parts]
    (
        cosine,
        sine,
        b_query,
        b_key,
        b_value,
        key_cache,
        value_cache,
        sink_keys,
        sink_values,
        context,
        k_buf,
        v_buf,
        score_buf,
        q_heads,
        k_extra,
        v_extra,
        k_sem,
        v_sem,
    ) = refs[n_parts:]
    count, heads_kv, cycle, size = key_cache.shape
    group = context.shape[1] // (heads_kv * size)
    pad = q_heads.shape[1] // heads_kv
    blocks = cycle // BLOCK
    scale = 1.0 / math.sqrt(size)

    def span(r):
        low = jnp.maximum(sink_count[r], lengths[r] - window[r])
        first = low // BLOCK
        visits = (lengths[r] - 1) // BLOCK - first + 1
        return low, first, jnp.maximum(visits, 0)

    spans = [span(r) for r in range(count)]

    def copy(cache, buf, sem, r, t):
        at = lax.rem(spans[r][1] + t, blocks)
        src = pl.ds(pl.multiple_of(at * BLOCK, BLOCK), BLOCK)
        dst = pl.ds(pl.multiple_of(t * BLOCK, BLOCK), BLOCK)
        return pltpu.make_async_copy(cache.at[r, :, src], buf.at[r, :, dst], sem.at[r, t])

    keys = (key_cache, k_buf, k_sem)
    values = (value_cache, v_buf, v_sem)
    for which in (keys, values):
        for r in range(count):

            @pl.loop(0, spans[r][2])
            def _(t):
                copy(*which, r, t).start()

    total = parts[0][...]
    for part in parts[1:]:
        total = total + part[...]
    q_cols, kv_cols = b_query.shape[1], b_key.shape[1]
    squares = total[:, q_cols + 2 * kv_cols : q_cols + 2 * kv_cols + 1]
    inv_rms = lax.rsqrt(squares / D + EPS)
    query = inv_rms * total[:, :q_cols] + b_query[...].astype(jnp.float32)
    key = inv_rms * total[:, q_cols : q_cols + kv_cols] + b_key[...].astype(jnp.float32)
    value = inv_rms * total[:, q_cols + kv_cols : q_cols + 2 * kv_cols] + b_value[...].astype(
        jnp.float32
    )
    cos, sin = cosine[...], sine[...]

    def rotated(x):
        return x * cos + pltpu.roll(x, size // 2, 1) * sin

    q_heads[...] = jnp.zeros_like(q_heads)
    k_extra[...] = jnp.zeros_like(k_extra)
    v_extra[...] = jnp.zeros_like(v_extra)
    for h in range(heads_kv):
        lanes = slice(h * size, (h + 1) * size)
        for g in range(group):
            head = h * group + g
            block = rotated(query[:, head * size : (head + 1) * size])
            for r in range(count):
                q_heads[r, h * pad + g : h * pad + g + 1, lanes] = block[r : r + 1]
        k_rot = rotated(key[:, lanes])
        for r in range(count):
            k_extra[r, 0:SINKS, lanes] = sink_keys[r, h].astype(jnp.float32)
            v_extra[r, 0:SINKS, lanes] = sink_values[r, h].astype(jnp.float32)
            k_extra[r, SINKS : SINKS + 1, lanes] = k_rot[r : r + 1]
            v_extra[r, SINKS : SINKS + 1, lanes] = value[r : r + 1, lanes]

    contract_last = (((1,), (1,)), ((), ()))
    lane = lax.broadcasted_iota(jnp.int32, (1, EXTRA), 1)
    offset = lax.broadcasted_iota(jnp.int32, (1, BLOCK), 1)
    for r in range(count):
        length = lengths[r]
        low, first, visits = spans[r]
        q = q_heads[r].astype(jnp.bfloat16)
        extra = (
            lax.dot_general(
                q,
                k_extra[r].astype(jnp.bfloat16),
                contract_last,
                preferred_element_type=jnp.float32,
            )
            * scale
        )
        live = (lane < jnp.minimum(sink_count[r], length)) | (lane == SINKS)
        extra = jnp.where(live, extra, -jnp.inf)

        def both(buf, t):
            rows = pl.ds(pl.multiple_of(t * BLOCK, BLOCK), BLOCK)
            return jnp.concatenate([buf[r, h, rows] for h in range(heads_kv)], 1)

        def score(t, top):
            copy(*keys, r, t).wait()
            s = (
                lax.dot_general(
                    q, both(k_buf, t), contract_last, preferred_element_type=jnp.float32
                )
                * scale
            )
            position = (first + t) * BLOCK + offset
            s = jnp.where((position >= low) & (position < length), s, -jnp.inf)
            score_buf[t] = s
            return jnp.maximum(top, jnp.max(s, 1, keepdims=True))

        top = lax.fori_loop(0, visits, score, jnp.max(extra, 1, keepdims=True))
        weights = jnp.exp(extra - top)
        denom = jnp.sum(weights, 1, keepdims=True)
        numer = jnp.dot(
            weights.astype(jnp.bfloat16),
            v_extra[r].astype(jnp.bfloat16),
            preferred_element_type=jnp.float32,
        )

        def mix(t, carry):
            denom, numer = carry
            copy(*values, r, t).wait()
            weights = jnp.exp(score_buf[t] - top)
            denom = denom + jnp.sum(weights, 1, keepdims=True)
            numer = numer + jnp.dot(
                weights.astype(jnp.bfloat16), both(v_buf, t), preferred_element_type=jnp.float32
            )
            return denom, numer

        denom, numer = lax.fori_loop(0, visits, mix, (denom, numer))
        result = (numer / denom).astype(jnp.bfloat16).astype(jnp.float32)
        for h in range(heads_kv):
            for g in range(group):
                head = h * group + g
                context[r : r + 1, head * size : (head + 1) * size] = result[
                    h * pad + g : h * pad + g + 1, h * size : (h + 1) * size
                ]


def output_kernel(rows_kv, context, w_output, keep, send):
    size = context.shape[0]
    rows_req = size // lax.axis_size("req")
    order = row_order(
        size, rows_req, rows_kv, lax.axis_index("req"), lax.axis_index("kv"), True
    )
    rows = jnp.dot(order, context[...], preferred_element_type=jnp.float32).astype(jnp.bfloat16)
    product = jnp.dot(rows, w_output[...], preferred_element_type=jnp.float32)
    half = keep.shape[0]
    keep[...] = product[:half]
    send[...] = product[half:]


def spec(space=pltpu.VMEM):
    return pl.BlockSpec(memory_space=space)


def on_device(
    hidden,
    gain,
    w_query,
    w_key,
    w_value,
    b_query,
    b_key,
    b_value,
    w_output,
    key_cache,
    value_cache,
    sink_keys,
    sink_values,
    lengths,
    sink_count,
    window,
):
    n_req, n_kv = lax.axis_size("req"), lax.axis_size("kv")
    count, heads_kv, cycle, size = key_cache.shape
    rows_kv = hidden.shape[0]
    rows = count * n_req
    q_cols, kv_cols = w_query.shape[1], w_key.shape[1]
    group = q_cols // (heads_kv * size)
    wide = q_cols + 2 * kv_cols + EXTRA
    f32, bf16 = jnp.float32, jnp.bfloat16

    gathered = gather_blocks(hidden, "kv", n_kv)
    half = jax.ShapeDtypeStruct((rows // 2, wide), f32)
    keep, send = pl.pallas_call(
        lambda *refs: project_kernel(count, *refs),
        out_shape=(half, half),
        in_specs=[spec()] * 5,
        out_specs=(spec(), spec()),
        compiler_params=pltpu.CompilerParams(vmem_limit_bytes=16 << 20),
        name="project",
    )(gathered, gain.reshape(1, -1), w_query, w_key, w_value)

    req_stages = stages(n_req)
    received = swap(send, "req", n_req, req_stages[0][1])
    parts = [keep, received]
    for radix, unit in req_stages[1:]:
        x = sum(parts[1:], parts[0])
        chunk = x.shape[0] // radix
        parts = [x[:chunk]] + [
            swap(x[q * chunk : (q + 1) * chunk], "req", n_req, q * unit) for q in range(1, radix)
        ]

    freq = jnp.power(1000000.0, -2.0 * jnp.arange(size // 2, dtype=f32) / size)
    angle = lengths.astype(f32)[:, None] * freq
    cos, sin = jnp.cos(angle), jnp.sin(angle)
    cosine = jnp.concatenate([cos, cos], 1)
    sine = jnp.concatenate([-sin, sin], 1)

    visits = cycle // BLOCK + 1
    pad = -(-group // 8) * 8
    stored = visits * BLOCK
    context = pl.pallas_call(
        lambda *refs: attend_kernel(len(parts), *refs),
        out_shape=jax.ShapeDtypeStruct((count, q_cols), f32),
        in_specs=[spec(pltpu.SMEM)] * 3
        + [spec()] * (len(parts) + 5)
        + [spec(pl.ANY)] * 2
        + [spec()] * 2,
        out_specs=spec(),
        scratch_shapes=[
            pltpu.VMEM((count, heads_kv, stored, size), bf16),
            pltpu.VMEM((count, heads_kv, stored, size), bf16),
            pltpu.VMEM((visits, heads_kv * pad, BLOCK), f32),
            pltpu.VMEM((count, heads_kv * pad, heads_kv * size), f32),
            pltpu.VMEM((count, EXTRA, heads_kv * size), f32),
            pltpu.VMEM((count, EXTRA, heads_kv * size), f32),
            pltpu.SemaphoreType.DMA((count, visits)),
            pltpu.SemaphoreType.DMA((count, visits)),
        ],
        compiler_params=pltpu.CompilerParams(vmem_limit_bytes=32 << 20),
        name="attend",
    )(
        lengths,
        sink_count,
        window,
        *parts,
        cosine,
        sine,
        b_query.reshape(1, -1),
        b_key.reshape(1, -1),
        b_value.reshape(1, -1),
        key_cache,
        value_cache,
        sink_keys,
        sink_values,
    ).astype(bf16)

    everyone = gather_blocks(context, "req", n_req)
    half = jax.ShapeDtypeStruct((rows // 2, w_output.shape[1]), f32)
    keep, send = pl.pallas_call(
        lambda *refs: output_kernel(rows_kv, *refs),
        out_shape=(half, half),
        in_specs=[spec()] * 2,
        out_specs=(spec(), spec()),
        compiler_params=pltpu.CompilerParams(vmem_limit_bytes=16 << 20),
        name="output",
    )(everyone, w_output)
    kv_stages = stages(n_kv)
    x = keep + swap(send, "kv", n_kv, kv_stages[0][1])
    for radix, unit in kv_stages[1:]:
        chunk = x.shape[0] // radix
        parts = [x[:chunk]] + [
            swap(x[q * chunk : (q + 1) * chunk], "kv", n_kv, q * unit) for q in range(1, radix)
        ]
        x = sum(parts[1:], parts[0])
    return x.astype(bf16)


def solution(mesh):
    in_specs = (
        P("kv", "req"),
        P("req"),
        P("req", "kv"),
        P("req", "kv"),
        P("req", "kv"),
        P("kv"),
        P("kv"),
        P("kv"),
        P("kv", "req"),
        P("req", "kv", None, None),
        P("req", "kv", None, None),
        P("req", "kv", None, None),
        P("req", "kv", None, None),
        P("req"),
        P("req"),
        P("req"),
    )
    out_specs = P("kv", "req")
    return jax.shard_map(
        on_device, mesh=mesh, in_specs=in_specs, out_specs=out_specs, check_vma=False
    )
```

time: 221 us -> 66.5 us (0.30)
  waiting for transfers between devices: 133 us -> 22.3 us
  blocking collectives: 47.8 us -> 0 us
  starting transfers between devices: 0.04 us -> 17.9 us
  between operations: 14.9 us -> 0.1 us
  local copies, waits for them, and re-layouts: 3.37 us -> 16.3 us
  matrix products: 12.6 us -> 0 us
  other arithmetic: 8.74 us -> 2.92 us
  Pallas kernels: 0 us -> 5.8 us
    unnamed x4 -> x0, waiting for transfers between devices: 133 us -> none
    all_gather x2 -> x0, blocking collectives: 36.9 us -> none  [the longest x1 30.5 us: on_device(): lax.all_gather(context, 'req', axis=0, tiled=True)]
    ppermute x0 -> x12, waiting for transfers between devices: none -> 22.3 us  [swap(): return lax.ppermute(x, axis, [(i, i ^ offset) for i in range(n)])]
    ppermute x0 -> x12, starting transfers between devices: none -> 17.9 us  [swap(): return lax.ppermute(x, axis, [(i, i ^ offset) for i in range(n)])]
    dot_general x8 -> x0, matrix products: 12.6 us -> none  [the longest x1 5.96 us: on_device(): jnp.einsum('rkgd,rksd->rkgs', q_rot, key_cache, preferred_element_type=jn...]
    unnamed x1 -> x0, blocking collectives: 10.9 us -> none
    unnamed x16 -> x22, local copies, waits for them, and re-layouts: 2.69 us -> 13.5 us
    pallas_call x0 -> x3, Pallas kernels: none -> 5.8 us  [the longest x1 4.78 us: on_device(): pl.pallas_call(lambda *refs: attend_kernel(len(parts), *refs), out_shape=...]
  transfers between devices with their start and end apart: 2 -> 12, of which waited for: 2 -> 9; matrix products, arithmetic and copies ran while one was open for 4% -> 5% of each run, Pallas kernels for 0% -> 0%
where the time goes in v1:
time: 66.5 us; the launch traced here: 65.3 us
  waiting for transfers between devices  22.3 us (34%)
  starting transfers between devices  17.9 us (27%)
  local copies, waits for them, and re-layouts  16.3 us (25%)
  Pallas kernels  5.8 us (9%)
  other arithmetic  2.92 us (4%)
    ppermute x12, waiting for transfers between devices, swap(): return lax.ppermute(x, axis, [(i, i ^ offset) for i in range(n)])  22.3 us
    ppermute x12, starting transfers between devices, swap(): return lax.ppermute(x, axis, [(i, i ^ offset) for i in range(n)])  17.9 us
    unnamed x22, local copies, waits for them, and re-layouts  13.5 us
    pallas_call x1, Pallas kernels, on_device(): pl.pallas_call(lambda *refs: attend_kernel(len(parts), *refs), out_shape=...  4.78 us
    concatenate x3, other arithmetic, gather_blocks(): jnp.concatenate([x] + [swap(x, axis, n, q * unit) for q in range(1, radix...  1.44 us
  transfers between devices with their start and end apart: 12, of which 9 were waited for; matrix products, arithmetic and copies ran while one was open for 5% of the time, Pallas kernels for 0%

profile of v1, /device:TPU:0, one launch (start us, length us, event | category | flops | bytes accessed | tf_op | source)
XLA Modules:
  0.0 65.3 jit_solution(8380609955666653291)
XLA Ops:
  0.0 3.0 %collective-permute-start = (bf16[8,640]{1,0:T(8,128)(2,1)}, bf16[8,640]{1,0:T(8,128)(2,1)S(1)}, u32[]{:S(2)}, u32[]{:S(2)}) collective-permute-start(bf16[8,640]{1,0:T(8,128)(2,1)} %param.16), channel_id=1, source_target_pairs={{0,2},{1,3},{2,0},{3,1},{4,6},{5,7},{6,4},{7,5},{8,10},{9,11},{10,... | collective-permute-start | bytes 30728 | tf_op jit(solution)/shard_map/ppermute | solution.py:51
  3.0 1.9 %collective-permute-done = bf16[8,640]{1,0:T(8,128)(2,1)S(1)} collective-permute-done((bf16[8,640]{1,0:T(8,128)(2,1)}, bf16[8,640]{1,0:T(8,128)(2,1)S(1)}, u32[]{:S(2)}, u32[]{:S(2)}) %collective-permute-start) | collective-permute-done | bytes 10272 | tf_op jit(solution)/shard_map/ppermute | solution.py:51
  4.8 0.7 %pad_maximum_fusion.2 = bf16[16,640]{1,0:T(8,128)(2,1)S(1)} fusion(bf16[8,640]{1,0:T(8,128)(2,1)S(1)} %collective-permute-done, bf16[8,640]{1,0:T(8,128)(2,1)} %param.16), kind=kLoop, calls=%fused_computation.4 | loop fusion | flops 40960 | bytes 40960 | tf_op jit(solution)/shard_map/concatenate | solution.py:56
  5.5 0.0 collective-permute-start.1
  5.5 0.7 %reshape.18.refs_1_ = bf16[1,640]{1,0:T(2,128)(2,1)S(1)} reshape(bf16[640]{0:T(1024)(128)(2,1)} %param.17) | data formatting | bytes 2560 | tf_op jit(solution)/shard_map/reshape | solution.py:304
  6.2 0.7 %convert_element_type.9 = f32[4]{0:T(128)S(1)} convert(s32[4]{0:T(128)} %refs_0_.1) | non-fusion elementwise | flops 4 | bytes 32 | tf_op jit(solution)/shard_map/convert_element_type | solution.py:317
  6.9 0.0 collective-permute-done.1
  6.9 0.7 %pad_maximum_fusion.refs_0_ = bf16[32,640]{1,0:T(8,128)(2,1)S(1)} fusion(bf16[16,640]{1,0:T(8,128)(2,1)S(1)} %collective-permute-done.1, bf16[8,640]{1,0:T(8,128)(2,1)S(1)} %collective-permute-done, bf16[8,640]{1,0:T(8,128)(2,1)} %param.16), kind=kLoop, calls=%fused_computation | loop fusion | flops 122880 | bytes 81920 | tf_op jit(solution)/shard_map/concatenate | solution.py:56
  7.6 1.4 %copy-done.2 = bf16[640,1280]{1,0:T(8,128)(2,1)S(1)} copy-done((bf16[640,1280]{1,0:T(8,128)(2,1)S(1)}, bf16[640,1280]{1,0:T(8,128)(2,1)}, u32[]{:S(2)}) %copy-start.2) | copy-done | bytes 1638424
  9.0 1.0 %copy-done.4 = bf16[640,256]{1,0:T(8,128)(2,1)S(1)} copy-done((bf16[640,256]{1,0:T(8,128)(2,1)S(1)}, bf16[640,256]{1,0:T(8,128)(2,1)}, u32[]{:S(2)}) %copy-start.4) | copy-done | bytes 327704
  10.0 1.0 %copy-done.5 = bf16[640,256]{1,0:T(8,128)(2,1)S(1)} copy-done((bf16[640,256]{1,0:T(8,128)(2,1)S(1)}, bf16[640,256]{1,0:T(8,128)(2,1)}, u32[]{:S(2)}) %copy-start.5) | copy-done | bytes 327704
  11.0 0.5 project.1
  11.5 2.1 %collective-permute-start.2 = (f32[16,1920]{1,0:T(8,128)S(1)}, f32[16,1920]{1,0:T(8,128)S(1)}, u32[]{:S(2)}, u32[]{:S(2)}) collective-permute-start(f32[16,1920]{1,0:T(8,128)S(1)} %get-tuple-element.10), channel_id=1, source_target_pairs={{0,4},{4,0},{8,12},{12,8},{16,20},{20,16},{24,28},{28,24},{1,5},{5... | collective-permute-start | bytes 368648 | tf_op jit(solution)/shard_map/ppermute | solution.py:51
  13.6 0.1 fusion.1
  13.7 3.9 %collective-permute-done.2 = f32[16,1920]{1,0:T(8,128)S(1)} collective-permute-done((f32[16,1920]{1,0:T(8,128)S(1)}, f32[16,1920]{1,0:T(8,128)S(1)}, u32[]{:S(2)}, u32[]{:S(2)}) %collective-permute-start.2) | collective-permute-done | bytes 122912 | tf_op jit(solution)/shard_map/ppermute | solution.py:51
  17.6 1.9 %collective-permute-start.3 = (f32[4,1920]{1,0:T(4,128)S(1)}, f32[4,1920]{1,0:T(4,128)S(1)}, u32[]{:S(2)}, u32[]{:S(2)}) collective-permute-start(f32[4,1920]{1,0:T(4,128)S(1)} %get-tuple-element.15), channel_id=1, source_target_pairs={{0,8},{4,12},{8,0},{12,4},{16,24},{20,28},{24,16},{28,20},{1,9},{5... | collective-permute-start | bytes 92168 | tf_op jit(solution)/shard_map/ppermute | solution.py:51
  19.5 2.6 %collective-permute-start.4 = (f32[4,1920]{1,0:T(4,128)S(1)}, f32[4,1920]{1,0:T(4,128)S(1)}, u32[]{:S(2)}, u32[]{:S(2)}) collective-permute-start(f32[4,1920]{1,0:T(4,128)S(1)} %get-tuple-element.14), channel_id=1, source_target_pairs={{0,16},{4,20},{8,24},{12,28},{16,0},{20,4},{24,8},{28,12},{1,17},{... | collective-permute-start | bytes 92168 | tf_op jit(solution)/shard_map/ppermute | solution.py:51
  22.1 0.0 collective-permute-start.5
  22.1 0.1 pad_maximum_fusion.3
  22.2 0.7 %reshape.19.refs_9_ = bf16[1,1280]{1,0:T(2,128)(2,1)S(1)} reshape(bf16[1280]{0:T(1024)(128)(2,1)} %param.21) | data formatting | bytes 5120 | tf_op jit(solution)/shard_map/reshape | solution.py:352
  22.9 0.7 %reshape.20.refs_10_ = bf16[1,256]{1,0:T(2,128)(2,1)S(1)} reshape(bf16[256]{0:T(256)(128)(2,1)} %param.22) | data formatting | bytes 1024 | tf_op jit(solution)/shard_map/reshape | solution.py:353
  23.5 0.7 %reshape.21.refs_11_ = bf16[1,256]{1,0:T(2,128)(2,1)S(1)} reshape(bf16[256]{0:T(256)(128)(2,1)} %param.23) | data formatting | bytes 1024 | tf_op jit(solution)/shard_map/reshape | solution.py:354
  24.2 0.0 collective-permute-done.3.refs_4_
  24.2 0.5 collective-permute-done.4.refs_5_
  24.7 3.1 %collective-permute-done.5.refs_6_ = f32[4,1920]{1,0:T(4,128)S(1)} collective-permute-done((f32[4,1920]{1,0:T(4,128)S(1)}, f32[4,1920]{1,0:T(4,128)S(1)}, u32[]{:S(2)}, u32[]{:S(2)}) %collective-permute-start.5) | collective-permute-done | bytes 30752 | tf_op jit(solution)/shard_map/ppermute | solution.py:51
  27.8 3.4 %copy-done = bf16[4,2,4096,128]{3,2,1,0:T(8,128)(2,1)S(1)} copy-done((bf16[4,2,4096,128]{3,2,1,0:T(8,128)(2,1)S(1)}, bf16[4,2,4096,128]{3,2,1,0:T(8,128)(2,1)}, u32[]{:S(2)}) %copy-start) | copy-done | bytes 8388632
  31.2 3.4 %copy-done.1 = bf16[4,2,4096,128]{3,2,1,0:T(8,128)(2,1)S(1)} copy-done((bf16[4,2,4096,128]{3,2,1,0:T(8,128)(2,1)S(1)}, bf16[4,2,4096,128]{3,2,1,0:T(8,128)(2,1)}, u32[]{:S(2)}) %copy-start.1) | copy-done | bytes 8388632
  34.6 0.7 %copy-done.6 = bf16[4,2,4,128]{3,2,1,0:T(4,128)(2,1)S(1)} copy-done((bf16[4,2,4,128]{3,2,1,0:T(4,128)(2,1)S(1)}, bf16[4,2,4,128]{3,2,1,0:T(4,128)(2,1)}, u32[]{:S(2)}) %copy-start.6) | copy-done | bytes 8216
  35.2 0.7 %copy-done.7 = bf16[4,2,4,128]{3,2,1,0:T(4,128)(2,1)S(1)} copy-done((bf16[4,2,4,128]{3,2,1,0:T(4,128)(2,1)S(1)}, bf16[4,2,4,128]{3,2,1,0:T(4,128)(2,1)}, u32[]{:S(2)}) %copy-start.7) | copy-done | bytes 8216
  35.9 0.7 %copy-done.8 = s32[4]{0:T(128)S(1)} copy-done((s32[4]{0:T(128)S(1)}, s32[4]{0:T(128)}, u32[]{:S(2)}) %copy-start.8) | copy-done | bytes 40
  36.6 0.7 %copy-done.9 = s32[4]{0:T(128)S(1)} copy-done((s32[4]{0:T(128)S(1)}, s32[4]{0:T(128)}, u32[]{:S(2)}) %copy-start.9) | copy-done | bytes 40
  37.3 0.7 %copy-done.10 = s32[4]{0:T(128)S(1)} copy-done((s32[4]{0:T(128)S(1)}, s32[4]{0:T(128)}, u32[]{:S(2)}) %copy-start.10) | copy-done | bytes 40
  37.9 4.8 %attend.1 = f32[4,1280]{1,0:T(4,128)S(1)} custom-call(s32[4]{0:T(128)S(1)} %copy-done.8, s32[4]{0:T(128)S(1)} %copy-done.9, s32[4]{0:T(128)S(1)} %copy-done.10, f32[4,1920]{1,0:T(4,128)S(1)} %get-tuple-element.16.refs_3_, f32[4,1920]{1,0:T(4,128)S(1)} %collective-permute-done.3.refs_4_, f32[4,1920]{1,0:T(4,128)S(1)} %collective-permute-done.4.refs_5_, ...), custom_call_target="tpu_custom_call" | custom-call | tf_op jit(solution)/shard_map/attend/pallas_call | solution.py:325
  42.7 1.5 %collective-permute-start.6 = (bf16[4,1280]{1,0:T(4,128)(2,1)S(1)}, bf16[4,1280]{1,0:T(4,128)(2,1)S(1)}, u32[]{:S(2)}, u32[]{:S(2)}) collective-permute-start(bf16[4,1280]{1,0:T(4,128)(2,1)S(1)} %convert_element_type.10), channel_id=1, source_target_pairs={{0,8},{4,12},{8,0},{12,4},{16,24},{20,28},{24,16},{28,20},{1,9},{5... | collective-permute-start | bytes 30728 | tf_op jit(solution)/shard_map/ppermute | solution.py:51
  44.2 5.2 %collective-permute-start.7 = (bf16[4,1280]{1,0:T(4,128)(2,1)S(1)}, bf16[4,1280]{1,0:T(4,128)(2,1)S(1)}, u32[]{:S(2)}, u32[]{:S(2)}) collective-permute-start(bf16[4,1280]{1,0:T(4,128)(2,1)S(1)} %convert_element_type.10), channel_id=1, source_target_pairs={{0,16},{4,20},{8,24},{12,28},{16,0},{20,4},{24,8},{28,12},{1,17},{... | collective-permute-start | bytes 30728 | tf_op jit(solution)/shard_map/ppermute | solution.py:51
  49.4 0.0 collective-permute-start.8
  49.4 0.0 collective-permute-done.6
  49.4 1.6 %collective-permute-done.7 = bf16[4,1280]{1,0:T(4,128)(2,1)S(1)} collective-permute-done((bf16[4,1280]{1,0:T(4,128)(2,1)S(1)}, bf16[4,1280]{1,0:T(4,128)(2,1)S(1)}, u32[]{:S(2)}, u32[]{:S(2)}) %collective-permute-start.7) | collective-permute-done | bytes 10272 | tf_op jit(solution)/shard_map/ppermute | solution.py:51
  51.0 3.8 %collective-permute-done.8 = bf16[4,1280]{1,0:T(4,128)(2,1)S(1)} collective-permute-done((bf16[4,1280]{1,0:T(4,128)(2,1)S(1)}, bf16[4,1280]{1,0:T(4,128)(2,1)S(1)}, u32[]{:S(2)}, u32[]{:S(2)}) %collective-permute-start.8) | collective-permute-done | bytes 10272 | tf_op jit(solution)/shard_map/ppermute | solution.py:51
  54.9 0.1 collective-permute-start.9
  55.0 4.0 %collective-permute-done.9 = bf16[16,1280]{1,0:T(8,128)(2,1)S(1)} collective-permute-done((bf16[16,1280]{1,0:T(8,128)(2,1)S(1)}, bf16[16,1280]{1,0:T(8,128)(2,1)S(1)}, u32[]{:S(2)}, u32[]{:S(2)}) %collective-permute-start.9) | collective-permute-done | bytes 40992 | tf_op jit(solution)/shard_map/ppermute | solution.py:51
  59.0 0.1 concatenate.25.refs_0_
  59.0 0.5 output.1
  59.5 0.1 collective-permute-start.10
  59.6 1.2 %collective-permute-done.10 = f32[16,640]{1,0:T(8,128)S(1)} collective-permute-done((f32[16,640]{1,0:T(8,128)S(1)}, f32[16,640]{1,0:T(8,128)S(1)}, u32[]{:S(2)}, u32[]{:S(2)}) %collective-permute-start.10) | collective-permute-done | bytes 40992 | tf_op jit(solution)/shard_map/ppermute | solution.py:51
  60.8 1.6 %collective-permute-start.11 = (f32[8,640]{1,0:T(8,128)S(1)}, f32[8,640]{1,0:T(8,128)S(1)}, u32[]{:S(2)}, u32[]{:S(2)}) collective-permute-start(f32[8,640]{1,0:T(8,128)S(1)} %slice.29), channel_id=1, source_target_pairs={{0,2},{1,3},{2,0},{3,1},{4,6},{5,7},{6,4},{7,5},{8,10},{9,11},{10,... | collective-permute-start | bytes 61448 | tf_op jit(solution)/shard_map/ppermute | solution.py:51
  62.4 2.3 %collective-permute-done.11 = f32[8,640]{1,0:T(8,128)S(1)} collective-permute-done((f32[8,640]{1,0:T(8,128)S(1)}, f32[8,640]{1,0:T(8,128)S(1)}, u32[]{:S(2)}, u32[]{:S(2)}) %collective-permute-start.11) | collective-permute-done | bytes 20512 | tf_op jit(solution)/shard_map/ppermute | solution.py:51
  64.7 0.6 fusion
  (19 shorter events, 0.1 us)
Async XLA Ops:
  0.0 4.8 %collective-permute-start = (bf16[8,640]{1,0:T(8,128)(2,1)}, bf16[8,640]{1,0:T(8,128)(2,1)S(1)}, u32[]{:S(2)}, u32[]{:S(2)}) collective-permute-start(bf16[8,640]{1,0:T(8,128)(2,1)} %param.16), channel_id=1, source_target_pairs={{0,2},{1,3},{2,0},{3,1},{4,6},{5,7},{6,4},{7,5},{8,10},{9,11},{10,... | collective-permute-start | bytes 30728 | tf_op jit(solution)/shard_map/ppermute | solution.py:51
  5.5 1.4 %collective-permute-start.1 = (bf16[16,640]{1,0:T(8,128)(2,1)S(1)}, bf16[16,640]{1,0:T(8,128)(2,1)S(1)}, u32[]{:S(2)}, u32[]{:S(2)}) collective-permute-start(bf16[16,640]{1,0:T(8,128)(2,1)S(1)} %pad_maximum_fusion.2), channel_id=1, source_target_pairs={{0,1},{1,0},{2,3},{3,2},{4,5},{5,4},{6,7},{7,6},{8,9},{9,8},{10,11... | collective-permute-start | bytes 61448 | tf_op jit(solution)/shard_map/ppermute | solution.py:51
  7.6 1.4 %copy-start.2 = (bf16[640,1280]{1,0:T(8,128)(2,1)S(1)}, bf16[640,1280]{1,0:T(8,128)(2,1)}, u32[]{:S(2)}) copy-start(bf16[640,1280]{1,0:T(8,128)(2,1)} %refs_2_.2) | copy-start | bytes 4915204
  9.0 1.0 %copy-start.4 = (bf16[640,256]{1,0:T(8,128)(2,1)S(1)}, bf16[640,256]{1,0:T(8,128)(2,1)}, u32[]{:S(2)}) copy-start(bf16[640,256]{1,0:T(8,128)(2,1)} %refs_3_.1) | copy-start | bytes 983044
  10.0 1.0 %copy-start.5 = (bf16[640,256]{1,0:T(8,128)(2,1)S(1)}, bf16[640,256]{1,0:T(8,128)(2,1)}, u32[]{:S(2)}) copy-start(bf16[640,256]{1,0:T(8,128)(2,1)} %refs_4_.1) | copy-start | bytes 983044
  11.5 6.1 %collective-permute-start.2 = (f32[16,1920]{1,0:T(8,128)S(1)}, f32[16,1920]{1,0:T(8,128)S(1)}, u32[]{:S(2)}, u32[]{:S(2)}) collective-permute-start(f32[16,1920]{1,0:T(8,128)S(1)} %get-tuple-element.10), channel_id=1, source_target_pairs={{0,4},{4,0},{8,12},{12,8},{16,20},{20,16},{24,28},{28,24},{1,5},{5... | collective-permute-start | bytes 368648 | tf_op jit(solution)/shard_map/ppermute | solution.py:51
  17.6 6.6 %collective-permute-start.3 = (f32[4,1920]{1,0:T(4,128)S(1)}, f32[4,1920]{1,0:T(4,128)S(1)}, u32[]{:S(2)}, u32[]{:S(2)}) collective-permute-start(f32[4,1920]{1,0:T(4,128)S(1)} %get-tuple-element.15), channel_id=1, source_target_pairs={{0,8},{4,12},{8,0},{12,4},{16,24},{20,28},{24,16},{28,20},{1,9},{5... | collective-permute-start | bytes 92168 | tf_op jit(solution)/shard_map/ppermute | solution.py:51
  19.5 5.2 %collective-permute-start.4 = (f32[4,1920]{1,0:T(4,128)S(1)}, f32[4,1920]{1,0:T(4,128)S(1)}, u32[]{:S(2)}, u32[]{:S(2)}) collective-permute-start(f32[4,1920]{1,0:T(4,128)S(1)} %get-tuple-element.14), channel_id=1, source_target_pairs={{0,16},{4,20},{8,24},{12,28},{16,0},{20,4},{24,8},{28,12},{1,17},{... | collective-permute-start | bytes 92168 | tf_op jit(solution)/shard_map/ppermute | solution.py:51
  22.1 5.7 %collective-permute-start.5 = (f32[4,1920]{1,0:T(4,128)S(1)}, f32[4,1920]{1,0:T(4,128)S(1)}, u32[]{:S(2)}, u32[]{:S(2)}) collective-permute-start(f32[4,1920]{1,0:T(4,128)S(1)} %get-tuple-element.13), channel_id=1, source_target_pairs={{0,24},{4,28},{8,16},{12,20},{16,8},{20,12},{24,0},{28,4},{1,25},{... | collective-permute-start | bytes 92168 | tf_op jit(solution)/shard_map/ppermute | solution.py:51
  27.8 3.4 %copy-start = (bf16[4,2,4096,128]{3,2,1,0:T(8,128)(2,1)S(1)}, bf16[4,2,4096,128]{3,2,1,0:T(8,128)(2,1)}, u32[]{:S(2)}) copy-start(bf16[4,2,4096,128]{3,2,1,0:T(8,128)(2,1)} %refs_12_.1) | copy-start | bytes 25165828
  31.2 3.4 %copy-start.1 = (bf16[4,2,4096,128]{3,2,1,0:T(8,128)(2,1)S(1)}, bf16[4,2,4096,128]{3,2,1,0:T(8,128)(2,1)}, u32[]{:S(2)}) copy-start(bf16[4,2,4096,128]{3,2,1,0:T(8,128)(2,1)} %refs_13_.1) | copy-start | bytes 25165828
  34.5 0.7 %copy-start.6 = (bf16[4,2,4,128]{3,2,1,0:T(4,128)(2,1)S(1)}, bf16[4,2,4,128]{3,2,1,0:T(4,128)(2,1)}, u32[]{:S(2)}) copy-start(bf16[4,2,4,128]{3,2,1,0:T(4,128)(2,1)} %refs_14_.1) | copy-start | bytes 24580
  35.2 0.7 %copy-start.7 = (bf16[4,2,4,128]{3,2,1,0:T(4,128)(2,1)S(1)}, bf16[4,2,4,128]{3,2,1,0:T(4,128)(2,1)}, u32[]{:S(2)}) copy-start(bf16[4,2,4,128]{3,2,1,0:T(4,128)(2,1)} %refs_15_.1) | copy-start | bytes 24580
  35.9 0.7 %copy-start.8 = (s32[4]{0:T(128)S(1)}, s32[4]{0:T(128)}, u32[]{:S(2)}) copy-start(s32[4]{0:T(128)} %refs_0_.1) | copy-start | bytes 52
  36.6 0.7 %copy-start.9 = (s32[4]{0:T(128)S(1)}, s32[4]{0:T(128)}, u32[]{:S(2)}) copy-start(s32[4]{0:T(128)} %refs_1_.2) | copy-start | bytes 52
  37.3 0.7 %copy-start.10 = (s32[4]{0:T(128)S(1)}, s32[4]{0:T(128)}, u32[]{:S(2)}) copy-start(s32[4]{0:T(128)} %refs_2_.3) | copy-start | bytes 52
  37.9 21.1 %copy-start.3 = (bf16[1280,640]{1,0:T(8,128)(2,1)S(1)}, bf16[1280,640]{1,0:T(8,128)(2,1)}, u32[]{:S(2)}) copy-start(bf16[1280,640]{1,0:T(8,128)(2,1)} %refs_1_.3) | copy-start | bytes 4915204
  42.7 6.7 %collective-permute-start.6 = (bf16[4,1280]{1,0:T(4,128)(2,1)S(1)}, bf16[4,1280]{1,0:T(4,128)(2,1)S(1)}, u32[]{:S(2)}, u32[]{:S(2)}) collective-permute-start(bf16[4,1280]{1,0:T(4,128)(2,1)S(1)} %convert_element_type.10), channel_id=1, source_target_pairs={{0,8},{4,12},{8,0},{12,4},{16,24},{20,28},{24,16},{28,20},{1,9},{5... | collective-permute-start | bytes 30728 | tf_op jit(solution)/shard_map/ppermute | solution.py:51
  44.2 6.9 %collective-permute-start.7 = (bf16[4,1280]{1,0:T(4,128)(2,1)S(1)}, bf16[4,1280]{1,0:T(4,128)(2,1)S(1)}, u32[]{:S(2)}, u32[]{:S(2)}) collective-permute-start(bf16[4,1280]{1,0:T(4,128)(2,1)S(1)} %convert_element_type.10), channel_id=1, source_target_pairs={{0,16},{4,20},{8,24},{12,28},{16,0},{20,4},{24,8},{28,12},{1,17},{... | collective-permute-start | bytes 30728 | tf_op jit(solution)/shard_map/ppermute | solution.py:51
  49.4 5.5 %collective-permute-start.8 = (bf16[4,1280]{1,0:T(4,128)(2,1)S(1)}, bf16[4,1280]{1,0:T(4,128)(2,1)S(1)}, u32[]{:S(2)}, u32[]{:S(2)}) collective-permute-start(bf16[4,1280]{1,0:T(4,128)(2,1)S(1)} %convert_element_type.10), channel_id=1, source_target_pairs={{0,24},{4,28},{8,16},{12,20},{16,8},{20,12},{24,0},{28,4},{1,25},{... | collective-permute-start | bytes 30728 | tf_op jit(solution)/shard_map/ppermute | solution.py:51
  54.9 4.1 %collective-permute-start.9 = (bf16[16,1280]{1,0:T(8,128)(2,1)S(1)}, bf16[16,1280]{1,0:T(8,128)(2,1)S(1)}, u32[]{:S(2)}, u32[]{:S(2)}) collective-permute-start(bf16[16,1280]{1,0:T(8,128)(2,1)S(1)} %pad_maximum_fusion.1), channel_id=1, source_target_pairs={{0,4},{4,0},{8,12},{12,8},{16,20},{20,16},{24,28},{28,24},{1,5},{5... | collective-permute-start | bytes 122888 | tf_op jit(solution)/shard_map/ppermute | solution.py:51
  59.5 1.3 %collective-permute-start.10 = (f32[16,640]{1,0:T(8,128)S(1)}, f32[16,640]{1,0:T(8,128)S(1)}, u32[]{:S(2)}, u32[]{:S(2)}) collective-permute-start(f32[16,640]{1,0:T(8,128)S(1)} %get-tuple-element.12), channel_id=1, source_target_pairs={{0,1},{1,0},{2,3},{3,2},{4,5},{5,4},{6,7},{7,6},{8,9},{9,8},{10,11... | collective-permute-start | bytes 122888 | tf_op jit(solution)/shard_map/ppermute | solution.py:51
  60.8 3.8 %collective-permute-start.11 = (f32[8,640]{1,0:T(8,128)S(1)}, f32[8,640]{1,0:T(8,128)S(1)}, u32[]{:S(2)}, u32[]{:S(2)}) collective-permute-start(f32[8,640]{1,0:T(8,128)S(1)} %slice.29), channel_id=1, source_target_pairs={{0,2},{1,3},{2,0},{3,1},{4,6},{5,7},{6,4},{7,5},{8,10},{9,11},{10,... | collective-permute-start | bytes 61448 | tf_op jit(solution)/shard_map/ppermute | solution.py:51

commit v2 on v1

v2 whole, which is shorter than its diff:
```python
import math

import jax
import jax.numpy as jnp
from jax import lax
from jax.experimental import pallas as pl
from jax.experimental.pallas import tpu as pltpu
from jax.sharding import PartitionSpec as P

D = 5120
SINKS = 4
EPS = 1e-06
BLOCK = 512
PLAN_BITS = 4
TOGETHER = 4
LANES = 128
STAGE_BITS = 2

EXTRA_ROWS = 16


def log2(n):
    bits = n.bit_length() - 1
    assert n == 1 << bits
    return bits


def stages(n, most):
    bits = log2(n)
    if bits == 0:
        return []
    result = [(2, 1)]
    left = bits - 1
    while left:
        take = most if left % most == 0 else 1
        left -= take
        result.append((1 << take, 2 << left))
    return result


def crossed(offset, kv):
    low = offset & 3
    turned = ((low & 1) << 1) | (low >> 1)
    return offset ^ ((low ^ turned) * (kv & 1))


def place_to_offset(place, n):
    bits = log2(n)
    if bits == 0:
        return place
    return ((place << 1) | (place >> (bits - 1))) & (n - 1)


def swap_req(x, n_req, n_kv, offset):
    pairs = [
        (i * n_kv + j, (i ^ (crossed(offset, j) if n_req > 2 else offset)) * n_kv + j)
        for i in range(n_req)
        for j in range(n_kv)
    ]
    return lax.ppermute(x, ("req", "kv"), pairs)


def swap_kv(x, n_kv, offset):
    return lax.ppermute(x, "kv", [(j, j ^ offset) for j in range(n_kv)])


def row_order(size, rows_req, rows_kv, to_kv):
    req, kv = lax.axis_index("req"), lax.axis_index("kv")
    n_req = size // rows_req
    shape = (size, size)
    req_row = lax.broadcasted_iota(jnp.int32, shape, 1 if to_kv else 0)
    kv_row = lax.broadcasted_iota(jnp.int32, shape, 0 if to_kv else 1)
    offset = place_to_offset(req_row >> log2(rows_req), n_req)
    if n_req > 2:
        offset = crossed(offset, kv)
    request = ((offset ^ req) << log2(rows_req)) | (req_row & (rows_req - 1))
    kv_request = (((request >> log2(rows_kv)) ^ kv) << log2(rows_kv)) | (request & (rows_kv - 1))
    return (kv_request == kv_row).astype(jnp.bfloat16)


def load_weights_kernel(*refs):
    n = len(refs) // 2
    sem = refs[-1]
    copies = [
        pltpu.make_async_copy(refs[i], refs[n + i], sem.at[i]) for i in range(n)
    ]
    for copy in copies:
        copy.start()
    for copy in copies:
        copy.wait()


def project_kernel(rows_req, n_kv, *refs):
    pieces, (gain, w_query, w_key, w_value, keep, send) = refs[:n_kv], refs[n_kv:]
    rows_kv = pieces[0].shape[0]
    size = rows_kv * n_kv
    order = row_order(size, rows_req, rows_kv, False)
    hidden = jnp.concatenate([piece[...].astype(jnp.float32) for piece in pieces], 0)
    xf = jnp.dot(order, hidden.astype(jnp.bfloat16), preferred_element_type=jnp.float32)
    rows = gain[...].astype(jnp.float32)
    wide_gain = jnp.concatenate([rows[i : i + 1] for i in range(rows.shape[0])], 1)
    scaled = (xf * wide_gain).astype(jnp.bfloat16)
    half = keep.shape[0]

    def put(start, block):
        width = block.shape[1]
        keep[:, start : start + width] = block[:half]
        send[:, start : start + width] = block[half:]

    at = 0
    for weight in (w_query, w_key, w_value):
        put(at, jnp.dot(scaled, weight[...], preferred_element_type=jnp.float32))
        at += weight.shape[1]
    squares = jnp.sum(xf * xf, 1, keepdims=True)
    put(at, jnp.broadcast_to(squares, (size, LANES)))


def plan_of(lengths, sink_count, window):
    count = lengths.shape[0]
    low = jnp.maximum(sink_count, lengths - window)
    first = low // BLOCK
    visits = (lengths - 1) // BLOCK - first + 1
    shift = PLAN_BITS * 2 * jnp.arange(count, dtype=jnp.int32)
    plan = jnp.stack(
        [
            low - first * BLOCK,
            lengths - first * BLOCK,
            jnp.minimum(sink_count, lengths),
            (first | (visits << PLAN_BITS)) << shift,
        ]
    )
    return jnp.broadcast_to(plan[:, :, None], (4, count, LANES))


def visits_of(plan, count):
    mask = (1 << PLAN_BITS) - 1
    packed = sum(plan[3, r : r + 1] for r in range(count))[0, 0]
    fields = [
        lax.shift_right_logical(packed, jnp.int32(PLAN_BITS * i)) & mask for i in range(2 * count)
    ]
    return list(zip(fields[::2], fields[1::2]))


def load_cache_kernel(plan, cache, buf, sem):
    count, blocks = cache.shape[0], cache.shape[2] // BLOCK
    planned = visits_of(plan, count)

    def each(act):
        for r, (first, visits) in enumerate(planned):

            @pl.loop(0, visits)
            def _(t):
                at = (first + t) & (blocks - 1)
                src = pl.ds(pl.multiple_of(at * BLOCK, BLOCK), BLOCK)
                dst = pl.ds(pl.multiple_of(t * BLOCK, BLOCK), BLOCK)
                act(pltpu.make_async_copy(cache.at[r, :, src], buf.at[r, :, dst], sem.at[r, t]))

    each(lambda copy: copy.start())
    each(lambda copy: copy.wait())


def attend_kernel(n_parts, plan, *refs):
    parts = refs[:n_parts]
    (
        cosine,
        sine,
        b_query,
        b_key,
        b_value,
        k_buf,
        v_buf,
        sink_keys,
        sink_values,
        context,
        score_buf,
        q_heads,
        k_extra,
        v_extra,
        result_buf,
    ) = refs[n_parts:]
    count, heads_kv, _, size = k_buf.shape
    q_cols, kv_cols = context.shape[1], heads_kv * size
    group = q_cols // kv_cols
    pad = q_heads.shape[1] // heads_kv
    scale = 1.0 / math.sqrt(size)
    planned = visits_of(plan, count)

    total = parts[0][...]
    for part in parts[1:]:
        total = total + part[...]
    columns = q_cols + 2 * kv_cols
    inv_rms = lax.rsqrt(total[:, columns : columns + 1] / D + EPS)
    bias = jnp.concatenate([b[...].astype(jnp.float32) for b in (b_query, b_key, b_value)], 0)

    def head_of(i):
        return inv_rms * total[:, i * size : (i + 1) * size] + bias[i : i + 1]

    cos, sin = cosine[...], sine[...]

    def rotated(x):
        return x * cos + pltpu.roll(x, size // 2, 1) * sin

    q_heads[...] = jnp.zeros_like(q_heads)
    k_extra[...] = jnp.zeros_like(k_extra)
    v_extra[...] = jnp.zeros_like(v_extra)
    for h in range(heads_kv):
        lanes = slice(h * size, (h + 1) * size)
        for g in range(group):
            head = h * group + g
            block = rotated(head_of(head))
            for r in range(count):
                q_heads[r, h * pad + g : h * pad + g + 1, lanes] = block[r : r + 1]
        k_rot = rotated(head_of(heads_kv * group + h))
        value = head_of(heads_kv * group + heads_kv + h)
        for r in range(count):
            k_extra[r, 0:SINKS, lanes] = sink_keys[r, h].astype(jnp.float32)
            v_extra[r, 0:SINKS, lanes] = sink_values[r, h].astype(jnp.float32)
            k_extra[r, SINKS : SINKS + 1, lanes] = k_rot[r : r + 1]
            v_extra[r, SINKS : SINKS + 1, lanes] = value[r : r + 1]

    contract_last = (((1,), (1,)), ((), ()))
    lane = lax.broadcasted_iota(jnp.int32, (1, EXTRA_ROWS), 1)
    offset = lax.broadcasted_iota(jnp.int32, (1, BLOCK), 1)
    repeats = BLOCK // LANES
    queries = [q_heads[r].astype(jnp.bfloat16) for r in range(count)]

    def both(buf, r, t):
        rows = pl.ds(pl.multiple_of(t * BLOCK, BLOCK), BLOCK)
        return jnp.concatenate([buf[r, h, rows] for h in range(heads_kv)], 1)

    def fold(x, op):
        pieces = [x[:, i : i + LANES] for i in range(0, x.shape[1], LANES)]
        while len(pieces) > 1:
            pieces = [op(*pieces[i : i + 2]) for i in range(0, len(pieces), 2)]
        return pieces[0]

    def score(r, t, last):
        s = (
            lax.dot_general(
                queries[r],
                both(k_buf, r, jnp.minimum(t, last)),
                contract_last,
                preferred_element_type=jnp.float32,
            )
            * scale
        )
        position = t * BLOCK + offset
        low, high = (jnp.concatenate([plan[i, r : r + 1]] * repeats, 1) for i in range(2))
        s = jnp.where((position >= low) & (position < high), s, -jnp.inf)
        score_buf[r, t] = s
        return fold(s, jnp.maximum)

    def mix(r, t, last, top):
        weights = jnp.exp(score_buf[r, t] - top)
        product = jnp.dot(
            weights.astype(jnp.bfloat16),
            both(v_buf, r, jnp.minimum(t, last)),
            preferred_element_type=jnp.float32,
        )
        return fold(weights, jnp.add), product

    def rounds(visits):
        return (visits - 1 + TOGETHER - 1) // TOGETHER

    extras, tops = [], []
    for r in range(count):
        extra = (
            lax.dot_general(
                queries[r],
                k_extra[r].astype(jnp.bfloat16),
                contract_last,
                preferred_element_type=jnp.float32,
            )
            * scale
        )
        live = (lane < plan[2, r : r + 1, :EXTRA_ROWS]) | (lane == SINKS)
        extras.append(jnp.where(live, extra, -jnp.inf))
        tops.append(score(r, 0, 0))
    for r in range(count):
        visits = planned[r][1]

        def more_scores(k, top):
            for i in range(TOGETHER):
                top = jnp.maximum(top, score(r, 1 + k * TOGETHER + i, visits - 1))
            return top

        tops[r] = lax.fori_loop(0, rounds(visits), more_scores, tops[r])
    sums = []
    for r in range(count):
        tops[r] = jnp.maximum(
            jnp.max(tops[r], 1, keepdims=True), jnp.max(extras[r], 1, keepdims=True)
        )
        extras[r] = jnp.exp(extras[r] - tops[r])
        numer = jnp.dot(
            extras[r].astype(jnp.bfloat16),
            v_extra[r].astype(jnp.bfloat16),
            preferred_element_type=jnp.float32,
        )
        denom, product = mix(r, 0, 0, tops[r])
        sums.append((denom, numer + product))
    for r in range(count):
        visits = planned[r][1]

        def more_values(k, carry):
            denom, numer = carry
            for i in range(TOGETHER):
                d, n = mix(r, 1 + k * TOGETHER + i, visits - 1, tops[r])
                denom, numer = denom + d, numer + n
            return denom, numer

        sums[r] = lax.fori_loop(0, rounds(visits), more_values, sums[r])
    for r in range(count):
        denom, numer = sums[r]
        denom = jnp.sum(denom, 1, keepdims=True) + jnp.sum(extras[r], 1, keepdims=True)
        result = numer / denom
        for h in range(heads_kv):
            for g in range(group):
                head = h * group + g
                result_buf[r : r + 1, head * size : (head + 1) * size] = result[
                    h * pad + g : h * pad + g + 1, h * size : (h + 1) * size
                ]
    context[...] = result_buf[...].astype(context.dtype)


def output_kernel(rows_kv, context, w_output, *outs):
    size = context.shape[0]
    rows_req = size // lax.axis_size("req")
    order = row_order(size, rows_req, rows_kv, True)
    rows = jnp.dot(order, context[...], preferred_element_type=jnp.float32).astype(jnp.bfloat16)
    product = jnp.dot(rows, w_output[...], preferred_element_type=jnp.float32)
    for u, out in enumerate(outs):
        out[...] = product[u * rows_kv : (u + 1) * rows_kv]


def spec(space=pltpu.VMEM):
    return pl.BlockSpec(memory_space=space)


def in_hbm(x):
    return pltpu.with_memory_space_constraint(x, pltpu.HBM)


def on_device(
    hidden,
    gain,
    w_query,
    w_key,
    w_value,
    b_query,
    b_key,
    b_value,
    w_output,
    key_cache,
    value_cache,
    sink_keys,
    sink_values,
    lengths,
    sink_count,
    window,
):
    n_req, n_kv = lax.axis_size("req"), lax.axis_size("kv")
    count, heads_kv, cycle, size = key_cache.shape
    rows_kv = hidden.shape[0]
    rows = count * n_req
    q_cols, kv_cols = w_query.shape[1], w_key.shape[1]
    group = q_cols // (heads_kv * size)
    wide = q_cols + 2 * kv_cols + LANES
    f32, bf16 = jnp.float32, jnp.bfloat16

    others = [swap_kv(hidden, n_kv, u) for u in range(1, n_kv)]
    chunk = LANES if gain.shape[0] % LANES == 0 else gain.shape[0]
    wanted = (
        w_query,
        w_key,
        w_value,
        hidden,
        gain.reshape(-1, chunk),
        b_query.reshape(-1, size),
        b_key.reshape(-1, size),
        b_value.reshape(-1, size),
        sink_keys,
        sink_values,
        lengths,
        sink_count,
        window,
    )
    fetched = pl.pallas_call(
        load_weights_kernel,
        out_shape=tuple(jax.ShapeDtypeStruct(w.shape, w.dtype) for w in wanted),
        in_specs=[spec(pltpu.HBM)] * len(wanted),
        out_specs=(spec(),) * len(wanted),
        scratch_shapes=[pltpu.SemaphoreType.DMA((len(wanted),))],
        compiler_params=pltpu.CompilerParams(vmem_limit_bytes=1 << 20),
        cost_estimate=pl.CostEstimate(flops=0, transcendentals=0, bytes_accessed=6 << 20),
        name="load_weights",
    )(*[in_hbm(w) for w in wanted])
    *weights, mine, gain, b_query, b_key, b_value, sink_keys, sink_values = fetched[:-3]
    lengths, sink_count, window = fetched[-3:]
    pieces = [mine] + others
    half = jax.ShapeDtypeStruct((rows // 2, wide), f32)
    keep, send = pl.pallas_call(
        lambda *refs: project_kernel(count, n_kv, *refs),
        out_shape=(half, half),
        in_specs=[spec()] * (n_kv + 4),
        out_specs=(spec(), spec()),
        compiler_params=pltpu.CompilerParams(vmem_limit_bytes=16 << 20),
        name="project",
    )(*pieces, gain, *weights)

    visits = cycle // BLOCK + 1

    def load(cache, plan, name):
        return pl.pallas_call(
            load_cache_kernel,
            out_shape=jax.ShapeDtypeStruct((count, heads_kv, visits * BLOCK, size), bf16),
            in_specs=[spec(), spec(pltpu.HBM)],
            out_specs=spec(),
            scratch_shapes=[pltpu.SemaphoreType.DMA((count, visits))],
            compiler_params=pltpu.CompilerParams(vmem_limit_bytes=1 << 20),
            cost_estimate=pl.CostEstimate(flops=0, transcendentals=0, bytes_accessed=6 << 20),
            name=name,
        )(plan, in_hbm(cache))

    req_stages = stages(n_req, STAGE_BITS)
    plan = plan_of(lengths, sink_count, window)
    keep, plan = lax.optimization_barrier((keep, plan))
    received = swap_req(send, n_req, n_kv, req_stages[0][1])
    k_live = load(key_cache, plan, "load_keys")
    keep, k_live = lax.optimization_barrier((keep, k_live))
    parts = [keep, received]
    for radix, unit in req_stages[1:]:
        x = sum(parts[1:], parts[0])
        chunk = x.shape[0] // radix
        parts = [x[:chunk]] + [
            swap_req(x[q * chunk : (q + 1) * chunk], n_req, n_kv, q * unit)
            for q in range(1, radix)
        ]
    parts[0], plan = lax.optimization_barrier((parts[0], plan))
    v_live = load(value_cache, plan, "load_values")

    freq = jnp.power(1000000.0, -2.0 * jnp.arange(size // 2, dtype=f32) / size)
    angle = lengths.astype(f32)[:, None] * freq
    cos, sin = jnp.cos(angle), jnp.sin(angle)
    cosine = jnp.concatenate([cos, cos], 1)
    sine = jnp.concatenate([-sin, sin], 1)

    pad = -(-group // 8) * 8
    context = pl.pallas_call(
        lambda *refs: attend_kernel(len(parts), *refs),
        out_shape=jax.ShapeDtypeStruct((count, q_cols), bf16),
        in_specs=[spec()] * (len(parts) + 10),
        out_specs=spec(),
        scratch_shapes=[
            pltpu.VMEM((count, visits + TOGETHER, heads_kv * pad, BLOCK), f32),
            pltpu.VMEM((count, heads_kv * pad, heads_kv * size), f32),
            pltpu.VMEM((count, EXTRA_ROWS, heads_kv * size), f32),
            pltpu.VMEM((count, EXTRA_ROWS, heads_kv * size), f32),
            pltpu.VMEM((count, q_cols), f32),
        ],
        compiler_params=pltpu.CompilerParams(vmem_limit_bytes=8 << 20),
        name="attend",
    )(
        plan,
        *parts,
        cosine,
        sine,
        b_query,
        b_key,
        b_value,
        k_live,
        v_live,
        sink_keys,
        sink_values,
    )

    everyone = context
    for radix, unit in reversed(stages(n_req, STAGE_BITS)):
        blocks = [swap_req(everyone, n_req, n_kv, q * unit) for q in range(1, radix)]
        everyone = jnp.concatenate([everyone] + blocks, 0)
    piece = jax.ShapeDtypeStruct((rows_kv, w_output.shape[1]), f32)
    products = pl.pallas_call(
        lambda *refs: output_kernel(rows_kv, *refs),
        out_shape=(piece,) * n_kv,
        in_specs=[spec()] * 2,
        out_specs=(spec(),) * n_kv,
        compiler_params=pltpu.CompilerParams(vmem_limit_bytes=16 << 20),
        name="output",
    )(everyone, w_output)
    result = products[0]
    for u in range(1, n_kv):
        result = result + swap_kv(products[u], n_kv, u)
    return result.astype(bf16)


def solution(mesh):
    in_specs = (
        P("kv", "req"),
        P("req"),
        P("req", "kv"),
        P("req", "kv"),
        P("req", "kv"),
        P("kv"),
        P("kv"),
        P("kv"),
        P("kv", "req"),
        P("req", "kv", None, None),
        P("req", "kv", None, None),
        P("req", "kv", None, None),
        P("req", "kv", None, None),
        P("req"),
        P("req"),
        P("req"),
    )
    out_specs = P("kv", "req")
    return jax.shard_map(
        on_device, mesh=mesh, in_specs=in_specs, out_specs=out_specs, check_vma=False
    )
```

time: 66.5 us -> 39.8 us (0.60); the launches traced: 65.3 us -> 40 us
  local copies, waits for them, and re-layouts: 16.3 us -> 0.15 us
  waiting for transfers between devices: 22.3 us -> 14.5 us
  Pallas kernels: 5.8 us -> 7.86 us
  other arithmetic: 2.92 us -> 0.89 us
  starting transfers between devices: 17.9 us -> 16.5 us
    unnamed x22 -> x2, local copies, waits for them, and re-layouts: 13.5 us -> 0.01 us
    ppermute x12 -> x14, waiting for transfers between devices: 22.3 us -> 14.5 us  [the longest x8 10.2 us: swap_req(): return lax.ppermute(x, ('req', 'kv'), pairs)]
    pallas_call x2 -> x5, Pallas kernels: 1.03 us -> 6.18 us  [the longest x2 3.45 us: load(): pl.pallas_call(load_cache_kernel, out_shape=jax.ShapeDtypeStruct((count,...]
    pallas_call x1, Pallas kernels: 4.78 us -> 1.69 us  [on_device(): pl.pallas_call(lambda *refs: attend_kernel(len(parts), *refs), out_shape=...]
    reshape x4 -> x0, local copies, waits for them, and re-layouts: 2.7 us -> none  [the longest x1 0.69 us: on_device(): b_query.reshape(1, -1)]
    ppermute x12 -> x14, starting transfers between devices: 17.9 us -> 16.5 us  [the longest x8 11.5 us: swap_req(): return lax.ppermute(x, ('req', 'kv'), pairs)]
    concatenate x3 -> x1, other arithmetic: 1.44 us -> 0.03 us  [on_device(): everyone = jnp.concatenate([everyone] + blocks, 0)]
  transfers between devices with their start and end apart: 12 -> 14, of which waited for: 9 -> 7; matrix products, arithmetic and copies ran while one was open for 5% -> 1% of each run, Pallas kernels for 0% -> 13%
where the time goes in v2:
time: 39.8 us; the launch traced here: 40 us
  starting transfers between devices  16.5 us (41%)
  waiting for transfers between devices  14.5 us (36%)
  Pallas kernels  7.86 us (20%)
  other arithmetic  0.89 us (2%)
    ppermute x8, starting transfers between devices, swap_req(): return lax.ppermute(x, ('req', 'kv'), pairs)  11.5 us
    ppermute x8, waiting for transfers between devices, swap_req(): return lax.ppermute(x, ('req', 'kv'), pairs)  10.2 us
    ppermute x6, starting transfers between devices, swap_kv(): return lax.ppermute(x, 'kv', [(j, j ^ offset) for j in range(n_kv)])  5.02 us
    ppermute x6, waiting for transfers between devices, swap_kv(): return lax.ppermute(x, 'kv', [(j, j ^ offset) for j in range(n_kv)])  4.24 us
    pallas_call x2, Pallas kernels, load(): pl.pallas_call(load_cache_kernel, out_shape=jax.ShapeDtypeStruct((count,...  3.45 us
    pallas_call x1, Pallas kernels, on_device(): pl.pallas_call(load_weights_kernel, out_shape=tuple((jax.ShapeDtypeStruct...  1.69 us
    pallas_call x1, Pallas kernels, on_device(): pl.pallas_call(lambda *refs: attend_kernel(len(parts), *refs), out_shape=...  1.69 us
  transfers between devices with their start and end apart: 14, of which 7 were waited for; matrix products, arithmetic and copies ran while one was open for 1% of the time, Pallas kernels for 13%

profile of v2, /device:TPU:0, one launch (start us, length us, event | category | flops | bytes accessed | tf_op | source)
XLA Modules:
  0.0 40.0 jit_solution(9392397277574977587)
XLA Ops:
  0.0 0.5 %collective-permute-start = (bf16[8,640]{1,0:T(8,128)(2,1)}, bf16[8,640]{1,0:T(8,128)(2,1)S(1)}, u32[]{:S(2)}, u32[]{:S(2)}) collective-permute-start(bf16[8,640]{1,0:T(8,128)(2,1)} %refs_3_.1), channel_id=1, source_target_pairs={{0,1},{1,0},{2,3},{3,2},{4,5},{5,4},{6,7},{7,6},{8,9},{9,8},{10,11... | collective-permute-start | bytes 30728 | tf_op jit(solution)/shard_map/ppermute | solution.py:64
  0.5 2.6 %collective-permute-start.2 = (bf16[8,640]{1,0:T(8,128)(2,1)}, bf16[8,640]{1,0:T(8,128)(2,1)S(1)}, u32[]{:S(2)}, u32[]{:S(2)}) collective-permute-start(bf16[8,640]{1,0:T(8,128)(2,1)} %refs_3_.1), channel_id=1, source_target_pairs={{0,3},{1,2},{2,1},{3,0},{4,7},{5,6},{6,5},{7,4},{8,11},{9,10},{10,... | collective-permute-start | bytes 30728 | tf_op jit(solution)/shard_map/ppermute | solution.py:64
  3.1 0.0 collective-permute-start.1
  3.1 1.7 %load_weights.1 = (bf16[640,1280]{1,0:T(8,128)(2,1)S(1)}, bf16[640,256]{1,0:T(8,128)(2,1)S(1)}, bf16[640,256]{1,0:T(8,128)(2,1)S(1)}, bf16[8,640]{1,0:T(8,128)(2...) custom-call(bf16[640,1280]{1,0:T(8,128)(2,1)} %refs_0_.1, ...), custom_call_target="tpu_custom_call" | custom-call | bytes 6291456 | tf_op jit(solution)/shard_map/load_weights/pallas_call | solution.py:387
  4.8 0.0 collective-permute-done.refs_1_
  4.9 0.0 collective-permute-done.2.refs_3_
  4.9 2.1 %collective-permute-done.1.refs_2_ = bf16[8,640]{1,0:T(8,128)(2,1)S(1)} collective-permute-done((bf16[8,640]{1,0:T(8,128)(2,1)}, bf16[8,640]{1,0:T(8,128)(2,1)S(1)}, u32[]{:S(2)}, u32[]{:S(2)}) %collective-permute-start.1) | collective-permute-done | bytes 10272 | tf_op jit(solution)/shard_map/ppermute | solution.py:64
  7.0 0.5 %project.1 = (f32[16,1920]{1,0:T(8,128)S(1)}, f32[16,1920]{1,0:T(8,128)S(1)}) custom-call(bf16[8,640]{1,0:T(8,128)(2,1)S(1)} %get-tuple-element.30.refs_0_, bf16[8,640]{1,0:T(8,128)(2,1)S(1)} %collective-permute-done.refs_1_, bf16[8,640]{1,0:T(8,128)(2,1)S(1)} %collective-permute-done.1.refs_2_, bf16[8,640]{1,0:T(8,128)(2,1)S(1)} %collective-permute-done.2.refs_3_, ...), custom_call_target="tpu_custom_call" | custom-call | tf_op jit(solution)/shard_map/project/pallas_call | solution.py:401
  7.5 1.6 %collective-permute-start.3 = (f32[16,1920]{1,0:T(8,128)S(1)}, f32[16,1920]{1,0:T(8,128)S(1)}, u32[]{:S(2)}, u32[]{:S(2)}) collective-permute-start(f32[16,1920]{1,0:T(8,128)S(1)} %get-tuple-element.42), channel_id=1, source_target_pairs={{0,4},{1,9},{2,6},{3,11},{4,0},{5,13},{6,2},{7,15},{8,12},{9,1},{1... | collective-permute-start | bytes 368648 | tf_op jit(solution)/shard_map/ppermute | solution.py:60
  9.1 0.1 fusion
  9.2 0.1 broadcast_in_dim.2.plan.refs_0_
  9.3 1.7 %load_keys.1.refs_10_ = bf16[4,2,4608,128]{3,2,1,0:T(8,128)(2,1)S(1)} custom-call(s32[4,4,128]{2,1,0:T(4,128)S(1)} %broadcast_in_dim.2.plan.refs_0_, bf16[4,2,4096,128]{3,2,1,0:T(8,128)(2,1)} %cache.2), custom_call_target="tpu_custom_call" | custom-call | bytes 6291456 | tf_op jit(solution)/shard_map/load_keys/pallas_call | solution.py:413
  11.0 1.5 %collective-permute-done.3 = f32[16,1920]{1,0:T(8,128)S(1)} collective-permute-done((f32[16,1920]{1,0:T(8,128)S(1)}, f32[16,1920]{1,0:T(8,128)S(1)}, u32[]{:S(2)}, u32[]{:S(2)}) %collective-permute-start.3) | collective-permute-done | bytes 122912 | tf_op jit(solution)/shard_map/ppermute | solution.py:60
  12.5 3.7 %collective-permute-start.6 = (f32[4,1920]{1,0:T(4,128)S(1)}, f32[4,1920]{1,0:T(4,128)S(1)}, u32[]{:S(2)}, u32[]{:S(2)}) collective-permute-start(f32[4,1920]{1,0:T(4,128)S(1)} %get-tuple-element.57), channel_id=1, source_target_pairs={{0,24},{1,21},{2,26},{3,23},{4,28},{5,17},{6,30},{7,19},{8,16},{9,... | collective-permute-start | bytes 92168 | tf_op jit(solution)/shard_map/ppermute | solution.py:60
  16.2 0.0 collective-permute-start.5
  16.2 0.8 %collective-permute-start.4 = (f32[4,1920]{1,0:T(4,128)S(1)}, f32[4,1920]{1,0:T(4,128)S(1)}, u32[]{:S(2)}, u32[]{:S(2)}) collective-permute-start(f32[4,1920]{1,0:T(4,128)S(1)} %get-tuple-element.59), channel_id=1, source_target_pairs={{0,8},{1,5},{2,10},{3,7},{4,12},{5,1},{6,14},{7,3},{8,0},{9,13},{1... | collective-permute-start | bytes 92168 | tf_op jit(solution)/shard_map/ppermute | solution.py:60
  16.9 0.1 pad_maximum_fusion.1
  17.0 1.7 %load_values.1.refs_11_ = bf16[4,2,4608,128]{3,2,1,0:T(8,128)(2,1)S(1)} custom-call(s32[4,4,128]{2,1,0:T(4,128)S(1)} %broadcast_in_dim.2.plan.refs_0_, bf16[4,2,4096,128]{3,2,1,0:T(8,128)(2,1)} %cache.3), custom_call_target="tpu_custom_call" | custom-call | bytes 6291456 | tf_op jit(solution)/shard_map/load_values/pallas_call | solution.py:413
  18.8 0.0 collective-permute-done.6.refs_4_
  18.8 2.2 %collective-permute-done.5.refs_3_ = f32[4,1920]{1,0:T(4,128)S(1)} collective-permute-done((f32[4,1920]{1,0:T(4,128)S(1)}, f32[4,1920]{1,0:T(4,128)S(1)}, u32[]{:S(2)}, u32[]{:S(2)}) %collective-permute-start.5) | collective-permute-done | bytes 30752 | tf_op jit(solution)/shard_map/ppermute | solution.py:60
  21.0 0.0 collective-permute-done.4.refs_2_
  21.0 0.0 copy-start
  21.0 1.7 %attend.1 = bf16[4,1280]{1,0:T(4,128)(2,1)S(1)} custom-call(s32[4,4,128]{2,1,0:T(4,128)S(1)} %broadcast_in_dim.2.plan.refs_0_, f32[4,1920]{1,0:T(4,128)S(1)} %get-tuple-element.44.refs_1_, f32[4,1920]{1,0:T(4,128)S(1)} %collective-permute-done.4.refs_2_, f32[4,1920]{1,0:T(4,128)S(1)} %collective-permute-done.5.refs_3_, ...), custom_call_target="tpu_custom_call" | custom-call | tf_op jit(solution)/shard_map/attend/pallas_call | solution.py:448
  22.6 3.4 %collective-permute-start.9 = (bf16[4,1280]{1,0:T(4,128)(2,1)S(1)}, bf16[4,1280]{1,0:T(4,128)(2,1)S(1)}, u32[]{:S(2)}, u32[]{:S(2)}) collective-permute-start(bf16[4,1280]{1,0:T(4,128)(2,1)S(1)} %attend.1), channel_id=1, source_target_pairs={{0,24},{1,21},{2,26},{3,23},{4,28},{5,17},{6,30},{7,19},{8,16},{9,... | collective-permute-start | bytes 30728 | tf_op jit(solution)/shard_map/ppermute | solution.py:60
  26.0 0.0 collective-permute-start.8
  26.0 1.1 %collective-permute-start.7 = (bf16[4,1280]{1,0:T(4,128)(2,1)S(1)}, bf16[4,1280]{1,0:T(4,128)(2,1)S(1)}, u32[]{:S(2)}, u32[]{:S(2)}) collective-permute-start(bf16[4,1280]{1,0:T(4,128)(2,1)S(1)} %attend.1), channel_id=1, source_target_pairs={{0,8},{1,5},{2,10},{3,7},{4,12},{5,1},{6,14},{7,3},{8,0},{9,13},{1... | collective-permute-start | bytes 30728 | tf_op jit(solution)/shard_map/ppermute | solution.py:60
  27.1 1.2 %collective-permute-done.9 = bf16[4,1280]{1,0:T(4,128)(2,1)S(1)} collective-permute-done((bf16[4,1280]{1,0:T(4,128)(2,1)S(1)}, bf16[4,1280]{1,0:T(4,128)(2,1)S(1)}, u32[]{:S(2)}, u32[]{:S(2)}) %collective-permute-start.9) | collective-permute-done | bytes 10272 | tf_op jit(solution)/shard_map/ppermute | solution.py:60
  28.3 2.3 %collective-permute-done.8 = bf16[4,1280]{1,0:T(4,128)(2,1)S(1)} collective-permute-done((bf16[4,1280]{1,0:T(4,128)(2,1)S(1)}, bf16[4,1280]{1,0:T(4,128)(2,1)S(1)}, u32[]{:S(2)}, u32[]{:S(2)}) %collective-permute-start.8) | collective-permute-done | bytes 10272 | tf_op jit(solution)/shard_map/ppermute | solution.py:60
  30.6 0.0 collective-permute-done.7
  30.6 1.0 %collective-permute-start.10 = (bf16[16,1280]{1,0:T(8,128)(2,1)S(1)}, bf16[16,1280]{1,0:T(8,128)(2,1)S(1)}, u32[]{:S(2)}, u32[]{:S(2)}) collective-permute-start(bf16[16,1280]{1,0:T(8,128)(2,1)S(1)} %pad_maximum_fusion), channel_id=1, source_target_pairs={{0,4},{1,9},{2,6},{3,11},{4,0},{5,13},{6,2},{7,15},{8,12},{9,1},{1... | collective-permute-start | bytes 122888 | tf_op jit(solution)/shard_map/ppermute | solution.py:60
  31.7 3.1 %collective-permute-done.10 = bf16[16,1280]{1,0:T(8,128)(2,1)S(1)} collective-permute-done((bf16[16,1280]{1,0:T(8,128)(2,1)S(1)}, bf16[16,1280]{1,0:T(8,128)(2,1)S(1)}, u32[]{:S(2)}, u32[]{:S(2)}) %collective-permute-start.10) | collective-permute-done | bytes 40992 | tf_op jit(solution)/shard_map/ppermute | solution.py:60
  34.7 0.1 concatenate.16.refs_0_
  34.8 0.0 copy-done
  34.8 0.5 %output.1 = (f32[8,640]{1,0:T(8,128)S(1)}, f32[8,640]{1,0:T(8,128)S(1)}, f32[8,640]{1,0:T(8,128)S(1)}, f32[8,640]{1,0:T(8,128)S(1)}) custom-call(bf16[32,1280]{1,0:T(8,128)(2,1)S(1)} %concatenate.16.refs_0_, bf16[1280,640]{1,0:T(8,128)(2,1)S(1)} %copy-done), custom_call_target="tpu_custom_call" | custom-call | tf_op jit(solution)/shard_map/output/pallas_call | solution.py:481
  35.3 0.1 collective-permute-start.11
  35.4 0.6 %collective-permute-start.12 = (f32[8,640]{1,0:T(8,128)S(1)}, f32[8,640]{1,0:T(8,128)S(1)}, u32[]{:S(2)}, u32[]{:S(2)}) collective-permute-start(f32[8,640]{1,0:T(8,128)S(1)} %get-tuple-element.53), channel_id=1, source_target_pairs={{0,2},{1,3},{2,0},{3,1},{4,6},{5,7},{6,4},{7,5},{8,10},{9,11},{10,... | collective-permute-start | bytes 61448 | tf_op jit(solution)/shard_map/ppermute | solution.py:64
  35.9 1.3 %collective-permute-start.13 = (f32[8,640]{1,0:T(8,128)S(1)}, f32[8,640]{1,0:T(8,128)S(1)}, u32[]{:S(2)}, u32[]{:S(2)}) collective-permute-start(f32[8,640]{1,0:T(8,128)S(1)} %get-tuple-element.54), channel_id=1, source_target_pairs={{0,3},{1,2},{2,1},{3,0},{4,7},{5,6},{6,5},{7,4},{8,11},{9,10},{10,... | collective-permute-start | bytes 61448 | tf_op jit(solution)/shard_map/ppermute | solution.py:64
  37.2 0.0 collective-permute-done.11
  37.2 2.1 %collective-permute-done.12 = f32[8,640]{1,0:T(8,128)S(1)} collective-permute-done((f32[8,640]{1,0:T(8,128)S(1)}, f32[8,640]{1,0:T(8,128)S(1)}, u32[]{:S(2)}, u32[]{:S(2)}) %collective-permute-start.12) | collective-permute-done | bytes 20512 | tf_op jit(solution)/shard_map/ppermute | solution.py:64
  39.4 0.0 collective-permute-done.13
  39.4 0.6 %add_convert_fusion = bf16[8,640]{1,0:T(8,128)(2,1)} fusion(f32[8,640]{1,0:T(8,128)S(1)} %collective-permute-done.13, f32[8,640]{1,0:T(8,128)S(1)} %collective-permute-done.12, f32[8,640]{1,0:T(8,128)S(1)} %get-tuple-element.51, f32[8,640]{1,0:T(8,128)S(1)} %collective-permute-done.11), kind=kLoop, calls=%fused_computation.1 | loop fusion | flops 20480 | bytes 92160 | tf_op jit(solution)/shard_map/convert_element_type | solution.py:492
  (7 shorter events, 0.1 us)
Async XLA Ops:
  0.0 4.8 %collective-permute-start = (bf16[8,640]{1,0:T(8,128)(2,1)}, bf16[8,640]{1,0:T(8,128)(2,1)S(1)}, u32[]{:S(2)}, u32[]{:S(2)}) collective-permute-start(bf16[8,640]{1,0:T(8,128)(2,1)} %refs_3_.1), channel_id=1, source_target_pairs={{0,1},{1,0},{2,3},{3,2},{4,5},{5,4},{6,7},{7,6},{8,9},{9,8},{10,11... | collective-permute-start | bytes 30728 | tf_op jit(solution)/shard_map/ppermute | solution.py:64
  0.5 4.4 %collective-permute-start.2 = (bf16[8,640]{1,0:T(8,128)(2,1)}, bf16[8,640]{1,0:T(8,128)(2,1)S(1)}, u32[]{:S(2)}, u32[]{:S(2)}) collective-permute-start(bf16[8,640]{1,0:T(8,128)(2,1)} %refs_3_.1), channel_id=1, source_target_pairs={{0,3},{1,2},{2,1},{3,0},{4,7},{5,6},{6,5},{7,4},{8,11},{9,10},{10,... | collective-permute-start | bytes 30728 | tf_op jit(solution)/shard_map/ppermute | solution.py:64
  3.1 3.9 %collective-permute-start.1 = (bf16[8,640]{1,0:T(8,128)(2,1)}, bf16[8,640]{1,0:T(8,128)(2,1)S(1)}, u32[]{:S(2)}, u32[]{:S(2)}) collective-permute-start(bf16[8,640]{1,0:T(8,128)(2,1)} %refs_3_.1), channel_id=1, source_target_pairs={{0,2},{1,3},{2,0},{3,1},{4,6},{5,7},{6,4},{7,5},{8,10},{9,11},{10,... | collective-permute-start | bytes 30728 | tf_op jit(solution)/shard_map/ppermute | solution.py:64
  7.5 4.9 %collective-permute-start.3 = (f32[16,1920]{1,0:T(8,128)S(1)}, f32[16,1920]{1,0:T(8,128)S(1)}, u32[]{:S(2)}, u32[]{:S(2)}) collective-permute-start(f32[16,1920]{1,0:T(8,128)S(1)} %get-tuple-element.42), channel_id=1, source_target_pairs={{0,4},{1,9},{2,6},{3,11},{4,0},{5,13},{6,2},{7,15},{8,12},{9,1},{1... | collective-permute-start | bytes 368648 | tf_op jit(solution)/shard_map/ppermute | solution.py:60
  12.5 6.3 %collective-permute-start.6 = (f32[4,1920]{1,0:T(4,128)S(1)}, f32[4,1920]{1,0:T(4,128)S(1)}, u32[]{:S(2)}, u32[]{:S(2)}) collective-permute-start(f32[4,1920]{1,0:T(4,128)S(1)} %get-tuple-element.57), channel_id=1, source_target_pairs={{0,24},{1,21},{2,26},{3,23},{4,28},{5,17},{6,30},{7,19},{8,16},{9,... | collective-permute-start | bytes 92168 | tf_op jit(solution)/shard_map/ppermute | solution.py:60
  16.2 4.8 %collective-permute-start.5 = (f32[4,1920]{1,0:T(4,128)S(1)}, f32[4,1920]{1,0:T(4,128)S(1)}, u32[]{:S(2)}, u32[]{:S(2)}) collective-permute-start(f32[4,1920]{1,0:T(4,128)S(1)} %get-tuple-element.58), channel_id=1, source_target_pairs={{0,16},{1,17},{2,18},{3,19},{4,20},{5,21},{6,22},{7,23},{8,24},{9,... | collective-permute-start | bytes 92168 | tf_op jit(solution)/shard_map/ppermute | solution.py:60
  16.2 4.8 %collective-permute-start.4 = (f32[4,1920]{1,0:T(4,128)S(1)}, f32[4,1920]{1,0:T(4,128)S(1)}, u32[]{:S(2)}, u32[]{:S(2)}) collective-permute-start(f32[4,1920]{1,0:T(4,128)S(1)} %get-tuple-element.59), channel_id=1, source_target_pairs={{0,8},{1,5},{2,10},{3,7},{4,12},{5,1},{6,14},{7,3},{8,0},{9,13},{1... | collective-permute-start | bytes 92168 | tf_op jit(solution)/shard_map/ppermute | solution.py:60
  21.0 13.8 %copy-start = (bf16[1280,640]{1,0:T(8,128)(2,1)S(1)}, bf16[1280,640]{1,0:T(8,128)(2,1)}, u32[]{:S(2)}) copy-start(bf16[1280,640]{1,0:T(8,128)(2,1)} %refs_1_.3) | copy-start | bytes 4915204
  22.6 5.6 %collective-permute-start.9 = (bf16[4,1280]{1,0:T(4,128)(2,1)S(1)}, bf16[4,1280]{1,0:T(4,128)(2,1)S(1)}, u32[]{:S(2)}, u32[]{:S(2)}) collective-permute-start(bf16[4,1280]{1,0:T(4,128)(2,1)S(1)} %attend.1), channel_id=1, source_target_pairs={{0,24},{1,21},{2,26},{3,23},{4,28},{5,17},{6,30},{7,19},{8,16},{9,... | collective-permute-start | bytes 30728 | tf_op jit(solution)/shard_map/ppermute | solution.py:60
  26.0 4.6 %collective-permute-start.8 = (bf16[4,1280]{1,0:T(4,128)(2,1)S(1)}, bf16[4,1280]{1,0:T(4,128)(2,1)S(1)}, u32[]{:S(2)}, u32[]{:S(2)}) collective-permute-start(bf16[4,1280]{1,0:T(4,128)(2,1)S(1)} %attend.1), channel_id=1, source_target_pairs={{0,16},{1,17},{2,18},{3,19},{4,20},{5,21},{6,22},{7,23},{8,24},{9,... | collective-permute-start | bytes 30728 | tf_op jit(solution)/shard_map/ppermute | solution.py:60
  26.0 4.6 %collective-permute-start.7 = (bf16[4,1280]{1,0:T(4,128)(2,1)S(1)}, bf16[4,1280]{1,0:T(4,128)(2,1)S(1)}, u32[]{:S(2)}, u32[]{:S(2)}) collective-permute-start(bf16[4,1280]{1,0:T(4,128)(2,1)S(1)} %attend.1), channel_id=1, source_target_pairs={{0,8},{1,5},{2,10},{3,7},{4,12},{5,1},{6,14},{7,3},{8,0},{9,13},{1... | collective-permute-start | bytes 30728 | tf_op jit(solution)/shard_map/ppermute | solution.py:60
  30.6 4.1 %collective-permute-start.10 = (bf16[16,1280]{1,0:T(8,128)(2,1)S(1)}, bf16[16,1280]{1,0:T(8,128)(2,1)S(1)}, u32[]{:S(2)}, u32[]{:S(2)}) collective-permute-start(bf16[16,1280]{1,0:T(8,128)(2,1)S(1)} %pad_maximum_fusion), channel_id=1, source_target_pairs={{0,4},{1,9},{2,6},{3,11},{4,0},{5,13},{6,2},{7,15},{8,12},{9,1},{1... | collective-permute-start | bytes 122888 | tf_op jit(solution)/shard_map/ppermute | solution.py:60
  35.3 1.9 %collective-permute-start.11 = (f32[8,640]{1,0:T(8,128)S(1)}, f32[8,640]{1,0:T(8,128)S(1)}, u32[]{:S(2)}, u32[]{:S(2)}) collective-permute-start(f32[8,640]{1,0:T(8,128)S(1)} %get-tuple-element.52), channel_id=1, source_target_pairs={{0,1},{1,0},{2,3},{3,2},{4,5},{5,4},{6,7},{7,6},{8,9},{9,8},{10,11... | collective-permute-start | bytes 61448 | tf_op jit(solution)/shard_map/ppermute | solution.py:64
  35.4 4.0 %collective-permute-start.12 = (f32[8,640]{1,0:T(8,128)S(1)}, f32[8,640]{1,0:T(8,128)S(1)}, u32[]{:S(2)}, u32[]{:S(2)}) collective-permute-start(f32[8,640]{1,0:T(8,128)S(1)} %get-tuple-element.53), channel_id=1, source_target_pairs={{0,2},{1,3},{2,0},{3,1},{4,6},{5,7},{6,4},{7,5},{8,10},{9,11},{10,... | collective-permute-start | bytes 61448 | tf_op jit(solution)/shard_map/ppermute | solution.py:64
  35.9 3.4 %collective-permute-start.13 = (f32[8,640]{1,0:T(8,128)S(1)}, f32[8,640]{1,0:T(8,128)S(1)}, u32[]{:S(2)}, u32[]{:S(2)}) collective-permute-start(f32[8,640]{1,0:T(8,128)S(1)} %get-tuple-element.54), channel_id=1, source_target_pairs={{0,3},{1,2},{2,1},{3,0},{4,7},{5,6},{6,5},{7,4},{8,11},{9,10},{10,... | collective-permute-start | bytes 61448 | tf_op jit(solution)/shard_map/ppermute | solution.py:64

commit v3 on v2

--- a/solution.py
+++ b/solution.py
@@ -12,8 +12,9 @@
 EPS = 1e-06
 BLOCK = 512
 PLAN_BITS = 4
-TOGETHER = 4
+TOGETHER = 8
 LANES = 128
+FAR = 1 << 20
 STAGE_BITS = 2
 
 EXTRA_ROWS = 16
@@ -58,6 +59,10 @@
         for j in range(n_kv)
     ]
     return lax.ppermute(x, ("req", "kv"), pairs)
+
+
+def kept(n_kv):
+    return [0] + list(range(3, n_kv, 2))
 
 
 def swap_kv(x, n_kv, offset):
@@ -177,6 +182,10 @@
         k_extra,
         v_extra,
         result_buf,
+        q_rows,
+        tops,
+        denoms,
+        numers,
     ) = refs[n_parts:]
     count, heads_kv, _, size = k_buf.shape
     q_cols, kv_cols = context.shape[1], heads_kv * size
@@ -222,7 +231,7 @@
     lane = lax.broadcasted_iota(jnp.int32, (1, EXTRA_ROWS), 1)
     offset = lax.broadcasted_iota(jnp.int32, (1, BLOCK), 1)
     repeats = BLOCK // LANES
-    queries = [q_heads[r].astype(jnp.bfloat16) for r in range(count)]
+    q_rows[...] = q_heads[...].astype(jnp.bfloat16)
 
     def both(buf, r, t):
         rows = pl.ds(pl.multiple_of(t * BLOCK, BLOCK), BLOCK)
@@ -234,39 +243,48 @@
             pieces = [op(*pieces[i : i + 2]) for i in range(0, len(pieces), 2)]
         return pieces[0]
 
-    def score(r, t, last):
+    def score(r, t, place, at):
         s = (
             lax.dot_general(
-                queries[r],
-                both(k_buf, r, jnp.minimum(t, last)),
-                contract_last,
-                preferred_element_type=jnp.float32,
+                q_rows[r], both(k_buf, r, t), contract_last, preferred_element_type=jnp.float32
             )
             * scale
         )
-        position = t * BLOCK + offset
-        low, high = (jnp.concatenate([plan[i, r : r + 1]] * repeats, 1) for i in range(2))
+        position = at + offset
+        low, high = (
+            jnp.concatenate([plan[i, pl.ds(r, 1)]] * repeats, 1) for i in range(2)
+        )
         s = jnp.where((position >= low) & (position < high), s, -jnp.inf)
-        score_buf[r, t] = s
+        score_buf[place] = s
         return fold(s, jnp.maximum)
 
-    def mix(r, t, last, top):
-        weights = jnp.exp(score_buf[r, t] - top)
+    def mix(r, t, place):
+        weights = jnp.exp(score_buf[place] - jnp.concatenate([tops[r]] * repeats, 1))
         product = jnp.dot(
-            weights.astype(jnp.bfloat16),
-            both(v_buf, r, jnp.minimum(t, last)),
-            preferred_element_type=jnp.float32,
+            weights.astype(jnp.bfloat16), both(v_buf, r, t), preferred_element_type=jnp.float32
         )
         return fold(weights, jnp.add), product
 
-    def rounds(visits):
-        return (visits - 1 + TOGETHER - 1) // TOGETHER
-
-    extras, tops = [], []
+    starts = [0]
+    for _, visits in planned:
+        starts.append(starts[-1] + visits - 1)
+    left = starts[-1]
+
+    def block_of(place):
+        inside = jnp.minimum(place, left - 1)
+        r, start = 0, 0
+        for i in range(1, count):
+            past = inside >= starts[i]
+            r = jnp.where(past, i, r)
+            start = jnp.where(past, starts[i], start)
+        return r, inside - start + 1
+
+    rounds = (left + TOGETHER - 1) // TOGETHER
+    extras = []
     for r in range(count):
         extra = (
             lax.dot_general(
-                queries[r],
+                q_rows[r],
                 k_extra[r].astype(jnp.bfloat16),
                 contract_last,
                 preferred_element_type=jnp.float32,
@@ -275,44 +293,42 @@
         )
         live = (lane < plan[2, r : r + 1, :EXTRA_ROWS]) | (lane == SINKS)
         extras.append(jnp.where(live, extra, -jnp.inf))
-        tops.append(score(r, 0, 0))
+        tops[r] = score(r, 0, r, 0)
+
+    @pl.loop(0, rounds)
+    def _(k):
+        for i in range(TOGETHER):
+            place = k * TOGETHER + i
+            r, t = block_of(place)
+            at = jnp.where(place < left, t * BLOCK, FAR)
+            tops[r] = jnp.maximum(tops[r], score(r, t, count + place, at))
+
     for r in range(count):
-        visits = planned[r][1]
-
-        def more_scores(k, top):
-            for i in range(TOGETHER):
-                top = jnp.maximum(top, score(r, 1 + k * TOGETHER + i, visits - 1))
-            return top
-
-        tops[r] = lax.fori_loop(0, rounds(visits), more_scores, tops[r])
-    sums = []
-    for r in range(count):
-        tops[r] = jnp.maximum(
+        top = jnp.maximum(
             jnp.max(tops[r], 1, keepdims=True), jnp.max(extras[r], 1, keepdims=True)
         )
-        extras[r] = jnp.exp(extras[r] - tops[r])
+        tops[r] = jnp.broadcast_to(top, tops.shape[1:])
+        extras[r] = jnp.exp(extras[r] - top)
         numer = jnp.dot(
             extras[r].astype(jnp.bfloat16),
             v_extra[r].astype(jnp.bfloat16),
             preferred_element_type=jnp.float32,
         )
-        denom, product = mix(r, 0, 0, tops[r])
-        sums.append((denom, numer + product))
+        denoms[r], product = mix(r, 0, r)
+        numers[r] = numer + product
+
+    @pl.loop(0, rounds)
+    def _(k):
+        for i in range(TOGETHER):
+            place = k * TOGETHER + i
+            r, t = block_of(place)
+            denom, product = mix(r, t, count + place)
+            denoms[r] += denom
+            numers[r] += product
+
     for r in range(count):
-        visits = planned[r][1]
-
-        def more_values(k, carry):
-            denom, numer = carry
-            for i in range(TOGETHER):
-                d, n = mix(r, 1 + k * TOGETHER + i, visits - 1, tops[r])
-                denom, numer = denom + d, numer + n
-            return denom, numer
-
-        sums[r] = lax.fori_loop(0, rounds(visits), more_values, sums[r])
-    for r in range(count):
-        denom, numer = sums[r]
-        denom = jnp.sum(denom, 1, keepdims=True) + jnp.sum(extras[r], 1, keepdims=True)
-        result = numer / denom
+        denom = jnp.sum(denoms[r], 1, keepdims=True) + jnp.sum(extras[r], 1, keepdims=True)
+        result = numers[r] / denom
         for h in range(heads_kv):
             for g in range(group):
                 head = h * group + g
@@ -322,18 +338,47 @@
     context[...] = result_buf[...].astype(context.dtype)
 
 
-def output_kernel(rows_kv, context, w_output, *outs):
+def output_kernel(rows_kv, context, w_output, keep, send):
     size = context.shape[0]
     rows_req = size // lax.axis_size("req")
     order = row_order(size, rows_req, rows_kv, True)
     rows = jnp.dot(order, context[...], preferred_element_type=jnp.float32).astype(jnp.bfloat16)
     product = jnp.dot(rows, w_output[...], preferred_element_type=jnp.float32)
-    for u, out in enumerate(outs):
-        out[...] = product[u * rows_kv : (u + 1) * rows_kv]
+    for i, u in enumerate(kept(size // rows_kv)):
+        place = slice(i * rows_kv, (i + 1) * rows_kv)
+        keep[place] = product[u * rows_kv : (u + 1) * rows_kv]
+        send[place] = product[(u ^ 1) * rows_kv : ((u ^ 1) + 1) * rows_kv]
 
 
 def spec(space=pltpu.VMEM):
     return pl.BlockSpec(memory_space=space)
+
+
+def attend_call(plan, parts, cosine, sine, b_query, b_key, b_value, k_live, v_live, *sinks):
+    count, heads_kv, stored, size = k_live.shape
+    group = b_query.shape[0] // heads_kv
+    rows, kv_cols = heads_kv * (-(-group // 8) * 8), heads_kv * size
+    q_cols = b_query.shape[0] * size
+    args = (plan, *parts, cosine, sine, b_query, b_key, b_value, k_live, v_live, *sinks)
+    return pl.pallas_call(
+        lambda *refs: attend_kernel(len(parts), *refs),
+        out_shape=jax.ShapeDtypeStruct((count, q_cols), jnp.bfloat16),
+        in_specs=[spec()] * len(args),
+        out_specs=spec(),
+        scratch_shapes=[
+            pltpu.VMEM((count * (stored // BLOCK) + TOGETHER, rows, BLOCK), jnp.float32),
+            pltpu.VMEM((count, rows, kv_cols), jnp.float32),
+            pltpu.VMEM((count, EXTRA_ROWS, kv_cols), jnp.float32),
+            pltpu.VMEM((count, EXTRA_ROWS, kv_cols), jnp.float32),
+            pltpu.VMEM((count, q_cols), jnp.float32),
+            pltpu.VMEM((count, rows, kv_cols), jnp.bfloat16),
+            pltpu.VMEM((count, rows, LANES), jnp.float32),
+            pltpu.VMEM((count, rows, LANES), jnp.float32),
+            pltpu.VMEM((count, rows, kv_cols), jnp.float32),
+        ],
+        compiler_params=pltpu.CompilerParams(vmem_limit_bytes=8 << 20),
+        name="attend",
+    )(*args)
 
 
 def in_hbm(x):
@@ -363,11 +408,10 @@
     rows_kv = hidden.shape[0]
     rows = count * n_req
     q_cols, kv_cols = w_query.shape[1], w_key.shape[1]
-    group = q_cols // (heads_kv * size)
     wide = q_cols + 2 * kv_cols + LANES
     f32, bf16 = jnp.float32, jnp.bfloat16
 
-    others = [swap_kv(hidden, n_kv, u) for u in range(1, n_kv)]
+    others = [swap_kv(hidden, n_kv, u) for u in range(1, n_kv, 2)]
     chunk = LANES if gain.shape[0] % LANES == 0 else gain.shape[0]
     wanted = (
         w_query,
@@ -396,7 +440,9 @@
     )(*[in_hbm(w) for w in wanted])
     *weights, mine, gain, b_query, b_key, b_value, sink_keys, sink_values = fetched[:-3]
     lengths, sink_count, window = fetched[-3:]
-    pieces = [mine] + others
+    pieces = [mine, others[0]]
+    for far in others[1:]:
+        pieces += [swap_kv(far, n_kv, 1), far]
     half = jax.ShapeDtypeStruct((rows // 2, wide), f32)
     keep, send = pl.pallas_call(
         lambda *refs: project_kernel(count, n_kv, *refs),
@@ -444,51 +490,27 @@
     cosine = jnp.concatenate([cos, cos], 1)
     sine = jnp.concatenate([-sin, sin], 1)
 
-    pad = -(-group // 8) * 8
-    context = pl.pallas_call(
-        lambda *refs: attend_kernel(len(parts), *refs),
-        out_shape=jax.ShapeDtypeStruct((count, q_cols), bf16),
-        in_specs=[spec()] * (len(parts) + 10),
-        out_specs=spec(),
-        scratch_shapes=[
-            pltpu.VMEM((count, visits + TOGETHER, heads_kv * pad, BLOCK), f32),
-            pltpu.VMEM((count, heads_kv * pad, heads_kv * size), f32),
-            pltpu.VMEM((count, EXTRA_ROWS, heads_kv * size), f32),
-            pltpu.VMEM((count, EXTRA_ROWS, heads_kv * size), f32),
-            pltpu.VMEM((count, q_cols), f32),
-        ],
-        compiler_params=pltpu.CompilerParams(vmem_limit_bytes=8 << 20),
-        name="attend",
-    )(
-        plan,
-        *parts,
-        cosine,
-        sine,
-        b_query,
-        b_key,
-        b_value,
-        k_live,
-        v_live,
-        sink_keys,
-        sink_values,
+    context = attend_call(
+        plan, parts, cosine, sine, b_query, b_key, b_value, k_live, v_live, sink_keys, sink_values
     )
 
     everyone = context
     for radix, unit in reversed(stages(n_req, STAGE_BITS)):
         blocks = [swap_req(everyone, n_req, n_kv, q * unit) for q in range(1, radix)]
         everyone = jnp.concatenate([everyone] + blocks, 0)
-    piece = jax.ShapeDtypeStruct((rows_kv, w_output.shape[1]), f32)
-    products = pl.pallas_call(
+    half = jax.ShapeDtypeStruct((rows // 2, w_output.shape[1]), f32)
+    keep, send = pl.pallas_call(
         lambda *refs: output_kernel(rows_kv, *refs),
-        out_shape=(piece,) * n_kv,
+        out_shape=(half, half),
         in_specs=[spec()] * 2,
-        out_specs=(spec(),) * n_kv,
+        out_specs=(spec(), spec()),
         compiler_params=pltpu.CompilerParams(vmem_limit_bytes=16 << 20),
         name="output",
     )(everyone, w_output)
-    result = products[0]
-    for u in range(1, n_kv):
-        result = result + swap_kv(products[u], n_kv, u)
+    both = keep + swap_kv(send, n_kv, 1)
+    result = both[:rows_kv]
+    for i, u in enumerate(kept(n_kv)[1:], 1):
+        result = result + swap_kv(both[i * rows_kv : (i + 1) * rows_kv], n_kv, u)
     return result.astype(bf16)
 
 

time: 39.8 us -> 39.3 us (0.987); the launches traced: 40 us -> 39 us
  waiting for transfers between devices: 14.5 us -> 13.3 us
  Pallas kernels: 7.86 us -> 8.45 us
  starting transfers between devices: 16.5 us -> 16.1 us
    ppermute x8, waiting for transfers between devices: 10.2 us -> 8.93 us  [swap_req(): return lax.ppermute(x, ('req', 'kv'), pairs)]
    ppermute x6 -> x5, starting transfers between devices: 5.02 us -> 4.52 us  [swap_kv(): return lax.ppermute(x, 'kv', [(j, j ^ offset) for j in range(n_kv)])]
    pallas_call x2, Pallas kernels: 2.19 us -> 2.62 us  [the longest x1 2.12 us: attend_call(): pl.pallas_call(lambda *refs: attend_kernel(len(parts), *refs), out_shape=...]
    ppermute x6 -> x5, waiting for transfers between devices: 4.24 us -> 4.32 us  [swap_kv(): return lax.ppermute(x, 'kv', [(j, j ^ offset) for j in range(n_kv)])]
  transfers between devices with their start and end apart: 14 -> 13, of which waited for: 7 -> 9; matrix products, arithmetic and copies ran while one was open for 1% -> 1% of each run, Pallas kernels for 13% -> 14%
where the time goes in v3:
time: 39.3 us; the launch traced here: 39 us
  starting transfers between devices  16.1 us (41%)
  waiting for transfers between devices  13.3 us (34%)
  Pallas kernels  8.45 us (22%)
  other arithmetic  0.89 us (2%)
    ppermute x8, starting transfers between devices, swap_req(): return lax.ppermute(x, ('req', 'kv'), pairs)  11.6 us
    ppermute x8, waiting for transfers between devices, swap_req(): return lax.ppermute(x, ('req', 'kv'), pairs)  8.93 us
    ppermute x5, starting transfers between devices, swap_kv(): return lax.ppermute(x, 'kv', [(j, j ^ offset) for j in range(n_kv)])  4.52 us
    ppermute x5, waiting for transfers between devices, swap_kv(): return lax.ppermute(x, 'kv', [(j, j ^ offset) for j in range(n_kv)])  4.32 us
    pallas_call x2, Pallas kernels, load(): pl.pallas_call(load_cache_kernel, out_shape=jax.ShapeDtypeStruct((count,...  3.61 us
    pallas_call x1, Pallas kernels, attend_call(): pl.pallas_call(lambda *refs: attend_kernel(len(parts), *refs), out_shape=...  2.12 us
    pallas_call x1, Pallas kernels, on_device(): pl.pallas_call(load_weights_kernel, out_shape=tuple((jax.ShapeDtypeStruct...  1.69 us
  transfers between devices with their start and end apart: 13, of which 9 were waited for; matrix products, arithmetic and copies ran while one was open for 1% of the time, Pallas kernels for 14%

profile of v3, /device:TPU:0, one launch (start us, length us, event | category | flops | bytes accessed | tf_op | source)
XLA Modules:
  0.0 39.0 jit_solution(2613043349871031968)
XLA Ops:
  0.0 2.4 %collective-permute-start.1 = (bf16[8,640]{1,0:T(8,128)(2,1)}, bf16[8,640]{1,0:T(8,128)(2,1)S(1)}, u32[]{:S(2)}, u32[]{:S(2)}) collective-permute-start(bf16[8,640]{1,0:T(8,128)(2,1)} %refs_3_.1), channel_id=1, source_target_pairs={{0,3},{1,2},{2,1},{3,0},{4,7},{5,6},{6,5},{7,4},{8,11},{9,10},{10,... | collective-permute-start | bytes 30728 | tf_op jit(solution)/shard_map/ppermute | solution.py:69
  2.4 0.7 %collective-permute-start = (bf16[8,640]{1,0:T(8,128)(2,1)}, bf16[8,640]{1,0:T(8,128)(2,1)S(1)}, u32[]{:S(2)}, u32[]{:S(2)}) collective-permute-start(bf16[8,640]{1,0:T(8,128)(2,1)} %refs_3_.1), channel_id=1, source_target_pairs={{0,1},{1,0},{2,3},{3,2},{4,5},{5,4},{6,7},{7,6},{8,9},{9,8},{10,11... | collective-permute-start | bytes 30728 | tf_op jit(solution)/shard_map/ppermute | solution.py:69
  3.1 1.7 %load_weights.1 = (bf16[640,1280]{1,0:T(8,128)(2,1)S(1)}, bf16[640,256]{1,0:T(8,128)(2,1)S(1)}, bf16[640,256]{1,0:T(8,128)(2,1)S(1)}, bf16[8,640]{1,0:T(8,128)(2...) custom-call(bf16[640,1280]{1,0:T(8,128)(2,1)} %refs_0_.1, ...), custom_call_target="tpu_custom_call" | custom-call | bytes 6291456 | tf_op jit(solution)/shard_map/load_weights/pallas_call | solution.py:431
  4.8 0.0 collective-permute-done.1.refs_3_
  4.8 0.1 collective-permute-start.2
  4.9 0.0 collective-permute-done.refs_1_
  4.9 1.1 %collective-permute-done.2.refs_2_ = bf16[8,640]{1,0:T(8,128)(2,1)S(1)} collective-permute-done((bf16[8,640]{1,0:T(8,128)(2,1)S(1)}, bf16[8,640]{1,0:T(8,128)(2,1)S(1)}, u32[]{:S(2)}, u32[]{:S(2)}) %collective-permute-start.2) | collective-permute-done | bytes 10272 | tf_op jit(solution)/shard_map/ppermute | solution.py:69
  6.1 0.5 %project.1 = (f32[16,1920]{1,0:T(8,128)S(1)}, f32[16,1920]{1,0:T(8,128)S(1)}) custom-call(bf16[8,640]{1,0:T(8,128)(2,1)S(1)} %get-tuple-element.28.refs_0_, bf16[8,640]{1,0:T(8,128)(2,1)S(1)} %collective-permute-done.refs_1_, bf16[8,640]{1,0:T(8,128)(2,1)S(1)} %collective-permute-done.2.refs_2_, bf16[8,640]{1,0:T(8,128)(2,1)S(1)} %collective-permute-done.1.refs_3_, ...), custom_call_target="tpu_custom_call" | custom-call | tf_op jit(solution)/shard_map/project/pallas_call | solution.py:447
  6.6 1.6 %collective-permute-start.3 = (f32[16,1920]{1,0:T(8,128)S(1)}, f32[16,1920]{1,0:T(8,128)S(1)}, u32[]{:S(2)}, u32[]{:S(2)}) collective-permute-start(f32[16,1920]{1,0:T(8,128)S(1)} %get-tuple-element.40), channel_id=1, source_target_pairs={{0,4},{1,9},{2,6},{3,11},{4,0},{5,13},{6,2},{7,15},{8,12},{9,1},{1... | collective-permute-start | bytes 368648 | tf_op jit(solution)/shard_map/ppermute | solution.py:61
  8.2 0.1 fusion.1
  8.3 0.1 broadcast_in_dim.2.plan.refs_0_
  8.4 1.8 %load_keys.1.refs_10_ = bf16[4,2,4608,128]{3,2,1,0:T(8,128)(2,1)S(1)} custom-call(s32[4,4,128]{2,1,0:T(4,128)S(1)} %broadcast_in_dim.2.plan.refs_0_, bf16[4,2,4096,128]{3,2,1,0:T(8,128)(2,1)} %cache.2), custom_call_target="tpu_custom_call" | custom-call | bytes 6291456 | tf_op jit(solution)/shard_map/load_keys/pallas_call | solution.py:459
  10.2 1.4 %collective-permute-done.3 = f32[16,1920]{1,0:T(8,128)S(1)} collective-permute-done((f32[16,1920]{1,0:T(8,128)S(1)}, f32[16,1920]{1,0:T(8,128)S(1)}, u32[]{:S(2)}, u32[]{:S(2)}) %collective-permute-start.3) | collective-permute-done | bytes 122912 | tf_op jit(solution)/shard_map/ppermute | solution.py:61
  11.6 3.7 %collective-permute-start.6 = (f32[4,1920]{1,0:T(4,128)S(1)}, f32[4,1920]{1,0:T(4,128)S(1)}, u32[]{:S(2)}, u32[]{:S(2)}) collective-permute-start(f32[4,1920]{1,0:T(4,128)S(1)} %get-tuple-element.53), channel_id=1, source_target_pairs={{0,24},{1,21},{2,26},{3,23},{4,28},{5,17},{6,30},{7,19},{8,16},{9,... | collective-permute-start | bytes 92168 | tf_op jit(solution)/shard_map/ppermute | solution.py:61
  15.3 0.0 collective-permute-start.5
  15.3 0.8 %collective-permute-start.4 = (f32[4,1920]{1,0:T(4,128)S(1)}, f32[4,1920]{1,0:T(4,128)S(1)}, u32[]{:S(2)}, u32[]{:S(2)}) collective-permute-start(f32[4,1920]{1,0:T(4,128)S(1)} %get-tuple-element.55), channel_id=1, source_target_pairs={{0,8},{1,5},{2,10},{3,7},{4,12},{5,1},{6,14},{7,3},{8,0},{9,13},{1... | collective-permute-start | bytes 92168 | tf_op jit(solution)/shard_map/ppermute | solution.py:61
  16.1 0.1 pad_maximum_fusion.1
  16.1 1.8 %load_values.1.refs_11_ = bf16[4,2,4608,128]{3,2,1,0:T(8,128)(2,1)S(1)} custom-call(s32[4,4,128]{2,1,0:T(4,128)S(1)} %broadcast_in_dim.2.plan.refs_0_, bf16[4,2,4096,128]{3,2,1,0:T(8,128)(2,1)} %cache.3), custom_call_target="tpu_custom_call" | custom-call | bytes 6291456 | tf_op jit(solution)/shard_map/load_values/pallas_call | solution.py:459
  17.9 0.0 collective-permute-done.6.refs_4_
  18.0 2.1 %collective-permute-done.5.refs_3_ = f32[4,1920]{1,0:T(4,128)S(1)} collective-permute-done((f32[4,1920]{1,0:T(4,128)S(1)}, f32[4,1920]{1,0:T(4,128)S(1)}, u32[]{:S(2)}, u32[]{:S(2)}) %collective-permute-start.5) | collective-permute-done | bytes 30752 | tf_op jit(solution)/shard_map/ppermute | solution.py:61
  20.1 0.0 collective-permute-done.4.refs_2_
  20.1 0.0 copy-start
  20.1 2.1 %attend.1 = bf16[4,1280]{1,0:T(4,128)(2,1)S(1)} custom-call(s32[4,4,128]{2,1,0:T(4,128)S(1)} %broadcast_in_dim.2.plan.refs_0_, f32[4,1920]{1,0:T(4,128)S(1)} %get-tuple-element.42.refs_1_, f32[4,1920]{1,0:T(4,128)S(1)} %collective-permute-done.4.refs_2_, f32[4,1920]{1,0:T(4,128)S(1)} %collective-permute-done.5.refs_3_, ...), custom_call_target="tpu_custom_call" | custom-call | tf_op jit(solution)/shard_map/attend/pallas_call | solution.py:363
  22.2 1.8 %collective-permute-start.9 = (bf16[4,1280]{1,0:T(4,128)(2,1)S(1)}, bf16[4,1280]{1,0:T(4,128)(2,1)S(1)}, u32[]{:S(2)}, u32[]{:S(2)}) collective-permute-start(bf16[4,1280]{1,0:T(4,128)(2,1)S(1)} %attend.1), channel_id=1, source_target_pairs={{0,24},{1,21},{2,26},{3,23},{4,28},{5,17},{6,30},{7,19},{8,16},{9,... | collective-permute-start | bytes 30728 | tf_op jit(solution)/shard_map/ppermute | solution.py:61
  24.0 1.4 %collective-permute-start.8 = (bf16[4,1280]{1,0:T(4,128)(2,1)S(1)}, bf16[4,1280]{1,0:T(4,128)(2,1)S(1)}, u32[]{:S(2)}, u32[]{:S(2)}) collective-permute-start(bf16[4,1280]{1,0:T(4,128)(2,1)S(1)} %attend.1), channel_id=1, source_target_pairs={{0,16},{1,17},{2,18},{3,19},{4,20},{5,21},{6,22},{7,23},{8,24},{9,... | collective-permute-start | bytes 30728 | tf_op jit(solution)/shard_map/ppermute | solution.py:61
  25.4 1.2 %collective-permute-start.7 = (bf16[4,1280]{1,0:T(4,128)(2,1)S(1)}, bf16[4,1280]{1,0:T(4,128)(2,1)S(1)}, u32[]{:S(2)}, u32[]{:S(2)}) collective-permute-start(bf16[4,1280]{1,0:T(4,128)(2,1)S(1)} %attend.1), channel_id=1, source_target_pairs={{0,8},{1,5},{2,10},{3,7},{4,12},{5,1},{6,14},{7,3},{8,0},{9,13},{1... | collective-permute-start | bytes 30728 | tf_op jit(solution)/shard_map/ppermute | solution.py:61
  26.6 1.1 %collective-permute-done.9 = bf16[4,1280]{1,0:T(4,128)(2,1)S(1)} collective-permute-done((bf16[4,1280]{1,0:T(4,128)(2,1)S(1)}, bf16[4,1280]{1,0:T(4,128)(2,1)S(1)}, u32[]{:S(2)}, u32[]{:S(2)}) %collective-permute-start.9) | collective-permute-done | bytes 10272 | tf_op jit(solution)/shard_map/ppermute | solution.py:61
  27.7 0.9 %collective-permute-done.8 = bf16[4,1280]{1,0:T(4,128)(2,1)S(1)} collective-permute-done((bf16[4,1280]{1,0:T(4,128)(2,1)S(1)}, bf16[4,1280]{1,0:T(4,128)(2,1)S(1)}, u32[]{:S(2)}, u32[]{:S(2)}) %collective-permute-start.8) | collective-permute-done | bytes 10272 | tf_op jit(solution)/shard_map/ppermute | solution.py:61
  28.6 0.6 %collective-permute-done.7 = bf16[4,1280]{1,0:T(4,128)(2,1)S(1)} collective-permute-done((bf16[4,1280]{1,0:T(4,128)(2,1)S(1)}, bf16[4,1280]{1,0:T(4,128)(2,1)S(1)}, u32[]{:S(2)}, u32[]{:S(2)}) %collective-permute-start.7) | collective-permute-done | bytes 10272 | tf_op jit(solution)/shard_map/ppermute | solution.py:61
  29.2 1.1 %collective-permute-start.10 = (bf16[16,1280]{1,0:T(8,128)(2,1)S(1)}, bf16[16,1280]{1,0:T(8,128)(2,1)S(1)}, u32[]{:S(2)}, u32[]{:S(2)}) collective-permute-start(bf16[16,1280]{1,0:T(8,128)(2,1)S(1)} %pad_maximum_fusion), channel_id=1, source_target_pairs={{0,4},{1,9},{2,6},{3,11},{4,0},{5,13},{6,2},{7,15},{8,12},{9,1},{1... | collective-permute-start | bytes 122888 | tf_op jit(solution)/shard_map/ppermute | solution.py:61
  30.3 2.9 %collective-permute-done.10 = bf16[16,1280]{1,0:T(8,128)(2,1)S(1)} collective-permute-done((bf16[16,1280]{1,0:T(8,128)(2,1)S(1)}, bf16[16,1280]{1,0:T(8,128)(2,1)S(1)}, u32[]{:S(2)}, u32[]{:S(2)}) %collective-permute-start.10) | collective-permute-done | bytes 40992 | tf_op jit(solution)/shard_map/ppermute | solution.py:61
  33.3 0.1 concatenate.16.refs_0_
  33.3 0.0 copy-done
  33.3 0.5 %output.1 = (f32[16,640]{1,0:T(8,128)S(1)}, f32[16,640]{1,0:T(8,128)S(1)}) custom-call(bf16[32,1280]{1,0:T(8,128)(2,1)S(1)} %concatenate.16.refs_0_, bf16[1280,640]{1,0:T(8,128)(2,1)S(1)} %copy-done), custom_call_target="tpu_custom_call" | custom-call | tf_op jit(solution)/shard_map/output/pallas_call | solution.py:502
  33.8 0.1 collective-permute-start.11
  33.9 1.2 %collective-permute-done.11 = f32[16,640]{1,0:T(8,128)S(1)} collective-permute-done((f32[16,640]{1,0:T(8,128)S(1)}, f32[16,640]{1,0:T(8,128)S(1)}, u32[]{:S(2)}, u32[]{:S(2)}) %collective-permute-start.11) | collective-permute-done | bytes 40992 | tf_op jit(solution)/shard_map/ppermute | solution.py:69
  35.1 1.3 %collective-permute-start.12 = (f32[8,640]{1,0:T(8,128)S(1)}, f32[8,640]{1,0:T(8,128)S(1)}, u32[]{:S(2)}, u32[]{:S(2)}) collective-permute-start(f32[8,640]{1,0:T(8,128)S(1)} %slice.29), channel_id=1, source_target_pairs={{0,3},{1,2},{2,1},{3,0},{4,7},{5,6},{6,5},{7,4},{8,11},{9,10},{10,... | collective-permute-start | bytes 61448 | tf_op jit(solution)/shard_map/ppermute | solution.py:69
  36.4 2.0 %collective-permute-done.12 = f32[8,640]{1,0:T(8,128)S(1)} collective-permute-done((f32[8,640]{1,0:T(8,128)S(1)}, f32[8,640]{1,0:T(8,128)S(1)}, u32[]{:S(2)}, u32[]{:S(2)}) %collective-permute-start.12) | collective-permute-done | bytes 20512 | tf_op jit(solution)/shard_map/ppermute | solution.py:69
  38.4 0.6 %fusion = bf16[8,640]{1,0:T(8,128)(2,1)} fusion(f32[8,640]{1,0:T(8,128)S(1)} %collective-permute-done.12, f32[16,640]{1,0:T(8,128)S(1)} %add.17), kind=kLoop, calls=%fused_computation.2 | loop fusion | flops 10240 | bytes 51200 | tf_op jit(solution)/shard_map/convert_element_type | solution.py:514
  (9 shorter events, 0.1 us)
Async XLA Ops:
  0.0 4.8 %collective-permute-start.1 = (bf16[8,640]{1,0:T(8,128)(2,1)}, bf16[8,640]{1,0:T(8,128)(2,1)S(1)}, u32[]{:S(2)}, u32[]{:S(2)}) collective-permute-start(bf16[8,640]{1,0:T(8,128)(2,1)} %refs_3_.1), channel_id=1, source_target_pairs={{0,3},{1,2},{2,1},{3,0},{4,7},{5,6},{6,5},{7,4},{8,11},{9,10},{10,... | collective-permute-start | bytes 30728 | tf_op jit(solution)/shard_map/ppermute | solution.py:69
  2.4 2.5 %collective-permute-start = (bf16[8,640]{1,0:T(8,128)(2,1)}, bf16[8,640]{1,0:T(8,128)(2,1)S(1)}, u32[]{:S(2)}, u32[]{:S(2)}) collective-permute-start(bf16[8,640]{1,0:T(8,128)(2,1)} %refs_3_.1), channel_id=1, source_target_pairs={{0,1},{1,0},{2,3},{3,2},{4,5},{5,4},{6,7},{7,6},{8,9},{9,8},{10,11... | collective-permute-start | bytes 30728 | tf_op jit(solution)/shard_map/ppermute | solution.py:69
  4.8 1.2 %collective-permute-start.2 = (bf16[8,640]{1,0:T(8,128)(2,1)S(1)}, bf16[8,640]{1,0:T(8,128)(2,1)S(1)}, u32[]{:S(2)}, u32[]{:S(2)}) collective-permute-start(bf16[8,640]{1,0:T(8,128)(2,1)S(1)} %collective-permute-done.1.refs_3_), channel_id=1, source_target_pairs={{0,1},{1,0},{2,3},{3,2},{4,5},{5,4},{6,7},{7,6},{8,9},{9,8},{10,11... | collective-permute-start | bytes 30728 | tf_op jit(solution)/shard_map/ppermute | solution.py:69
  6.6 4.9 %collective-permute-start.3 = (f32[16,1920]{1,0:T(8,128)S(1)}, f32[16,1920]{1,0:T(8,128)S(1)}, u32[]{:S(2)}, u32[]{:S(2)}) collective-permute-start(f32[16,1920]{1,0:T(8,128)S(1)} %get-tuple-element.40), channel_id=1, source_target_pairs={{0,4},{1,9},{2,6},{3,11},{4,0},{5,13},{6,2},{7,15},{8,12},{9,1},{1... | collective-permute-start | bytes 368648 | tf_op jit(solution)/shard_map/ppermute | solution.py:61
  11.6 6.3 %collective-permute-start.6 = (f32[4,1920]{1,0:T(4,128)S(1)}, f32[4,1920]{1,0:T(4,128)S(1)}, u32[]{:S(2)}, u32[]{:S(2)}) collective-permute-start(f32[4,1920]{1,0:T(4,128)S(1)} %get-tuple-element.53), channel_id=1, source_target_pairs={{0,24},{1,21},{2,26},{3,23},{4,28},{5,17},{6,30},{7,19},{8,16},{9,... | collective-permute-start | bytes 92168 | tf_op jit(solution)/shard_map/ppermute | solution.py:61
  15.3 4.8 %collective-permute-start.5 = (f32[4,1920]{1,0:T(4,128)S(1)}, f32[4,1920]{1,0:T(4,128)S(1)}, u32[]{:S(2)}, u32[]{:S(2)}) collective-permute-start(f32[4,1920]{1,0:T(4,128)S(1)} %get-tuple-element.54), channel_id=1, source_target_pairs={{0,16},{1,17},{2,18},{3,19},{4,20},{5,21},{6,22},{7,23},{8,24},{9,... | collective-permute-start | bytes 92168 | tf_op jit(solution)/shard_map/ppermute | solution.py:61
  15.3 4.8 %collective-permute-start.4 = (f32[4,1920]{1,0:T(4,128)S(1)}, f32[4,1920]{1,0:T(4,128)S(1)}, u32[]{:S(2)}, u32[]{:S(2)}) collective-permute-start(f32[4,1920]{1,0:T(4,128)S(1)} %get-tuple-element.55), channel_id=1, source_target_pairs={{0,8},{1,5},{2,10},{3,7},{4,12},{5,1},{6,14},{7,3},{8,0},{9,13},{1... | collective-permute-start | bytes 92168 | tf_op jit(solution)/shard_map/ppermute | solution.py:61
  20.1 13.3 %copy-start = (bf16[1280,640]{1,0:T(8,128)(2,1)S(1)}, bf16[1280,640]{1,0:T(8,128)(2,1)}, u32[]{:S(2)}) copy-start(bf16[1280,640]{1,0:T(8,128)(2,1)} %refs_1_.3) | copy-start | bytes 4915204
  22.2 5.5 %collective-permute-start.9 = (bf16[4,1280]{1,0:T(4,128)(2,1)S(1)}, bf16[4,1280]{1,0:T(4,128)(2,1)S(1)}, u32[]{:S(2)}, u32[]{:S(2)}) collective-permute-start(bf16[4,1280]{1,0:T(4,128)(2,1)S(1)} %attend.1), channel_id=1, source_target_pairs={{0,24},{1,21},{2,26},{3,23},{4,28},{5,17},{6,30},{7,19},{8,16},{9,... | collective-permute-start | bytes 30728 | tf_op jit(solution)/shard_map/ppermute | solution.py:61
  24.0 4.6 %collective-permute-start.8 = (bf16[4,1280]{1,0:T(4,128)(2,1)S(1)}, bf16[4,1280]{1,0:T(4,128)(2,1)S(1)}, u32[]{:S(2)}, u32[]{:S(2)}) collective-permute-start(bf16[4,1280]{1,0:T(4,128)(2,1)S(1)} %attend.1), channel_id=1, source_target_pairs={{0,16},{1,17},{2,18},{3,19},{4,20},{5,21},{6,22},{7,23},{8,24},{9,... | collective-permute-start | bytes 30728 | tf_op jit(solution)/shard_map/ppermute | solution.py:61
  25.4 3.7 %collective-permute-start.7 = (bf16[4,1280]{1,0:T(4,128)(2,1)S(1)}, bf16[4,1280]{1,0:T(4,128)(2,1)S(1)}, u32[]{:S(2)}, u32[]{:S(2)}) collective-permute-start(bf16[4,1280]{1,0:T(4,128)(2,1)S(1)} %attend.1), channel_id=1, source_target_pairs={{0,8},{1,5},{2,10},{3,7},{4,12},{5,1},{6,14},{7,3},{8,0},{9,13},{1... | collective-permute-start | bytes 30728 | tf_op jit(solution)/shard_map/ppermute | solution.py:61
  29.2 4.1 %collective-permute-start.10 = (bf16[16,1280]{1,0:T(8,128)(2,1)S(1)}, bf16[16,1280]{1,0:T(8,128)(2,1)S(1)}, u32[]{:S(2)}, u32[]{:S(2)}) collective-permute-start(bf16[16,1280]{1,0:T(8,128)(2,1)S(1)} %pad_maximum_fusion), channel_id=1, source_target_pairs={{0,4},{1,9},{2,6},{3,11},{4,0},{5,13},{6,2},{7,15},{8,12},{9,1},{1... | collective-permute-start | bytes 122888 | tf_op jit(solution)/shard_map/ppermute | solution.py:61
  33.8 1.3 %collective-permute-start.11 = (f32[16,640]{1,0:T(8,128)S(1)}, f32[16,640]{1,0:T(8,128)S(1)}, u32[]{:S(2)}, u32[]{:S(2)}) collective-permute-start(f32[16,640]{1,0:T(8,128)S(1)} %get-tuple-element.50), channel_id=1, source_target_pairs={{0,1},{1,0},{2,3},{3,2},{4,5},{5,4},{6,7},{7,6},{8,9},{9,8},{10,11... | collective-permute-start | bytes 122888 | tf_op jit(solution)/shard_map/ppermute | solution.py:69
  35.1 3.3 %collective-permute-start.12 = (f32[8,640]{1,0:T(8,128)S(1)}, f32[8,640]{1,0:T(8,128)S(1)}, u32[]{:S(2)}, u32[]{:S(2)}) collective-permute-start(f32[8,640]{1,0:T(8,128)S(1)} %slice.29), channel_id=1, source_target_pairs={{0,3},{1,2},{2,1},{3,0},{4,7},{5,6},{6,5},{7,4},{8,11},{9,10},{10,... | collective-permute-start | bytes 61448 | tf_op jit(solution)/shard_map/ppermute | solution.py:69

commit v4 on v3

--- a/solution.py
+++ b/solution.py
@@ -15,8 +15,6 @@
 TOGETHER = 8
 LANES = 128
 FAR = 1 << 20
-STAGE_BITS = 2
-
 EXTRA_ROWS = 16
 
 
@@ -26,14 +24,14 @@
     return bits
 
 
-def stages(n, most):
+def stages(n):
     bits = log2(n)
     if bits == 0:
         return []
     result = [(2, 1)]
     left = bits - 1
     while left:
-        take = most if left % most == 0 else 1
+        take = 2 if left % 2 == 0 else 1
         left -= take
         result.append((1 << take, 2 << left))
     return result
@@ -45,11 +43,12 @@
     return offset ^ ((low ^ turned) * (kv & 1))
 
 
-def place_to_offset(place, n):
-    bits = log2(n)
-    if bits == 0:
-        return place
-    return ((place << 1) | (place >> (bits - 1))) & (n - 1)
+def place_to_offset(place, n, gathered):
+    offset = place * 0
+    for radix, unit in stages(n) if gathered else reversed(stages(n)):
+        offset = offset + (place & (radix - 1)) * unit
+        place = place >> log2(radix)
+    return offset
 
 
 def swap_req(x, n_req, n_kv, offset):
@@ -61,10 +60,6 @@
     return lax.ppermute(x, ("req", "kv"), pairs)
 
 
-def kept(n_kv):
-    return [0] + list(range(3, n_kv, 2))
-
-
 def swap_kv(x, n_kv, offset):
     return lax.ppermute(x, "kv", [(j, j ^ offset) for j in range(n_kv)])
 
@@ -75,7 +70,7 @@
     shape = (size, size)
     req_row = lax.broadcasted_iota(jnp.int32, shape, 1 if to_kv else 0)
     kv_row = lax.broadcasted_iota(jnp.int32, shape, 0 if to_kv else 1)
-    offset = place_to_offset(req_row >> log2(rows_req), n_req)
+    offset = place_to_offset(req_row >> log2(rows_req), n_req, to_kv)
     if n_req > 2:
         offset = crossed(offset, kv)
     request = ((offset ^ req) << log2(rows_req)) | (req_row & (rows_req - 1))
@@ -86,9 +81,7 @@
 def load_weights_kernel(*refs):
     n = len(refs) // 2
     sem = refs[-1]
-    copies = [
-        pltpu.make_async_copy(refs[i], refs[n + i], sem.at[i]) for i in range(n)
-    ]
+    copies = [pltpu.make_async_copy(refs[i], refs[n + i], sem.at[i]) for i in range(n)]
     for copy in copies:
         copy.start()
     for copy in copies:
@@ -146,22 +139,32 @@
     return list(zip(fields[::2], fields[1::2]))
 
 
-def load_cache_kernel(plan, cache, buf, sem):
-    count, blocks = cache.shape[0], cache.shape[2] // BLOCK
+def load_cache_kernel(plan, cache, out, buf, sem):
+    count, heads_kv, cycle, size = cache.shape
     planned = visits_of(plan, count)
+    target = out if buf is None else buf
 
     def each(act):
         for r, (first, visits) in enumerate(planned):
 
             @pl.loop(0, visits)
             def _(t):
-                at = (first + t) & (blocks - 1)
+                at = (first + t) & (cycle // BLOCK - 1)
                 src = pl.ds(pl.multiple_of(at * BLOCK, BLOCK), BLOCK)
                 dst = pl.ds(pl.multiple_of(t * BLOCK, BLOCK), BLOCK)
-                act(pltpu.make_async_copy(cache.at[r, :, src], buf.at[r, :, dst], sem.at[r, t]))
-
-    each(lambda copy: copy.start())
-    each(lambda copy: copy.wait())
+                copy = pltpu.make_async_copy(
+                    cache.at[r, :, src], target.at[r, :, dst], sem.at[r, t]
+                )
+                act(copy, r, dst)
+
+    def finish(copy, r, slots):
+        copy.wait()
+        if buf is not None:
+            for h in range(heads_kv):
+                out[r, h * size : (h + 1) * size, slots] = buf[r, h, slots].T
+
+    each(lambda copy, r, slots: copy.start())
+    each(finish)
 
 
 def attend_kernel(n_parts, plan, *refs):
@@ -187,7 +190,7 @@
         denoms,
         numers,
     ) = refs[n_parts:]
-    count, heads_kv, _, size = k_buf.shape
+    count, heads_kv, _, size = v_buf.shape
     q_cols, kv_cols = context.shape[1], heads_kv * size
     group = q_cols // kv_cols
     pad = q_heads.shape[1] // heads_kv
@@ -245,8 +248,10 @@
 
     def score(r, t, place, at):
         s = (
-            lax.dot_general(
-                q_rows[r], both(k_buf, r, t), contract_last, preferred_element_type=jnp.float32
+            jnp.dot(
+                q_rows[r],
+                k_buf[r, :, pl.ds(pl.multiple_of(t * BLOCK, BLOCK), BLOCK)],
+                preferred_element_type=jnp.float32,
             )
             * scale
         )
@@ -279,7 +284,10 @@
             start = jnp.where(past, starts[i], start)
         return r, inside - start + 1
 
-    rounds = (left + TOGETHER - 1) // TOGETHER
+    tail = TOGETHER // 2
+    spare = left & (TOGETHER - 1)
+    rounds = (left >> log2(TOGETHER)) + jnp.where(spare > tail, 1, 0)
+    tails = jnp.where((spare > 0) & (spare <= tail), 1, 0)
     extras = []
     for r in range(count):
         extra = (
@@ -295,14 +303,26 @@
         extras.append(jnp.where(live, extra, -jnp.inf))
         tops[r] = score(r, 0, r, 0)
 
-    @pl.loop(0, rounds)
-    def _(k):
-        for i in range(TOGETHER):
-            place = k * TOGETHER + i
+    def score_some(start, number):
+        for i in range(number):
+            place = start + i
             r, t = block_of(place)
             at = jnp.where(place < left, t * BLOCK, FAR)
             tops[r] = jnp.maximum(tops[r], score(r, t, count + place, at))
 
+    def mix_some(start, number):
+        for i in range(number):
+            place = start + i
+            r, t = block_of(place)
+            denom, product = mix(r, t, count + place)
+            denoms[r] += denom
+            numers[r] += product
+
+    def all_others(some):
+        pl.loop(0, rounds)(lambda k: some(k * TOGETHER, TOGETHER))
+        pl.loop(0, tails)(lambda k: some(rounds * TOGETHER, tail))
+
+    all_others(score_some)
     for r in range(count):
         top = jnp.maximum(
             jnp.max(tops[r], 1, keepdims=True), jnp.max(extras[r], 1, keepdims=True)
@@ -317,14 +337,7 @@
         denoms[r], product = mix(r, 0, r)
         numers[r] = numer + product
 
-    @pl.loop(0, rounds)
-    def _(k):
-        for i in range(TOGETHER):
-            place = k * TOGETHER + i
-            r, t = block_of(place)
-            denom, product = mix(r, t, count + place)
-            denoms[r] += denom
-            numers[r] += product
+    all_others(mix_some)
 
     for r in range(count):
         denom = jnp.sum(denoms[r], 1, keepdims=True) + jnp.sum(extras[r], 1, keepdims=True)
@@ -338,16 +351,14 @@
     context[...] = result_buf[...].astype(context.dtype)
 
 
-def output_kernel(rows_kv, context, w_output, keep, send):
-    size = context.shape[0]
+def output_kernel(context, w_output, *outs):
+    size, rows_kv = context.shape[0], outs[0].shape[0]
     rows_req = size // lax.axis_size("req")
     order = row_order(size, rows_req, rows_kv, True)
     rows = jnp.dot(order, context[...], preferred_element_type=jnp.float32).astype(jnp.bfloat16)
     product = jnp.dot(rows, w_output[...], preferred_element_type=jnp.float32)
-    for i, u in enumerate(kept(size // rows_kv)):
-        place = slice(i * rows_kv, (i + 1) * rows_kv)
-        keep[place] = product[u * rows_kv : (u + 1) * rows_kv]
-        send[place] = product[(u ^ 1) * rows_kv : ((u ^ 1) + 1) * rows_kv]
+    for i, out in enumerate(outs):
+        out[...] = product[i * rows_kv : (i + 1) * rows_kv]
 
 
 def spec(space=pltpu.VMEM):
@@ -355,7 +366,7 @@
 
 
 def attend_call(plan, parts, cosine, sine, b_query, b_key, b_value, k_live, v_live, *sinks):
-    count, heads_kv, stored, size = k_live.shape
+    count, heads_kv, stored, size = v_live.shape
     group = b_query.shape[0] // heads_kv
     rows, kv_cols = heads_kv * (-(-group // 8) * 8), heads_kv * size
     q_cols = b_query.shape[0] * size
@@ -455,23 +466,29 @@
 
     visits = cycle // BLOCK + 1
 
-    def load(cache, plan, name):
+    def load(cache, plan, turn, name):
+        loaded = (count, heads_kv, visits * BLOCK, size)
+        turned = (count, heads_kv * size, visits * BLOCK)
+        sem = pltpu.SemaphoreType.DMA((count, visits))
+        kernel = load_cache_kernel
+        if not turn:
+            kernel = lambda plan, cache, out, sem: load_cache_kernel(plan, cache, out, None, sem)
         return pl.pallas_call(
-            load_cache_kernel,
-            out_shape=jax.ShapeDtypeStruct((count, heads_kv, visits * BLOCK, size), bf16),
+            kernel,
+            out_shape=jax.ShapeDtypeStruct(turned if turn else loaded, bf16),
             in_specs=[spec(), spec(pltpu.HBM)],
             out_specs=spec(),
-            scratch_shapes=[pltpu.SemaphoreType.DMA((count, visits))],
-            compiler_params=pltpu.CompilerParams(vmem_limit_bytes=1 << 20),
+            scratch_shapes=([pltpu.VMEM(loaded, bf16)] if turn else []) + [sem],
+            compiler_params=pltpu.CompilerParams(vmem_limit_bytes=(12 if turn else 1) << 20),
             cost_estimate=pl.CostEstimate(flops=0, transcendentals=0, bytes_accessed=6 << 20),
             name=name,
         )(plan, in_hbm(cache))
 
-    req_stages = stages(n_req, STAGE_BITS)
+    req_stages = stages(n_req)
     plan = plan_of(lengths, sink_count, window)
     keep, plan = lax.optimization_barrier((keep, plan))
     received = swap_req(send, n_req, n_kv, req_stages[0][1])
-    k_live = load(key_cache, plan, "load_keys")
+    k_live = load(key_cache, plan, True, "load_keys")
     keep, k_live = lax.optimization_barrier((keep, k_live))
     parts = [keep, received]
     for radix, unit in req_stages[1:]:
@@ -482,7 +499,7 @@
             for q in range(1, radix)
         ]
     parts[0], plan = lax.optimization_barrier((parts[0], plan))
-    v_live = load(value_cache, plan, "load_values")
+    v_live = load(value_cache, plan, False, "load_values")
 
     freq = jnp.power(1000000.0, -2.0 * jnp.arange(size // 2, dtype=f32) / size)
     angle = lengths.astype(f32)[:, None] * freq
@@ -495,22 +512,21 @@
     )
 
     everyone = context
-    for radix, unit in reversed(stages(n_req, STAGE_BITS)):
+    for radix, unit in stages(n_req):
         blocks = [swap_req(everyone, n_req, n_kv, q * unit) for q in range(1, radix)]
         everyone = jnp.concatenate([everyone] + blocks, 0)
-    half = jax.ShapeDtypeStruct((rows // 2, w_output.shape[1]), f32)
-    keep, send = pl.pallas_call(
-        lambda *refs: output_kernel(rows_kv, *refs),
-        out_shape=(half, half),
+    piece = jax.ShapeDtypeStruct((rows_kv, w_output.shape[1]), f32)
+    products = pl.pallas_call(
+        output_kernel,
+        out_shape=(piece,) * n_kv,
         in_specs=[spec()] * 2,
-        out_specs=(spec(), spec()),
+        out_specs=(spec(),) * n_kv,
         compiler_params=pltpu.CompilerParams(vmem_limit_bytes=16 << 20),
         name="output",
     )(everyone, w_output)
-    both = keep + swap_kv(send, n_kv, 1)
-    result = both[:rows_kv]
-    for i, u in enumerate(kept(n_kv)[1:], 1):
-        result = result + swap_kv(both[i * rows_kv : (i + 1) * rows_kv], n_kv, u)
+    result = products[0]
+    for u in range(n_kv - 1, 0, -1):
+        result = result + swap_kv(products[u], n_kv, u)
     return result.astype(bf16)
 
 

time: 39.3 us -> 37.6 us (0.957); the launches traced: 39 us -> 38 us
  waiting for transfers between devices: 13.3 us -> 9.1 us
  Pallas kernels: 8.45 us -> 10.4 us
  starting transfers between devices: 16.1 us -> 17.4 us
    ppermute x8, waiting for transfers between devices: 8.93 us -> 5.95 us  [swap_req(): return lax.ppermute(x, ('req', 'kv'), pairs)]
    pallas_call x3, Pallas kernels: 4.11 us -> 5.93 us  [the longest x2 5.43 us: load(): pl.pallas_call(kernel, out_shape=jax.ShapeDtypeStruct(turned if turn else...]
    ppermute x5 -> x6, waiting for transfers between devices: 4.32 us -> 3.14 us  [swap_kv(): return lax.ppermute(x, 'kv', [(j, j ^ offset) for j in range(n_kv)])]
    ppermute x8, starting transfers between devices: 11.6 us -> 12.3 us  [swap_req(): return lax.ppermute(x, ('req', 'kv'), pairs)]
    ppermute x5 -> x6, starting transfers between devices: 4.52 us -> 5.07 us  [swap_kv(): return lax.ppermute(x, 'kv', [(j, j ^ offset) for j in range(n_kv)])]
  transfers between devices with their start and end apart: 13 -> 14, of which waited for: 9 -> 8; matrix products, arithmetic and copies ran while one was open for 1% -> 1% of each run, Pallas kernels for 14% -> 19%
where the time goes in v4:
time: 37.6 us; the launch traced here: 38 us
  starting transfers between devices  17.4 us (46%)
  Pallas kernels  10.4 us (28%)
  waiting for transfers between devices  9.1 us (24%)
  other arithmetic  0.88 us (2%)
    ppermute x8, starting transfers between devices, swap_req(): return lax.ppermute(x, ('req', 'kv'), pairs)  12.3 us
    ppermute x8, waiting for transfers between devices, swap_req(): return lax.ppermute(x, ('req', 'kv'), pairs)  5.95 us
    pallas_call x2, Pallas kernels, load(): pl.pallas_call(kernel, out_shape=jax.ShapeDtypeStruct(turned if turn else...  5.43 us
    ppermute x6, starting transfers between devices, swap_kv(): return lax.ppermute(x, 'kv', [(j, j ^ offset) for j in range(n_kv)])  5.07 us
    ppermute x6, waiting for transfers between devices, swap_kv(): return lax.ppermute(x, 'kv', [(j, j ^ offset) for j in range(n_kv)])  3.14 us
    pallas_call x1, Pallas kernels, attend_call(): pl.pallas_call(lambda *refs: attend_kernel(len(parts), *refs), out_shape=...  2.22 us
    pallas_call x1, Pallas kernels, on_device(): pl.pallas_call(load_weights_kernel, out_shape=tuple((jax.ShapeDtypeStruct...  1.69 us
  transfers between devices with their start and end apart: 14, of which 8 were waited for; matrix products, arithmetic and copies ran while one was open for 1% of the time, Pallas kernels for 19%

profile of v4, /device:TPU:0, one launch (start us, length us, event | category | flops | bytes accessed | tf_op | source)
XLA Modules:
  0.0 38.0 jit_solution(6935188260080207391)
XLA Ops:
  0.0 2.4 %collective-permute-start.1 = (bf16[8,640]{1,0:T(8,128)(2,1)}, bf16[8,640]{1,0:T(8,128)(2,1)S(1)}, u32[]{:S(2)}, u32[]{:S(2)}) collective-permute-start(bf16[8,640]{1,0:T(8,128)(2,1)} %refs_3_.1), channel_id=1, source_target_pairs={{0,3},{1,2},{2,1},{3,0},{4,7},{5,6},{6,5},{7,4},{8,11},{9,10},{10,... | collective-permute-start | bytes 30728 | tf_op jit(solution)/shard_map/ppermute | solution.py:64
  2.4 0.7 %collective-permute-start = (bf16[8,640]{1,0:T(8,128)(2,1)}, bf16[8,640]{1,0:T(8,128)(2,1)S(1)}, u32[]{:S(2)}, u32[]{:S(2)}) collective-permute-start(bf16[8,640]{1,0:T(8,128)(2,1)} %refs_3_.1), channel_id=1, source_target_pairs={{0,1},{1,0},{2,3},{3,2},{4,5},{5,4},{6,7},{7,6},{8,9},{9,8},{10,11... | collective-permute-start | bytes 30728 | tf_op jit(solution)/shard_map/ppermute | solution.py:64
  3.1 1.7 %load_weights.1 = (bf16[640,1280]{1,0:T(8,128)(2,1)S(1)}, bf16[640,256]{1,0:T(8,128)(2,1)S(1)}, bf16[640,256]{1,0:T(8,128)(2,1)S(1)}, bf16[8,640]{1,0:T(8,128)(2...) custom-call(bf16[640,1280]{1,0:T(8,128)(2,1)} %refs_0_.1, ...), custom_call_target="tpu_custom_call" | custom-call | bytes 6291456 | tf_op jit(solution)/shard_map/load_weights/pallas_call | solution.py:442
  4.8 0.0 collective-permute-done.1.refs_3_
  4.8 0.1 collective-permute-start.2
  4.9 0.0 collective-permute-done.refs_1_
  4.9 1.1 %collective-permute-done.2.refs_2_ = bf16[8,640]{1,0:T(8,128)(2,1)S(1)} collective-permute-done((bf16[8,640]{1,0:T(8,128)(2,1)S(1)}, bf16[8,640]{1,0:T(8,128)(2,1)S(1)}, u32[]{:S(2)}, u32[]{:S(2)}) %collective-permute-start.2) | collective-permute-done | bytes 10272 | tf_op jit(solution)/shard_map/ppermute | solution.py:64
  6.1 0.5 %project.1 = (f32[16,1920]{1,0:T(8,128)S(1)}, f32[16,1920]{1,0:T(8,128)S(1)}) custom-call(bf16[8,640]{1,0:T(8,128)(2,1)S(1)} %get-tuple-element.30.refs_0_, bf16[8,640]{1,0:T(8,128)(2,1)S(1)} %collective-permute-done.refs_1_, bf16[8,640]{1,0:T(8,128)(2,1)S(1)} %collective-permute-done.2.refs_2_, bf16[8,640]{1,0:T(8,128)(2,1)S(1)} %collective-permute-done.1.refs_3_, ...), custom_call_target="tpu_custom_call" | custom-call | tf_op jit(solution)/shard_map/project/pallas_call | solution.py:458
  6.6 1.6 %collective-permute-start.3 = (f32[16,1920]{1,0:T(8,128)S(1)}, f32[16,1920]{1,0:T(8,128)S(1)}, u32[]{:S(2)}, u32[]{:S(2)}) collective-permute-start(f32[16,1920]{1,0:T(8,128)S(1)} %get-tuple-element.42), channel_id=1, source_target_pairs={{0,4},{1,9},{2,6},{3,11},{4,0},{5,13},{6,2},{7,15},{8,12},{9,1},{1... | collective-permute-start | bytes 368648 | tf_op jit(solution)/shard_map/ppermute | solution.py:60
  8.2 0.1 fusion
  8.3 0.1 broadcast_in_dim.2.plan.refs_0_
  8.4 3.1 %load_keys.1.refs_10_ = bf16[4,256,4608]{2,1,0:T(8,128)(2,1)S(1)} custom-call(s32[4,4,128]{2,1,0:T(4,128)S(1)} %broadcast_in_dim.2.plan.refs_0_, bf16[4,2,4096,128]{3,2,1,0:T(8,128)(2,1)} %cache.2), custom_call_target="tpu_custom_call" | custom-call | bytes 6291456 | tf_op jit(solution)/shard_map/load_keys/pallas_call | solution.py:476
  11.4 0.1 collective-permute-done.3
  11.6 3.7 %collective-permute-start.6 = (f32[4,1920]{1,0:T(4,128)S(1)}, f32[4,1920]{1,0:T(4,128)S(1)}, u32[]{:S(2)}, u32[]{:S(2)}) collective-permute-start(f32[4,1920]{1,0:T(4,128)S(1)} %get-tuple-element.57), channel_id=1, source_target_pairs={{0,24},{1,21},{2,26},{3,23},{4,28},{5,17},{6,30},{7,19},{8,16},{9,... | collective-permute-start | bytes 92168 | tf_op jit(solution)/shard_map/ppermute | solution.py:60
  15.3 0.0 collective-permute-start.5
  15.3 0.8 %collective-permute-start.4 = (f32[4,1920]{1,0:T(4,128)S(1)}, f32[4,1920]{1,0:T(4,128)S(1)}, u32[]{:S(2)}, u32[]{:S(2)}) collective-permute-start(f32[4,1920]{1,0:T(4,128)S(1)} %get-tuple-element.59), channel_id=1, source_target_pairs={{0,8},{1,5},{2,10},{3,7},{4,12},{5,1},{6,14},{7,3},{8,0},{9,13},{1... | collective-permute-start | bytes 92168 | tf_op jit(solution)/shard_map/ppermute | solution.py:60
  16.1 0.1 pad_maximum_fusion.1
  16.1 2.4 %load_values.1.refs_11_ = bf16[4,2,4608,128]{3,2,1,0:T(8,128)(2,1)S(1)} custom-call(s32[4,4,128]{2,1,0:T(4,128)S(1)} %broadcast_in_dim.2.plan.refs_0_, bf16[4,2,4096,128]{3,2,1,0:T(8,128)(2,1)} %cache.3), custom_call_target="tpu_custom_call" | custom-call | bytes 6291456 | tf_op jit(solution)/shard_map/load_values/pallas_call | solution.py:476
  18.5 0.0 collective-permute-done.6.refs_4_
  18.5 1.5 %collective-permute-done.5.refs_3_ = f32[4,1920]{1,0:T(4,128)S(1)} collective-permute-done((f32[4,1920]{1,0:T(4,128)S(1)}, f32[4,1920]{1,0:T(4,128)S(1)}, u32[]{:S(2)}, u32[]{:S(2)}) %collective-permute-start.5) | collective-permute-done | bytes 30752 | tf_op jit(solution)/shard_map/ppermute | solution.py:60
  20.1 0.0 collective-permute-done.4.refs_2_
  20.1 0.0 copy-start
  20.1 2.2 %attend.1 = bf16[4,1280]{1,0:T(4,128)(2,1)S(1)} custom-call(s32[4,4,128]{2,1,0:T(4,128)S(1)} %broadcast_in_dim.2.plan.refs_0_, f32[4,1920]{1,0:T(4,128)S(1)} %get-tuple-element.44.refs_1_, f32[4,1920]{1,0:T(4,128)S(1)} %collective-permute-done.4.refs_2_, f32[4,1920]{1,0:T(4,128)S(1)} %collective-permute-done.5.refs_3_, ...), custom_call_target="tpu_custom_call" | custom-call | tf_op jit(solution)/shard_map/attend/pallas_call | solution.py:374
  22.3 1.8 %collective-permute-start.7 = (bf16[4,1280]{1,0:T(4,128)(2,1)S(1)}, bf16[4,1280]{1,0:T(4,128)(2,1)S(1)}, u32[]{:S(2)}, u32[]{:S(2)}) collective-permute-start(bf16[4,1280]{1,0:T(4,128)(2,1)S(1)} %attend.1), channel_id=1, source_target_pairs={{0,4},{1,9},{2,6},{3,11},{4,0},{5,13},{6,2},{7,15},{8,12},{9,1},{1... | collective-permute-start | bytes 30728 | tf_op jit(solution)/shard_map/ppermute | solution.py:60
  24.1 1.9 %collective-permute-done.7 = bf16[4,1280]{1,0:T(4,128)(2,1)S(1)} collective-permute-done((bf16[4,1280]{1,0:T(4,128)(2,1)S(1)}, bf16[4,1280]{1,0:T(4,128)(2,1)S(1)}, u32[]{:S(2)}, u32[]{:S(2)}) %collective-permute-start.7) | collective-permute-done | bytes 10272 | tf_op jit(solution)/shard_map/ppermute | solution.py:60
  26.1 2.2 %collective-permute-start.10 = (bf16[8,1280]{1,0:T(8,128)(2,1)S(1)}, bf16[8,1280]{1,0:T(8,128)(2,1)S(1)}, u32[]{:S(2)}, u32[]{:S(2)}) collective-permute-start(bf16[8,1280]{1,0:T(8,128)(2,1)S(1)} %pad_maximum_fusion), channel_id=1, source_target_pairs={{0,24},{1,21},{2,26},{3,23},{4,28},{5,17},{6,30},{7,19},{8,16},{9,... | collective-permute-start | bytes 61448 | tf_op jit(solution)/shard_map/ppermute | solution.py:60
  28.2 0.0 collective-permute-start.9
  28.2 2.3 %collective-permute-start.8 = (bf16[8,1280]{1,0:T(8,128)(2,1)S(1)}, bf16[8,1280]{1,0:T(8,128)(2,1)S(1)}, u32[]{:S(2)}, u32[]{:S(2)}) collective-permute-start(bf16[8,1280]{1,0:T(8,128)(2,1)S(1)} %pad_maximum_fusion), channel_id=1, source_target_pairs={{0,8},{1,5},{2,10},{3,7},{4,12},{5,1},{6,14},{7,3},{8,0},{9,13},{1... | collective-permute-start | bytes 61448 | tf_op jit(solution)/shard_map/ppermute | solution.py:60
  30.5 1.2 %collective-permute-done.10 = bf16[8,1280]{1,0:T(8,128)(2,1)S(1)} collective-permute-done((bf16[8,1280]{1,0:T(8,128)(2,1)S(1)}, bf16[8,1280]{1,0:T(8,128)(2,1)S(1)}, u32[]{:S(2)}, u32[]{:S(2)}) %collective-permute-start.10) | collective-permute-done | bytes 20512 | tf_op jit(solution)/shard_map/ppermute | solution.py:60
  31.7 1.2 %collective-permute-done.9 = bf16[8,1280]{1,0:T(8,128)(2,1)S(1)} collective-permute-done((bf16[8,1280]{1,0:T(8,128)(2,1)S(1)}, bf16[8,1280]{1,0:T(8,128)(2,1)S(1)}, u32[]{:S(2)}, u32[]{:S(2)}) %collective-permute-start.9) | collective-permute-done | bytes 20512 | tf_op jit(solution)/shard_map/ppermute | solution.py:60
  32.9 0.0 collective-permute-done.8
  32.9 0.0 copy-done
  32.9 0.5 %output.1 = (f32[8,640]{1,0:T(8,128)S(1)}, f32[8,640]{1,0:T(8,128)S(1)}, f32[8,640]{1,0:T(8,128)S(1)}, f32[8,640]{1,0:T(8,128)S(1)}) custom-call(bf16[32,1280]{1,0:T(8,128)(2,1)S(1)} %concatenate.16.context, bf16[1280,640]{1,0:T(8,128)(2,1)S(1)} %copy-done), custom_call_target="tpu_custom_call" | custom-call | tf_op jit(solution)/shard_map/output/pallas_call | solution.py:519
  33.4 0.1 collective-permute-start.11
  33.5 1.5 %collective-permute-start.12 = (f32[8,640]{1,0:T(8,128)S(1)}, f32[8,640]{1,0:T(8,128)S(1)}, u32[]{:S(2)}, u32[]{:S(2)}) collective-permute-start(f32[8,640]{1,0:T(8,128)S(1)} %get-tuple-element.53), channel_id=1, source_target_pairs={{0,2},{1,3},{2,0},{3,1},{4,6},{5,7},{6,4},{7,5},{8,10},{9,11},{10,... | collective-permute-start | bytes 61448 | tf_op jit(solution)/shard_map/ppermute | solution.py:64
  35.1 0.3 collective-permute-start.13
  35.4 1.5 %collective-permute-done.11 = f32[8,640]{1,0:T(8,128)S(1)} collective-permute-done((f32[8,640]{1,0:T(8,128)S(1)}, f32[8,640]{1,0:T(8,128)S(1)}, u32[]{:S(2)}, u32[]{:S(2)}) %collective-permute-start.11) | collective-permute-done | bytes 20512 | tf_op jit(solution)/shard_map/ppermute | solution.py:64
  36.9 0.5 %collective-permute-done.12 = f32[8,640]{1,0:T(8,128)S(1)} collective-permute-done((f32[8,640]{1,0:T(8,128)S(1)}, f32[8,640]{1,0:T(8,128)S(1)}, u32[]{:S(2)}, u32[]{:S(2)}) %collective-permute-start.12) | collective-permute-done | bytes 20512 | tf_op jit(solution)/shard_map/ppermute | solution.py:64
  37.4 0.0 collective-permute-done.13
  37.4 0.6 %add_convert_fusion = bf16[8,640]{1,0:T(8,128)(2,1)} fusion(f32[8,640]{1,0:T(8,128)S(1)} %collective-permute-done.13, f32[8,640]{1,0:T(8,128)S(1)} %collective-permute-done.12, f32[8,640]{1,0:T(8,128)S(1)} %get-tuple-element.51, f32[8,640]{1,0:T(8,128)S(1)} %collective-permute-done.11), kind=kLoop, calls=%fused_computation.1 | loop fusion | flops 20480 | bytes 92160 | tf_op jit(solution)/shard_map/convert_element_type | solution.py:530
  (8 shorter events, 0.1 us)
Async XLA Ops:
  0.0 4.8 %collective-permute-start.1 = (bf16[8,640]{1,0:T(8,128)(2,1)}, bf16[8,640]{1,0:T(8,128)(2,1)S(1)}, u32[]{:S(2)}, u32[]{:S(2)}) collective-permute-start(bf16[8,640]{1,0:T(8,128)(2,1)} %refs_3_.1), channel_id=1, source_target_pairs={{0,3},{1,2},{2,1},{3,0},{4,7},{5,6},{6,5},{7,4},{8,11},{9,10},{10,... | collective-permute-start | bytes 30728 | tf_op jit(solution)/shard_map/ppermute | solution.py:64
  2.4 2.5 %collective-permute-start = (bf16[8,640]{1,0:T(8,128)(2,1)}, bf16[8,640]{1,0:T(8,128)(2,1)S(1)}, u32[]{:S(2)}, u32[]{:S(2)}) collective-permute-start(bf16[8,640]{1,0:T(8,128)(2,1)} %refs_3_.1), channel_id=1, source_target_pairs={{0,1},{1,0},{2,3},{3,2},{4,5},{5,4},{6,7},{7,6},{8,9},{9,8},{10,11... | collective-permute-start | bytes 30728 | tf_op jit(solution)/shard_map/ppermute | solution.py:64
  4.8 1.2 %collective-permute-start.2 = (bf16[8,640]{1,0:T(8,128)(2,1)S(1)}, bf16[8,640]{1,0:T(8,128)(2,1)S(1)}, u32[]{:S(2)}, u32[]{:S(2)}) collective-permute-start(bf16[8,640]{1,0:T(8,128)(2,1)S(1)} %collective-permute-done.1.refs_3_), channel_id=1, source_target_pairs={{0,1},{1,0},{2,3},{3,2},{4,5},{5,4},{6,7},{7,6},{8,9},{9,8},{10,11... | collective-permute-start | bytes 30728 | tf_op jit(solution)/shard_map/ppermute | solution.py:64
  6.6 4.9 %collective-permute-start.3 = (f32[16,1920]{1,0:T(8,128)S(1)}, f32[16,1920]{1,0:T(8,128)S(1)}, u32[]{:S(2)}, u32[]{:S(2)}) collective-permute-start(f32[16,1920]{1,0:T(8,128)S(1)} %get-tuple-element.42), channel_id=1, source_target_pairs={{0,4},{1,9},{2,6},{3,11},{4,0},{5,13},{6,2},{7,15},{8,12},{9,1},{1... | collective-permute-start | bytes 368648 | tf_op jit(solution)/shard_map/ppermute | solution.py:60
  11.6 6.9 %collective-permute-start.6 = (f32[4,1920]{1,0:T(4,128)S(1)}, f32[4,1920]{1,0:T(4,128)S(1)}, u32[]{:S(2)}, u32[]{:S(2)}) collective-permute-start(f32[4,1920]{1,0:T(4,128)S(1)} %get-tuple-element.57), channel_id=1, source_target_pairs={{0,24},{1,21},{2,26},{3,23},{4,28},{5,17},{6,30},{7,19},{8,16},{9,... | collective-permute-start | bytes 92168 | tf_op jit(solution)/shard_map/ppermute | solution.py:60
  15.3 4.8 %collective-permute-start.5 = (f32[4,1920]{1,0:T(4,128)S(1)}, f32[4,1920]{1,0:T(4,128)S(1)}, u32[]{:S(2)}, u32[]{:S(2)}) collective-permute-start(f32[4,1920]{1,0:T(4,128)S(1)} %get-tuple-element.58), channel_id=1, source_target_pairs={{0,16},{1,17},{2,18},{3,19},{4,20},{5,21},{6,22},{7,23},{8,24},{9,... | collective-permute-start | bytes 92168 | tf_op jit(solution)/shard_map/ppermute | solution.py:60
  15.3 4.8 %collective-permute-start.4 = (f32[4,1920]{1,0:T(4,128)S(1)}, f32[4,1920]{1,0:T(4,128)S(1)}, u32[]{:S(2)}, u32[]{:S(2)}) collective-permute-start(f32[4,1920]{1,0:T(4,128)S(1)} %get-tuple-element.59), channel_id=1, source_target_pairs={{0,8},{1,5},{2,10},{3,7},{4,12},{5,1},{6,14},{7,3},{8,0},{9,13},{1... | collective-permute-start | bytes 92168 | tf_op jit(solution)/shard_map/ppermute | solution.py:60
  20.1 12.9 %copy-start = (bf16[1280,640]{1,0:T(8,128)(2,1)S(1)}, bf16[1280,640]{1,0:T(8,128)(2,1)}, u32[]{:S(2)}) copy-start(bf16[1280,640]{1,0:T(8,128)(2,1)} %w_output.1) | copy-start | bytes 4915204
  22.3 3.7 %collective-permute-start.7 = (bf16[4,1280]{1,0:T(4,128)(2,1)S(1)}, bf16[4,1280]{1,0:T(4,128)(2,1)S(1)}, u32[]{:S(2)}, u32[]{:S(2)}) collective-permute-start(bf16[4,1280]{1,0:T(4,128)(2,1)S(1)} %attend.1), channel_id=1, source_target_pairs={{0,4},{1,9},{2,6},{3,11},{4,0},{5,13},{6,2},{7,15},{8,12},{9,1},{1... | collective-permute-start | bytes 30728 | tf_op jit(solution)/shard_map/ppermute | solution.py:60
  26.1 5.6 %collective-permute-start.10 = (bf16[8,1280]{1,0:T(8,128)(2,1)S(1)}, bf16[8,1280]{1,0:T(8,128)(2,1)S(1)}, u32[]{:S(2)}, u32[]{:S(2)}) collective-permute-start(bf16[8,1280]{1,0:T(8,128)(2,1)S(1)} %pad_maximum_fusion), channel_id=1, source_target_pairs={{0,24},{1,21},{2,26},{3,23},{4,28},{5,17},{6,30},{7,19},{8,16},{9,... | collective-permute-start | bytes 61448 | tf_op jit(solution)/shard_map/ppermute | solution.py:60
  28.2 4.7 %collective-permute-start.9 = (bf16[8,1280]{1,0:T(8,128)(2,1)S(1)}, bf16[8,1280]{1,0:T(8,128)(2,1)S(1)}, u32[]{:S(2)}, u32[]{:S(2)}) collective-permute-start(bf16[8,1280]{1,0:T(8,128)(2,1)S(1)} %pad_maximum_fusion), channel_id=1, source_target_pairs={{0,16},{1,17},{2,18},{3,19},{4,20},{5,21},{6,22},{7,23},{8,24},{9,... | collective-permute-start | bytes 61448 | tf_op jit(solution)/shard_map/ppermute | solution.py:60
  28.2 4.7 %collective-permute-start.8 = (bf16[8,1280]{1,0:T(8,128)(2,1)S(1)}, bf16[8,1280]{1,0:T(8,128)(2,1)S(1)}, u32[]{:S(2)}, u32[]{:S(2)}) collective-permute-start(bf16[8,1280]{1,0:T(8,128)(2,1)S(1)} %pad_maximum_fusion), channel_id=1, source_target_pairs={{0,8},{1,5},{2,10},{3,7},{4,12},{5,1},{6,14},{7,3},{8,0},{9,13},{1... | collective-permute-start | bytes 61448 | tf_op jit(solution)/shard_map/ppermute | solution.py:60
  33.4 3.5 %collective-permute-start.11 = (f32[8,640]{1,0:T(8,128)S(1)}, f32[8,640]{1,0:T(8,128)S(1)}, u32[]{:S(2)}, u32[]{:S(2)}) collective-permute-start(f32[8,640]{1,0:T(8,128)S(1)} %get-tuple-element.52), channel_id=1, source_target_pairs={{0,3},{1,2},{2,1},{3,0},{4,7},{5,6},{6,5},{7,4},{8,11},{9,10},{10,... | collective-permute-start | bytes 61448 | tf_op jit(solution)/shard_map/ppermute | solution.py:64
  33.5 3.8 %collective-permute-start.12 = (f32[8,640]{1,0:T(8,128)S(1)}, f32[8,640]{1,0:T(8,128)S(1)}, u32[]{:S(2)}, u32[]{:S(2)}) collective-permute-start(f32[8,640]{1,0:T(8,128)S(1)} %get-tuple-element.53), channel_id=1, source_target_pairs={{0,2},{1,3},{2,0},{3,1},{4,6},{5,7},{6,4},{7,5},{8,10},{9,11},{10,... | collective-permute-start | bytes 61448 | tf_op jit(solution)/shard_map/ppermute | solution.py:64
  35.1 2.3 %collective-permute-start.13 = (f32[8,640]{1,0:T(8,128)S(1)}, f32[8,640]{1,0:T(8,128)S(1)}, u32[]{:S(2)}, u32[]{:S(2)}) collective-permute-start(f32[8,640]{1,0:T(8,128)S(1)} %get-tuple-element.54), channel_id=1, source_target_pairs={{0,1},{1,0},{2,3},{3,2},{4,5},{5,4},{6,7},{7,6},{8,9},{9,8},{10,11... | collective-permute-start | bytes 61448 | tf_op jit(solution)/shard_map/ppermute | solution.py:64

commit v5 on v4

--- a/solution.py
+++ b/solution.py
@@ -1,3 +1,4 @@
+import functools
 import math
 
 import jax
@@ -12,7 +13,8 @@
 EPS = 1e-06
 BLOCK = 512
 PLAN_BITS = 4
-TOGETHER = 8
+TOGETHER = 16
+STEP = 2
 LANES = 128
 FAR = 1 << 20
 EXTRA_ROWS = 16
@@ -284,10 +286,8 @@
             start = jnp.where(past, starts[i], start)
         return r, inside - start + 1
 
-    tail = TOGETHER // 2
-    spare = left & (TOGETHER - 1)
-    rounds = (left >> log2(TOGETHER)) + jnp.where(spare > tail, 1, 0)
-    tails = jnp.where((spare > 0) & (spare <= tail), 1, 0)
+    rounds = left >> log2(TOGETHER)
+    rest = left & (TOGETHER - 1)
     extras = []
     for r in range(count):
         extra = (
@@ -320,7 +320,9 @@
 
     def all_others(some):
         pl.loop(0, rounds)(lambda k: some(k * TOGETHER, TOGETHER))
-        pl.loop(0, tails)(lambda k: some(rounds * TOGETHER, tail))
+        for size in range(STEP, TOGETHER + 1, STEP):
+            fits = (rest > size - STEP) & (rest <= size)
+            pl.when(fits)(functools.partial(some, rounds * TOGETHER, size))
 
     all_others(score_some)
     for r in range(count):

time: 37.6 us -> 37.2 us (0.989)
  Pallas kernels: 10.4 us -> 7.61 us
  waiting for transfers between devices: 9.1 us -> 11.1 us
    ppermute x8, waiting for transfers between devices: 5.95 us -> 7.93 us  [swap_req(): return lax.ppermute(x, ('req', 'kv'), pairs)]
    pallas_call x2, Pallas kernels: 5.43 us -> 3.58 us  [load(): pl.pallas_call(kernel, out_shape=jax.ShapeDtypeStruct(turned if turn else...]
    pallas_call x1, Pallas kernels: 2.22 us -> 1.31 us  [attend_call(): pl.pallas_call(lambda *refs: attend_kernel(len(parts), *refs), out_shape=...]
  transfers between devices with their start and end apart: 14 -> 14, of which waited for: 8 -> 8; matrix products, arithmetic and copies ran while one was open for 1% -> 1% of each run, Pallas kernels for 19% -> 14%
where the time goes in v5:
time: 37.2 us; the launch traced here: 37.3 us
  starting transfers between devices  17.5 us (47%)
  waiting for transfers between devices  11.1 us (30%)
  Pallas kernels  7.61 us (20%)
  other arithmetic  0.88 us (2%)
    ppermute x8, starting transfers between devices, swap_req(): return lax.ppermute(x, ('req', 'kv'), pairs)  12.4 us
    ppermute x8, waiting for transfers between devices, swap_req(): return lax.ppermute(x, ('req', 'kv'), pairs)  7.93 us
    ppermute x6, starting transfers between devices, swap_kv(): return lax.ppermute(x, 'kv', [(j, j ^ offset) for j in range(n_kv)])  5.07 us
    pallas_call x2, Pallas kernels, load(): pl.pallas_call(kernel, out_shape=jax.ShapeDtypeStruct(turned if turn else...  3.58 us
    ppermute x6, waiting for transfers between devices, swap_kv(): return lax.ppermute(x, 'kv', [(j, j ^ offset) for j in range(n_kv)])  3.14 us
    pallas_call x1, Pallas kernels, on_device(): pl.pallas_call(load_weights_kernel, out_shape=tuple((jax.ShapeDtypeStruct...  1.69 us
    pallas_call x1, Pallas kernels, attend_call(): pl.pallas_call(lambda *refs: attend_kernel(len(parts), *refs), out_shape=...  1.31 us
  transfers between devices with their start and end apart: 14, of which 8 were waited for; matrix products, arithmetic and copies ran while one was open for 1% of the time, Pallas kernels for 14%

profile of v5, /device:TPU:0, one launch (start us, length us, event | category | flops | bytes accessed | tf_op | source)
XLA Modules:
  0.0 37.3 jit_solution(8968924898856743893)
XLA Ops:
  0.0 2.4 %collective-permute-start.1 = (bf16[8,640]{1,0:T(8,128)(2,1)}, bf16[8,640]{1,0:T(8,128)(2,1)S(1)}, u32[]{:S(2)}, u32[]{:S(2)}) collective-permute-start(bf16[8,640]{1,0:T(8,128)(2,1)} %refs_3_.1), channel_id=1, source_target_pairs={{0,3},{1,2},{2,1},{3,0},{4,7},{5,6},{6,5},{7,4},{8,11},{9,10},{10,... | collective-permute-start | bytes 30728 | tf_op jit(solution)/shard_map/ppermute | solution.py:66
  2.4 0.7 %collective-permute-start = (bf16[8,640]{1,0:T(8,128)(2,1)}, bf16[8,640]{1,0:T(8,128)(2,1)S(1)}, u32[]{:S(2)}, u32[]{:S(2)}) collective-permute-start(bf16[8,640]{1,0:T(8,128)(2,1)} %refs_3_.1), channel_id=1, source_target_pairs={{0,1},{1,0},{2,3},{3,2},{4,5},{5,4},{6,7},{7,6},{8,9},{9,8},{10,11... | collective-permute-start | bytes 30728 | tf_op jit(solution)/shard_map/ppermute | solution.py:66
  3.1 1.7 %load_weights.1 = (bf16[640,1280]{1,0:T(8,128)(2,1)S(1)}, bf16[640,256]{1,0:T(8,128)(2,1)S(1)}, bf16[640,256]{1,0:T(8,128)(2,1)S(1)}, bf16[8,640]{1,0:T(8,128)(2...) custom-call(bf16[640,1280]{1,0:T(8,128)(2,1)} %refs_0_.1, ...), custom_call_target="tpu_custom_call" | custom-call | bytes 6291456 | tf_op jit(solution)/shard_map/load_weights/pallas_call | solution.py:444
  4.8 0.0 collective-permute-done.1.refs_3_
  4.8 0.1 collective-permute-start.2
  4.9 0.0 collective-permute-done.refs_1_
  4.9 1.1 %collective-permute-done.2.refs_2_ = bf16[8,640]{1,0:T(8,128)(2,1)S(1)} collective-permute-done((bf16[8,640]{1,0:T(8,128)(2,1)S(1)}, bf16[8,640]{1,0:T(8,128)(2,1)S(1)}, u32[]{:S(2)}, u32[]{:S(2)}) %collective-permute-start.2) | collective-permute-done | bytes 10272 | tf_op jit(solution)/shard_map/ppermute | solution.py:66
  6.1 0.5 %project.1 = (f32[16,1920]{1,0:T(8,128)S(1)}, f32[16,1920]{1,0:T(8,128)S(1)}) custom-call(bf16[8,640]{1,0:T(8,128)(2,1)S(1)} %get-tuple-element.30.refs_0_, bf16[8,640]{1,0:T(8,128)(2,1)S(1)} %collective-permute-done.refs_1_, bf16[8,640]{1,0:T(8,128)(2,1)S(1)} %collective-permute-done.2.refs_2_, bf16[8,640]{1,0:T(8,128)(2,1)S(1)} %collective-permute-done.1.refs_3_, ...), custom_call_target="tpu_custom_call" | custom-call | tf_op jit(solution)/shard_map/project/pallas_call | solution.py:460
  6.6 1.6 %collective-permute-start.3 = (f32[16,1920]{1,0:T(8,128)S(1)}, f32[16,1920]{1,0:T(8,128)S(1)}, u32[]{:S(2)}, u32[]{:S(2)}) collective-permute-start(f32[16,1920]{1,0:T(8,128)S(1)} %get-tuple-element.42), channel_id=1, source_target_pairs={{0,4},{1,9},{2,6},{3,11},{4,0},{5,13},{6,2},{7,15},{8,12},{9,1},{1... | collective-permute-start | bytes 368648 | tf_op jit(solution)/shard_map/ppermute | solution.py:62
  8.2 0.1 fusion
  8.3 0.1 broadcast_in_dim.2.plan.refs_0_
  8.4 1.9 %load_keys.1.refs_10_ = bf16[4,256,4608]{2,1,0:T(8,128)(2,1)S(1)} custom-call(s32[4,4,128]{2,1,0:T(4,128)S(1)} %broadcast_in_dim.2.plan.refs_0_, bf16[4,2,4096,128]{3,2,1,0:T(8,128)(2,1)} %cache.2), custom_call_target="tpu_custom_call" | custom-call | bytes 6291456 | tf_op jit(solution)/shard_map/load_keys/pallas_call | solution.py:478
  10.3 1.2 %collective-permute-done.3 = f32[16,1920]{1,0:T(8,128)S(1)} collective-permute-done((f32[16,1920]{1,0:T(8,128)S(1)}, f32[16,1920]{1,0:T(8,128)S(1)}, u32[]{:S(2)}, u32[]{:S(2)}) %collective-permute-start.3) | collective-permute-done | bytes 122912 | tf_op jit(solution)/shard_map/ppermute | solution.py:62
  11.6 3.7 %collective-permute-start.6 = (f32[4,1920]{1,0:T(4,128)S(1)}, f32[4,1920]{1,0:T(4,128)S(1)}, u32[]{:S(2)}, u32[]{:S(2)}) collective-permute-start(f32[4,1920]{1,0:T(4,128)S(1)} %get-tuple-element.57), channel_id=1, source_target_pairs={{0,24},{1,21},{2,26},{3,23},{4,28},{5,17},{6,30},{7,19},{8,16},{9,... | collective-permute-start | bytes 92168 | tf_op jit(solution)/shard_map/ppermute | solution.py:62
  15.3 0.0 collective-permute-start.5
  15.3 0.8 %collective-permute-start.4 = (f32[4,1920]{1,0:T(4,128)S(1)}, f32[4,1920]{1,0:T(4,128)S(1)}, u32[]{:S(2)}, u32[]{:S(2)}) collective-permute-start(f32[4,1920]{1,0:T(4,128)S(1)} %get-tuple-element.59), channel_id=1, source_target_pairs={{0,8},{1,5},{2,10},{3,7},{4,12},{5,1},{6,14},{7,3},{8,0},{9,13},{1... | collective-permute-start | bytes 92168 | tf_op jit(solution)/shard_map/ppermute | solution.py:62
  16.1 0.1 pad_maximum_fusion.1
  16.1 1.6 %load_values.1.refs_11_ = bf16[4,2,4608,128]{3,2,1,0:T(8,128)(2,1)S(1)} custom-call(s32[4,4,128]{2,1,0:T(4,128)S(1)} %broadcast_in_dim.2.plan.refs_0_, bf16[4,2,4096,128]{3,2,1,0:T(8,128)(2,1)} %cache.3), custom_call_target="tpu_custom_call" | custom-call | bytes 6291456 | tf_op jit(solution)/shard_map/load_values/pallas_call | solution.py:478
  17.8 0.0 collective-permute-done.6.refs_4_
  17.8 2.3 %collective-permute-done.5.refs_3_ = f32[4,1920]{1,0:T(4,128)S(1)} collective-permute-done((f32[4,1920]{1,0:T(4,128)S(1)}, f32[4,1920]{1,0:T(4,128)S(1)}, u32[]{:S(2)}, u32[]{:S(2)}) %collective-permute-start.5) | collective-permute-done | bytes 30752 | tf_op jit(solution)/shard_map/ppermute | solution.py:62
  20.1 0.0 collective-permute-done.4.refs_2_
  20.1 0.0 copy-start
  20.1 1.3 %attend.1 = bf16[4,1280]{1,0:T(4,128)(2,1)S(1)} custom-call(s32[4,4,128]{2,1,0:T(4,128)S(1)} %broadcast_in_dim.2.plan.refs_0_, f32[4,1920]{1,0:T(4,128)S(1)} %get-tuple-element.44.refs_1_, f32[4,1920]{1,0:T(4,128)S(1)} %collective-permute-done.4.refs_2_, f32[4,1920]{1,0:T(4,128)S(1)} %collective-permute-done.5.refs_3_, ...), custom_call_target="tpu_custom_call" | custom-call | tf_op jit(solution)/shard_map/attend/pallas_call | solution.py:376
  21.4 2.0 %collective-permute-start.7 = (bf16[4,1280]{1,0:T(4,128)(2,1)S(1)}, bf16[4,1280]{1,0:T(4,128)(2,1)S(1)}, u32[]{:S(2)}, u32[]{:S(2)}) collective-permute-start(bf16[4,1280]{1,0:T(4,128)(2,1)S(1)} %attend.1), channel_id=1, source_target_pairs={{0,4},{1,9},{2,6},{3,11},{4,0},{5,13},{6,2},{7,15},{8,12},{9,1},{1... | collective-permute-start | bytes 30728 | tf_op jit(solution)/shard_map/ppermute | solution.py:62
  23.3 1.8 %collective-permute-done.7 = bf16[4,1280]{1,0:T(4,128)(2,1)S(1)} collective-permute-done((bf16[4,1280]{1,0:T(4,128)(2,1)S(1)}, bf16[4,1280]{1,0:T(4,128)(2,1)S(1)}, u32[]{:S(2)}, u32[]{:S(2)}) %collective-permute-start.7) | collective-permute-done | bytes 10272 | tf_op jit(solution)/shard_map/ppermute | solution.py:62
  25.1 2.4 %collective-permute-start.10 = (bf16[8,1280]{1,0:T(8,128)(2,1)S(1)}, bf16[8,1280]{1,0:T(8,128)(2,1)S(1)}, u32[]{:S(2)}, u32[]{:S(2)}) collective-permute-start(bf16[8,1280]{1,0:T(8,128)(2,1)S(1)} %pad_maximum_fusion), channel_id=1, source_target_pairs={{0,24},{1,21},{2,26},{3,23},{4,28},{5,17},{6,30},{7,19},{8,16},{9,... | collective-permute-start | bytes 61448 | tf_op jit(solution)/shard_map/ppermute | solution.py:62
  27.5 0.0 collective-permute-start.9
  27.6 2.0 %collective-permute-start.8 = (bf16[8,1280]{1,0:T(8,128)(2,1)S(1)}, bf16[8,1280]{1,0:T(8,128)(2,1)S(1)}, u32[]{:S(2)}, u32[]{:S(2)}) collective-permute-start(bf16[8,1280]{1,0:T(8,128)(2,1)S(1)} %pad_maximum_fusion), channel_id=1, source_target_pairs={{0,8},{1,5},{2,10},{3,7},{4,12},{5,1},{6,14},{7,3},{8,0},{9,13},{1... | collective-permute-start | bytes 61448 | tf_op jit(solution)/shard_map/ppermute | solution.py:62
  29.6 1.2 %collective-permute-done.10 = bf16[8,1280]{1,0:T(8,128)(2,1)S(1)} collective-permute-done((bf16[8,1280]{1,0:T(8,128)(2,1)S(1)}, bf16[8,1280]{1,0:T(8,128)(2,1)S(1)}, u32[]{:S(2)}, u32[]{:S(2)}) %collective-permute-start.10) | collective-permute-done | bytes 20512 | tf_op jit(solution)/shard_map/ppermute | solution.py:62
  30.8 1.4 %collective-permute-done.9 = bf16[8,1280]{1,0:T(8,128)(2,1)S(1)} collective-permute-done((bf16[8,1280]{1,0:T(8,128)(2,1)S(1)}, bf16[8,1280]{1,0:T(8,128)(2,1)S(1)}, u32[]{:S(2)}, u32[]{:S(2)}) %collective-permute-start.9) | collective-permute-done | bytes 20512 | tf_op jit(solution)/shard_map/ppermute | solution.py:62
  32.2 0.0 collective-permute-done.8
  32.3 0.0 copy-done
  32.3 0.5 %output.1 = (f32[8,640]{1,0:T(8,128)S(1)}, f32[8,640]{1,0:T(8,128)S(1)}, f32[8,640]{1,0:T(8,128)S(1)}, f32[8,640]{1,0:T(8,128)S(1)}) custom-call(bf16[32,1280]{1,0:T(8,128)(2,1)S(1)} %concatenate.16.context, bf16[1280,640]{1,0:T(8,128)(2,1)S(1)} %copy-done), custom_call_target="tpu_custom_call" | custom-call | tf_op jit(solution)/shard_map/output/pallas_call | solution.py:521
  32.8 0.1 collective-permute-start.11
  32.9 1.5 %collective-permute-start.12 = (f32[8,640]{1,0:T(8,128)S(1)}, f32[8,640]{1,0:T(8,128)S(1)}, u32[]{:S(2)}, u32[]{:S(2)}) collective-permute-start(f32[8,640]{1,0:T(8,128)S(1)} %get-tuple-element.53), channel_id=1, source_target_pairs={{0,2},{1,3},{2,0},{3,1},{4,6},{5,7},{6,4},{7,5},{8,10},{9,11},{10,... | collective-permute-start | bytes 61448 | tf_op jit(solution)/shard_map/ppermute | solution.py:66
  34.4 0.3 collective-permute-start.13
  34.7 1.5 %collective-permute-done.11 = f32[8,640]{1,0:T(8,128)S(1)} collective-permute-done((f32[8,640]{1,0:T(8,128)S(1)}, f32[8,640]{1,0:T(8,128)S(1)}, u32[]{:S(2)}, u32[]{:S(2)}) %collective-permute-start.11) | collective-permute-done | bytes 20512 | tf_op jit(solution)/shard_map/ppermute | solution.py:66
  36.3 0.5 %collective-permute-done.12 = f32[8,640]{1,0:T(8,128)S(1)} collective-permute-done((f32[8,640]{1,0:T(8,128)S(1)}, f32[8,640]{1,0:T(8,128)S(1)}, u32[]{:S(2)}, u32[]{:S(2)}) %collective-permute-start.12) | collective-permute-done | bytes 20512 | tf_op jit(solution)/shard_map/ppermute | solution.py:66
  36.7 0.0 collective-permute-done.13
  36.7 0.6 %add_convert_fusion = bf16[8,640]{1,0:T(8,128)(2,1)} fusion(f32[8,640]{1,0:T(8,128)S(1)} %collective-permute-done.13, f32[8,640]{1,0:T(8,128)S(1)} %collective-permute-done.12, f32[8,640]{1,0:T(8,128)S(1)} %get-tuple-element.51, f32[8,640]{1,0:T(8,128)S(1)} %collective-permute-done.11), kind=kLoop, calls=%fused_computation.1 | loop fusion | flops 20480 | bytes 92160 | tf_op jit(solution)/shard_map/convert_element_type | solution.py:532
  (8 shorter events, 0.1 us)
Async XLA Ops:
  0.0 4.8 %collective-permute-start.1 = (bf16[8,640]{1,0:T(8,128)(2,1)}, bf16[8,640]{1,0:T(8,128)(2,1)S(1)}, u32[]{:S(2)}, u32[]{:S(2)}) collective-permute-start(bf16[8,640]{1,0:T(8,128)(2,1)} %refs_3_.1), channel_id=1, source_target_pairs={{0,3},{1,2},{2,1},{3,0},{4,7},{5,6},{6,5},{7,4},{8,11},{9,10},{10,... | collective-permute-start | bytes 30728 | tf_op jit(solution)/shard_map/ppermute | solution.py:66
  2.4 2.5 %collective-permute-start = (bf16[8,640]{1,0:T(8,128)(2,1)}, bf16[8,640]{1,0:T(8,128)(2,1)S(1)}, u32[]{:S(2)}, u32[]{:S(2)}) collective-permute-start(bf16[8,640]{1,0:T(8,128)(2,1)} %refs_3_.1), channel_id=1, source_target_pairs={{0,1},{1,0},{2,3},{3,2},{4,5},{5,4},{6,7},{7,6},{8,9},{9,8},{10,11... | collective-permute-start | bytes 30728 | tf_op jit(solution)/shard_map/ppermute | solution.py:66
  4.8 1.2 %collective-permute-start.2 = (bf16[8,640]{1,0:T(8,128)(2,1)S(1)}, bf16[8,640]{1,0:T(8,128)(2,1)S(1)}, u32[]{:S(2)}, u32[]{:S(2)}) collective-permute-start(bf16[8,640]{1,0:T(8,128)(2,1)S(1)} %collective-permute-done.1.refs_3_), channel_id=1, source_target_pairs={{0,1},{1,0},{2,3},{3,2},{4,5},{5,4},{6,7},{7,6},{8,9},{9,8},{10,11... | collective-permute-start | bytes 30728 | tf_op jit(solution)/shard_map/ppermute | solution.py:66
  6.6 4.9 %collective-permute-start.3 = (f32[16,1920]{1,0:T(8,128)S(1)}, f32[16,1920]{1,0:T(8,128)S(1)}, u32[]{:S(2)}, u32[]{:S(2)}) collective-permute-start(f32[16,1920]{1,0:T(8,128)S(1)} %get-tuple-element.42), channel_id=1, source_target_pairs={{0,4},{1,9},{2,6},{3,11},{4,0},{5,13},{6,2},{7,15},{8,12},{9,1},{1... | collective-permute-start | bytes 368648 | tf_op jit(solution)/shard_map/ppermute | solution.py:62
  11.6 6.2 %collective-permute-start.6 = (f32[4,1920]{1,0:T(4,128)S(1)}, f32[4,1920]{1,0:T(4,128)S(1)}, u32[]{:S(2)}, u32[]{:S(2)}) collective-permute-start(f32[4,1920]{1,0:T(4,128)S(1)} %get-tuple-element.57), channel_id=1, source_target_pairs={{0,24},{1,21},{2,26},{3,23},{4,28},{5,17},{6,30},{7,19},{8,16},{9,... | collective-permute-start | bytes 92168 | tf_op jit(solution)/shard_map/ppermute | solution.py:62
  15.3 4.8 %collective-permute-start.5 = (f32[4,1920]{1,0:T(4,128)S(1)}, f32[4,1920]{1,0:T(4,128)S(1)}, u32[]{:S(2)}, u32[]{:S(2)}) collective-permute-start(f32[4,1920]{1,0:T(4,128)S(1)} %get-tuple-element.58), channel_id=1, source_target_pairs={{0,16},{1,17},{2,18},{3,19},{4,20},{5,21},{6,22},{7,23},{8,24},{9,... | collective-permute-start | bytes 92168 | tf_op jit(solution)/shard_map/ppermute | solution.py:62
  15.3 4.8 %collective-permute-start.4 = (f32[4,1920]{1,0:T(4,128)S(1)}, f32[4,1920]{1,0:T(4,128)S(1)}, u32[]{:S(2)}, u32[]{:S(2)}) collective-permute-start(f32[4,1920]{1,0:T(4,128)S(1)} %get-tuple-element.59), channel_id=1, source_target_pairs={{0,8},{1,5},{2,10},{3,7},{4,12},{5,1},{6,14},{7,3},{8,0},{9,13},{1... | collective-permute-start | bytes 92168 | tf_op jit(solution)/shard_map/ppermute | solution.py:62
  20.1 12.2 %copy-start = (bf16[1280,640]{1,0:T(8,128)(2,1)S(1)}, bf16[1280,640]{1,0:T(8,128)(2,1)}, u32[]{:S(2)}) copy-start(bf16[1280,640]{1,0:T(8,128)(2,1)} %w_output.1) | copy-start | bytes 4915204
  21.4 3.7 %collective-permute-start.7 = (bf16[4,1280]{1,0:T(4,128)(2,1)S(1)}, bf16[4,1280]{1,0:T(4,128)(2,1)S(1)}, u32[]{:S(2)}, u32[]{:S(2)}) collective-permute-start(bf16[4,1280]{1,0:T(4,128)(2,1)S(1)} %attend.1), channel_id=1, source_target_pairs={{0,4},{1,9},{2,6},{3,11},{4,0},{5,13},{6,2},{7,15},{8,12},{9,1},{1... | collective-permute-start | bytes 30728 | tf_op jit(solution)/shard_map/ppermute | solution.py:62
  25.1 5.6 %collective-permute-start.10 = (bf16[8,1280]{1,0:T(8,128)(2,1)S(1)}, bf16[8,1280]{1,0:T(8,128)(2,1)S(1)}, u32[]{:S(2)}, u32[]{:S(2)}) collective-permute-start(bf16[8,1280]{1,0:T(8,128)(2,1)S(1)} %pad_maximum_fusion), channel_id=1, source_target_pairs={{0,24},{1,21},{2,26},{3,23},{4,28},{5,17},{6,30},{7,19},{8,16},{9,... | collective-permute-start | bytes 61448 | tf_op jit(solution)/shard_map/ppermute | solution.py:62
  27.5 4.7 %collective-permute-start.9 = (bf16[8,1280]{1,0:T(8,128)(2,1)S(1)}, bf16[8,1280]{1,0:T(8,128)(2,1)S(1)}, u32[]{:S(2)}, u32[]{:S(2)}) collective-permute-start(bf16[8,1280]{1,0:T(8,128)(2,1)S(1)} %pad_maximum_fusion), channel_id=1, source_target_pairs={{0,16},{1,17},{2,18},{3,19},{4,20},{5,21},{6,22},{7,23},{8,24},{9,... | collective-permute-start | bytes 61448 | tf_op jit(solution)/shard_map/ppermute | solution.py:62
  27.6 4.7 %collective-permute-start.8 = (bf16[8,1280]{1,0:T(8,128)(2,1)S(1)}, bf16[8,1280]{1,0:T(8,128)(2,1)S(1)}, u32[]{:S(2)}, u32[]{:S(2)}) collective-permute-start(bf16[8,1280]{1,0:T(8,128)(2,1)S(1)} %pad_maximum_fusion), channel_id=1, source_target_pairs={{0,8},{1,5},{2,10},{3,7},{4,12},{5,1},{6,14},{7,3},{8,0},{9,13},{1... | collective-permute-start | bytes 61448 | tf_op jit(solution)/shard_map/ppermute | solution.py:62
  32.8 3.5 %collective-permute-start.11 = (f32[8,640]{1,0:T(8,128)S(1)}, f32[8,640]{1,0:T(8,128)S(1)}, u32[]{:S(2)}, u32[]{:S(2)}) collective-permute-start(f32[8,640]{1,0:T(8,128)S(1)} %get-tuple-element.52), channel_id=1, source_target_pairs={{0,3},{1,2},{2,1},{3,0},{4,7},{5,6},{6,5},{7,4},{8,11},{9,10},{10,... | collective-permute-start | bytes 61448 | tf_op jit(solution)/shard_map/ppermute | solution.py:66
  32.9 3.8 %collective-permute-start.12 = (f32[8,640]{1,0:T(8,128)S(1)}, f32[8,640]{1,0:T(8,128)S(1)}, u32[]{:S(2)}, u32[]{:S(2)}) collective-permute-start(f32[8,640]{1,0:T(8,128)S(1)} %get-tuple-element.53), channel_id=1, source_target_pairs={{0,2},{1,3},{2,0},{3,1},{4,6},{5,7},{6,4},{7,5},{8,10},{9,11},{10,... | collective-permute-start | bytes 61448 | tf_op jit(solution)/shard_map/ppermute | solution.py:66
  34.4 2.3 %collective-permute-start.13 = (f32[8,640]{1,0:T(8,128)S(1)}, f32[8,640]{1,0:T(8,128)S(1)}, u32[]{:S(2)}, u32[]{:S(2)}) collective-permute-start(f32[8,640]{1,0:T(8,128)S(1)} %get-tuple-element.54), channel_id=1, source_target_pairs={{0,1},{1,0},{2,3},{3,2},{4,5},{5,4},{6,7},{7,6},{8,9},{9,8},{10,11... | collective-permute-start | bytes 61448 | tf_op jit(solution)/shard_map/ppermute | solution.py:66

commit v6 on v5

--- a/solution.py
+++ b/solution.py
@@ -80,23 +80,33 @@
     return (kv_request == kv_row).astype(jnp.bfloat16)
 
 
-def load_weights_kernel(*refs):
-    n = len(refs) // 2
-    sem = refs[-1]
-    copies = [pltpu.make_async_copy(refs[i], refs[n + i], sem.at[i]) for i in range(n)]
+def prepare_kernel(rows_req, rows_kv, n, sink_keys, sink_values, *refs):
+    sources, copied = refs[:n], refs[n : 2 * n]
+    order_in, order_out, k_extra, v_extra, k_sinks, v_sinks, sem = refs[2 * n :]
+    pairs = list(zip(sources, copied)) + [(sink_keys, k_sinks), (sink_values, v_sinks)]
+    copies = [
+        pltpu.make_async_copy(source, target, sem.at[i]) for i, (source, target) in enumerate(pairs)
+    ]
     for copy in copies:
         copy.start()
+    size = order_in.shape[0]
+    order_in[...] = row_order(size, rows_req, rows_kv, False)
+    order_out[...] = row_order(size, rows_req, rows_kv, True)
+    k_extra[...] = jnp.zeros_like(k_extra)
+    v_extra[...] = jnp.zeros_like(v_extra)
     for copy in copies:
         copy.wait()
-
-
-def project_kernel(rows_req, n_kv, *refs):
-    pieces, (gain, w_query, w_key, w_value, keep, send) = refs[:n_kv], refs[n_kv:]
-    rows_kv = pieces[0].shape[0]
-    size = rows_kv * n_kv
-    order = row_order(size, rows_req, rows_kv, False)
+    for r in range(k_sinks.shape[0]):
+        for h in range(k_sinks.shape[1]):
+            lanes = slice(h * k_sinks.shape[3], (h + 1) * k_sinks.shape[3])
+            k_extra[r, 0:SINKS, lanes] = k_sinks[r, h].astype(jnp.float32)
+            v_extra[r, 0:SINKS, lanes] = v_sinks[r, h].astype(jnp.float32)
+
+
+def project_kernel(n_kv, *refs):
+    pieces, (order, gain, w_query, w_key, w_value, keep, send) = refs[:n_kv], refs[n_kv:]
     hidden = jnp.concatenate([piece[...].astype(jnp.float32) for piece in pieces], 0)
-    xf = jnp.dot(order, hidden.astype(jnp.bfloat16), preferred_element_type=jnp.float32)
+    xf = jnp.dot(order[...], hidden.astype(jnp.bfloat16), preferred_element_type=jnp.float32)
     rows = gain[...].astype(jnp.float32)
     wide_gain = jnp.concatenate([rows[i : i + 1] for i in range(rows.shape[0])], 1)
     scaled = (xf * wide_gain).astype(jnp.bfloat16)
@@ -112,7 +122,7 @@
         put(at, jnp.dot(scaled, weight[...], preferred_element_type=jnp.float32))
         at += weight.shape[1]
     squares = jnp.sum(xf * xf, 1, keepdims=True)
-    put(at, jnp.broadcast_to(squares, (size, LANES)))
+    put(at, jnp.broadcast_to(squares, (2 * half, LANES)))
 
 
 def plan_of(lengths, sink_count, window):
@@ -179,13 +189,11 @@
         b_value,
         k_buf,
         v_buf,
-        sink_keys,
-        sink_values,
+        k_extra,
+        v_extra,
         context,
         score_buf,
         q_heads,
-        k_extra,
-        v_extra,
         result_buf,
         q_rows,
         tops,
@@ -215,8 +223,7 @@
         return x * cos + pltpu.roll(x, size // 2, 1) * sin
 
     q_heads[...] = jnp.zeros_like(q_heads)
-    k_extra[...] = jnp.zeros_like(k_extra)
-    v_extra[...] = jnp.zeros_like(v_extra)
+    k_new, v_new = [], []
     for h in range(heads_kv):
         lanes = slice(h * size, (h + 1) * size)
         for g in range(group):
@@ -224,13 +231,13 @@
             block = rotated(head_of(head))
             for r in range(count):
                 q_heads[r, h * pad + g : h * pad + g + 1, lanes] = block[r : r + 1]
-        k_rot = rotated(head_of(heads_kv * group + h))
-        value = head_of(heads_kv * group + heads_kv + h)
-        for r in range(count):
-            k_extra[r, 0:SINKS, lanes] = sink_keys[r, h].astype(jnp.float32)
-            v_extra[r, 0:SINKS, lanes] = sink_values[r, h].astype(jnp.float32)
-            k_extra[r, SINKS : SINKS + 1, lanes] = k_rot[r : r + 1]
-            v_extra[r, SINKS : SINKS + 1, lanes] = value[r : r + 1]
+        k_new.append(rotated(head_of(heads_kv * group + h)))
+        v_new.append(head_of(heads_kv * group + heads_kv + h))
+    k_new, v_new = jnp.concatenate(k_new, 1), jnp.concatenate(v_new, 1)
+    own_row = lax.broadcasted_iota(jnp.int32, (EXTRA_ROWS, 1), 0) == SINKS
+
+    def extra_rows(base, new, r):
+        return jnp.where(own_row, new[r : r + 1], base[r]).astype(jnp.bfloat16)
 
     contract_last = (((1,), (1,)), ((), ()))
     lane = lax.broadcasted_iota(jnp.int32, (1, EXTRA_ROWS), 1)
@@ -293,7 +300,7 @@
         extra = (
             lax.dot_general(
                 q_rows[r],
-                k_extra[r].astype(jnp.bfloat16),
+                extra_rows(k_extra, k_new, r),
                 contract_last,
                 preferred_element_type=jnp.float32,
             )
@@ -333,7 +340,7 @@
         extras[r] = jnp.exp(extras[r] - top)
         numer = jnp.dot(
             extras[r].astype(jnp.bfloat16),
-            v_extra[r].astype(jnp.bfloat16),
+            extra_rows(v_extra, v_new, r),
             preferred_element_type=jnp.float32,
         )
         denoms[r], product = mix(r, 0, r)
@@ -353,11 +360,12 @@
     context[...] = result_buf[...].astype(context.dtype)
 
 
-def output_kernel(context, w_output, *outs):
-    size, rows_kv = context.shape[0], outs[0].shape[0]
-    rows_req = size // lax.axis_size("req")
-    order = row_order(size, rows_req, rows_kv, True)
-    rows = jnp.dot(order, context[...], preferred_element_type=jnp.float32).astype(jnp.bfloat16)
+def output_kernel(n_pieces, order, w_output, *refs):
+    pieces, outs = refs[:n_pieces], refs[n_pieces:]
+    rows_kv = outs[0].shape[0]
+    context = jnp.concatenate([piece[...].astype(jnp.float32) for piece in pieces], 0)
+    context = context.astype(jnp.bfloat16)
+    rows = jnp.dot(order[...], context, preferred_element_type=jnp.float32).astype(jnp.bfloat16)
     product = jnp.dot(rows, w_output[...], preferred_element_type=jnp.float32)
     for i, out in enumerate(outs):
         out[...] = product[i * rows_kv : (i + 1) * rows_kv]
@@ -367,12 +375,12 @@
     return pl.BlockSpec(memory_space=space)
 
 
-def attend_call(plan, parts, cosine, sine, b_query, b_key, b_value, k_live, v_live, *sinks):
+def attend_call(plan, parts, cosine, sine, b_query, b_key, b_value, k_live, v_live, *extras):
     count, heads_kv, stored, size = v_live.shape
     group = b_query.shape[0] // heads_kv
     rows, kv_cols = heads_kv * (-(-group // 8) * 8), heads_kv * size
     q_cols = b_query.shape[0] * size
-    args = (plan, *parts, cosine, sine, b_query, b_key, b_value, k_live, v_live, *sinks)
+    args = (plan, *parts, cosine, sine, b_query, b_key, b_value, k_live, v_live, *extras)
     return pl.pallas_call(
         lambda *refs: attend_kernel(len(parts), *refs),
         out_shape=jax.ShapeDtypeStruct((count, q_cols), jnp.bfloat16),
@@ -381,8 +389,6 @@
         scratch_shapes=[
             pltpu.VMEM((count * (stored // BLOCK) + TOGETHER, rows, BLOCK), jnp.float32),
             pltpu.VMEM((count, rows, kv_cols), jnp.float32),
-            pltpu.VMEM((count, EXTRA_ROWS, kv_cols), jnp.float32),
-            pltpu.VMEM((count, EXTRA_ROWS, kv_cols), jnp.float32),
             pltpu.VMEM((count, q_cols), jnp.float32),
             pltpu.VMEM((count, rows, kv_cols), jnp.bfloat16),
             pltpu.VMEM((count, rows, LANES), jnp.float32),
@@ -435,36 +441,43 @@
         b_query.reshape(-1, size),
         b_key.reshape(-1, size),
         b_value.reshape(-1, size),
-        sink_keys,
-        sink_values,
         lengths,
         sink_count,
         window,
     )
+    square = jax.ShapeDtypeStruct((rows, rows), bf16)
+    extra = jax.ShapeDtypeStruct((count, EXTRA_ROWS, kv_cols), f32)
+    outs = [jax.ShapeDtypeStruct(w.shape, w.dtype) for w in wanted] + [square] * 2 + [extra] * 2
+    n = len(wanted)
     fetched = pl.pallas_call(
-        load_weights_kernel,
-        out_shape=tuple(jax.ShapeDtypeStruct(w.shape, w.dtype) for w in wanted),
-        in_specs=[spec(pltpu.HBM)] * len(wanted),
-        out_specs=(spec(),) * len(wanted),
-        scratch_shapes=[pltpu.SemaphoreType.DMA((len(wanted),))],
-        compiler_params=pltpu.CompilerParams(vmem_limit_bytes=1 << 20),
+        lambda *refs: prepare_kernel(count, rows_kv, n, *refs),
+        out_shape=tuple(outs),
+        in_specs=[spec(pltpu.HBM)] * (n + 2),
+        out_specs=(spec(),) * len(outs),
+        scratch_shapes=[
+            pltpu.VMEM(sink_keys.shape, bf16),
+            pltpu.VMEM(sink_values.shape, bf16),
+            pltpu.SemaphoreType.DMA((n + 2,)),
+        ],
+        compiler_params=pltpu.CompilerParams(vmem_limit_bytes=2 << 20),
         cost_estimate=pl.CostEstimate(flops=0, transcendentals=0, bytes_accessed=6 << 20),
-        name="load_weights",
-    )(*[in_hbm(w) for w in wanted])
-    *weights, mine, gain, b_query, b_key, b_value, sink_keys, sink_values = fetched[:-3]
-    lengths, sink_count, window = fetched[-3:]
+        name="prepare",
+    )(*[in_hbm(w) for w in (sink_keys, sink_values, *wanted)])
+    *weights, mine, gain, b_query, b_key, b_value = fetched[: n - 3]
+    lengths, sink_count, window = fetched[n - 3 : n]
+    order_in, order_out, *extras = fetched[n:]
     pieces = [mine, others[0]]
     for far in others[1:]:
         pieces += [swap_kv(far, n_kv, 1), far]
     half = jax.ShapeDtypeStruct((rows // 2, wide), f32)
     keep, send = pl.pallas_call(
-        lambda *refs: project_kernel(count, n_kv, *refs),
+        lambda *refs: project_kernel(n_kv, *refs),
         out_shape=(half, half),
-        in_specs=[spec()] * (n_kv + 4),
+        in_specs=[spec()] * (n_kv + 5),
         out_specs=(spec(), spec()),
         compiler_params=pltpu.CompilerParams(vmem_limit_bytes=16 << 20),
         name="project",
-    )(*pieces, gain, *weights)
+    )(*pieces, order_in, gain, *weights)
 
     visits = cycle // BLOCK + 1
 
@@ -510,22 +523,23 @@
     sine = jnp.concatenate([-sin, sin], 1)
 
     context = attend_call(
-        plan, parts, cosine, sine, b_query, b_key, b_value, k_live, v_live, sink_keys, sink_values
+        plan, parts, cosine, sine, b_query, b_key, b_value, k_live, v_live, *extras
     )
 
-    everyone = context
+    pieces = [context]
     for radix, unit in stages(n_req):
+        everyone = jnp.concatenate(pieces, 0) if len(pieces) > 1 else pieces[0]
         blocks = [swap_req(everyone, n_req, n_kv, q * unit) for q in range(1, radix)]
-        everyone = jnp.concatenate([everyone] + blocks, 0)
+        pieces = [everyone] + blocks
     piece = jax.ShapeDtypeStruct((rows_kv, w_output.shape[1]), f32)
     products = pl.pallas_call(
-        output_kernel,
+        lambda *refs: output_kernel(len(pieces), *refs),
         out_shape=(piece,) * n_kv,
-        in_specs=[spec()] * 2,
+        in_specs=[spec()] * (len(pieces) + 2),
         out_specs=(spec(),) * n_kv,
         compiler_params=pltpu.CompilerParams(vmem_limit_bytes=16 << 20),
         name="output",
-    )(everyone, w_output)
+    )(order_out, w_output, *pieces)
     result = products[0]
     for u in range(n_kv - 1, 0, -1):
         result = result + swap_kv(products[u], n_kv, u)

time: 37.2 us -> 37.1 us (level)
  Pallas kernels: 7.61 us -> 10 us
  waiting for transfers between devices: 11.1 us -> 9.27 us
  starting transfers between devices: 17.5 us -> 16.7 us
    pallas_call x2, Pallas kernels: 3.58 us -> 5.43 us  [load(): pl.pallas_call(kernel, out_shape=jax.ShapeDtypeStruct(turned if turn else...]
    ppermute x8, waiting for transfers between devices: 7.93 us -> 6.13 us  [swap_req(): return lax.ppermute(x, ('req', 'kv'), pairs)]
    ppermute x8, starting transfers between devices: 12.4 us -> 11.6 us  [swap_req(): return lax.ppermute(x, ('req', 'kv'), pairs)]
    pallas_call x1, Pallas kernels: 1.31 us -> 1.87 us  [attend_call(): pl.pallas_call(lambda *refs: attend_kernel(len(parts), *refs), out_shape=...]
  transfers between devices with their start and end apart: 14 -> 14, of which waited for: 8 -> 9; matrix products, arithmetic and copies ran while one was open for 1% -> 1% of each run, Pallas kernels for 14% -> 19%
where the time goes in v6:
time: 37.1 us; the launch traced here: 37 us
  starting transfers between devices  16.7 us (45%)
  Pallas kernels  10 us (27%)
  waiting for transfers between devices  9.27 us (25%)
  other arithmetic  0.88 us (2%)
    ppermute x8, starting transfers between devices, swap_req(): return lax.ppermute(x, ('req', 'kv'), pairs)  11.6 us
    ppermute x8, waiting for transfers between devices, swap_req(): return lax.ppermute(x, ('req', 'kv'), pairs)  6.13 us
    pallas_call x2, Pallas kernels, load(): pl.pallas_call(kernel, out_shape=jax.ShapeDtypeStruct(turned if turn else...  5.43 us
    ppermute x6, starting transfers between devices, swap_kv(): return lax.ppermute(x, 'kv', [(j, j ^ offset) for j in range(n_kv)])  5.07 us
    ppermute x6, waiting for transfers between devices, swap_kv(): return lax.ppermute(x, 'kv', [(j, j ^ offset) for j in range(n_kv)])  3.14 us
    pallas_call x1, Pallas kernels, attend_call(): pl.pallas_call(lambda *refs: attend_kernel(len(parts), *refs), out_shape=...  1.87 us
    pallas_call x1, Pallas kernels, on_device(): pl.pallas_call(lambda *refs: prepare_kernel(count, rows_kv, n, *refs), ou...  1.71 us
  transfers between devices with their start and end apart: 14, of which 9 were waited for; matrix products, arithmetic and copies ran while one was open for 1% of the time, Pallas kernels for 19%

profile of v6, /device:TPU:0, one launch (start us, length us, event | category | flops | bytes accessed | tf_op | source)
XLA Modules:
  0.0 37.0 jit_solution(3663579220746011458)
XLA Ops:
  0.0 2.4 %collective-permute-start.1 = (bf16[8,640]{1,0:T(8,128)(2,1)}, bf16[8,640]{1,0:T(8,128)(2,1)S(1)}, u32[]{:S(2)}, u32[]{:S(2)}) collective-permute-start(bf16[8,640]{1,0:T(8,128)(2,1)} %refs_5_.1), channel_id=1, source_target_pairs={{0,3},{1,2},{2,1},{3,0},{4,7},{5,6},{6,5},{7,4},{8,11},{9,10},{10,... | collective-permute-start | bytes 30728 | tf_op jit(solution)/shard_map/ppermute | solution.py:66
  2.4 0.7 %collective-permute-start = (bf16[8,640]{1,0:T(8,128)(2,1)}, bf16[8,640]{1,0:T(8,128)(2,1)S(1)}, u32[]{:S(2)}, u32[]{:S(2)}) collective-permute-start(bf16[8,640]{1,0:T(8,128)(2,1)} %refs_5_.1), channel_id=1, source_target_pairs={{0,1},{1,0},{2,3},{3,2},{4,5},{5,4},{6,7},{7,6},{8,9},{9,8},{10,11... | collective-permute-start | bytes 30728 | tf_op jit(solution)/shard_map/ppermute | solution.py:66
  3.1 1.7 %prepare.1 = (bf16[640,1280]{1,0:T(8,128)(2,1)S(1)}, bf16[640,256]{1,0:T(8,128)(2,1)S(1)}, bf16[640,256]{1,0:T(8,128)(2,1)S(1)}, bf16[8,640]{1,0:T(8,128)(2,1)S(...) custom-call(bf16[4,2,4,128]{3,2,1,0:T(4,128)(2,1)} %refs_0_.1, ...), custom_call_target="tpu_custom_call" | custom-call | bytes 6291456 | tf_op jit(solution)/shard_map/prepare/pallas_call | solution.py:452
  4.8 0.0 collective-permute-done.1.refs_3_
  4.8 0.1 collective-permute-start.2
  4.9 0.0 collective-permute-done.refs_1_
  5.0 1.1 %collective-permute-done.2.refs_2_ = bf16[8,640]{1,0:T(8,128)(2,1)S(1)} collective-permute-done((bf16[8,640]{1,0:T(8,128)(2,1)S(1)}, bf16[8,640]{1,0:T(8,128)(2,1)S(1)}, u32[]{:S(2)}, u32[]{:S(2)}) %collective-permute-start.2) | collective-permute-done | bytes 10272 | tf_op jit(solution)/shard_map/ppermute | solution.py:66
  6.1 0.5 %project.1 = (f32[16,1920]{1,0:T(8,128)S(1)}, f32[16,1920]{1,0:T(8,128)S(1)}) custom-call(bf16[8,640]{1,0:T(8,128)(2,1)S(1)} %get-tuple-element.33.refs_0_, bf16[8,640]{1,0:T(8,128)(2,1)S(1)} %collective-permute-done.refs_1_, bf16[8,640]{1,0:T(8,128)(2,1)S(1)} %collective-permute-done.2.refs_2_, bf16[8,640]{1,0:T(8,128)(2,1)S(1)} %collective-permute-done.1.refs_3_, ...), custom_call_target="tpu_custom_call" | custom-call | tf_op jit(solution)/shard_map/project/pallas_call | solution.py:473
  6.6 1.6 %collective-permute-start.3 = (f32[16,1920]{1,0:T(8,128)S(1)}, f32[16,1920]{1,0:T(8,128)S(1)}, u32[]{:S(2)}, u32[]{:S(2)}) collective-permute-start(f32[16,1920]{1,0:T(8,128)S(1)} %get-tuple-element.46), channel_id=1, source_target_pairs={{0,4},{1,9},{2,6},{3,11},{4,0},{5,13},{6,2},{7,15},{8,12},{9,1},{1... | collective-permute-start | bytes 368648 | tf_op jit(solution)/shard_map/ppermute | solution.py:62
  8.2 0.1 fusion
  8.3 0.1 broadcast_in_dim.2.plan.refs_0_
  8.4 3.1 %load_keys.1.refs_10_ = bf16[4,256,4608]{2,1,0:T(8,128)(2,1)S(1)} custom-call(s32[4,4,128]{2,1,0:T(4,128)S(1)} %broadcast_in_dim.2.plan.refs_0_, bf16[4,2,4096,128]{3,2,1,0:T(8,128)(2,1)} %cache.2), custom_call_target="tpu_custom_call" | custom-call | bytes 6291456 | tf_op jit(solution)/shard_map/load_keys/pallas_call | solution.py:491
  11.4 0.1 collective-permute-done.3
  11.6 3.7 %collective-permute-start.6 = (f32[4,1920]{1,0:T(4,128)S(1)}, f32[4,1920]{1,0:T(4,128)S(1)}, u32[]{:S(2)}, u32[]{:S(2)}) collective-permute-start(f32[4,1920]{1,0:T(4,128)S(1)} %get-tuple-element.61), channel_id=1, source_target_pairs={{0,24},{1,21},{2,26},{3,23},{4,28},{5,17},{6,30},{7,19},{8,16},{9,... | collective-permute-start | bytes 92168 | tf_op jit(solution)/shard_map/ppermute | solution.py:62
  15.3 0.0 collective-permute-start.5
  15.3 0.8 %collective-permute-start.4 = (f32[4,1920]{1,0:T(4,128)S(1)}, f32[4,1920]{1,0:T(4,128)S(1)}, u32[]{:S(2)}, u32[]{:S(2)}) collective-permute-start(f32[4,1920]{1,0:T(4,128)S(1)} %get-tuple-element.63), channel_id=1, source_target_pairs={{0,8},{1,5},{2,10},{3,7},{4,12},{5,1},{6,14},{7,3},{8,0},{9,13},{1... | collective-permute-start | bytes 92168 | tf_op jit(solution)/shard_map/ppermute | solution.py:62
  16.1 0.1 pad_maximum_fusion.1
  16.1 2.4 %load_values.1.refs_11_ = bf16[4,2,4608,128]{3,2,1,0:T(8,128)(2,1)S(1)} custom-call(s32[4,4,128]{2,1,0:T(4,128)S(1)} %broadcast_in_dim.2.plan.refs_0_, bf16[4,2,4096,128]{3,2,1,0:T(8,128)(2,1)} %cache.3), custom_call_target="tpu_custom_call" | custom-call | bytes 6291456 | tf_op jit(solution)/shard_map/load_values/pallas_call | solution.py:491
  18.5 0.0 collective-permute-done.6.refs_4_
  18.5 1.5 %collective-permute-done.5.refs_3_ = f32[4,1920]{1,0:T(4,128)S(1)} collective-permute-done((f32[4,1920]{1,0:T(4,128)S(1)}, f32[4,1920]{1,0:T(4,128)S(1)}, u32[]{:S(2)}, u32[]{:S(2)}) %collective-permute-start.5) | collective-permute-done | bytes 30752 | tf_op jit(solution)/shard_map/ppermute | solution.py:62
  20.1 0.0 collective-permute-done.4.refs_2_
  20.1 0.0 copy-start
  20.1 1.9 %attend.1 = bf16[4,1280]{1,0:T(4,128)(2,1)S(1)} custom-call(s32[4,4,128]{2,1,0:T(4,128)S(1)} %broadcast_in_dim.2.plan.refs_0_, f32[4,1920]{1,0:T(4,128)S(1)} %get-tuple-element.48.refs_1_, f32[4,1920]{1,0:T(4,128)S(1)} %collective-permute-done.4.refs_2_, f32[4,1920]{1,0:T(4,128)S(1)} %collective-permute-done.5.refs_3_, ...), custom_call_target="tpu_custom_call" | custom-call | tf_op jit(solution)/shard_map/attend/pallas_call | solution.py:384
  21.9 1.1 %collective-permute-start.7 = (bf16[4,1280]{1,0:T(4,128)(2,1)S(1)}, bf16[4,1280]{1,0:T(4,128)(2,1)S(1)}, u32[]{:S(2)}, u32[]{:S(2)}) collective-permute-start(bf16[4,1280]{1,0:T(4,128)(2,1)S(1)} %attend.1), channel_id=1, source_target_pairs={{0,4},{1,9},{2,6},{3,11},{4,0},{5,13},{6,2},{7,15},{8,12},{9,1},{1... | collective-permute-start | bytes 30728 | tf_op jit(solution)/shard_map/ppermute | solution.py:62
  23.1 2.6 %collective-permute-done.7 = bf16[4,1280]{1,0:T(4,128)(2,1)S(1)} collective-permute-done((bf16[4,1280]{1,0:T(4,128)(2,1)S(1)}, bf16[4,1280]{1,0:T(4,128)(2,1)S(1)}, u32[]{:S(2)}, u32[]{:S(2)}) %collective-permute-start.7) | collective-permute-done | bytes 10272 | tf_op jit(solution)/shard_map/ppermute | solution.py:62
  25.7 1.2 %collective-permute-start.10 = (bf16[8,1280]{1,0:T(8,128)(2,1)S(1)}, bf16[8,1280]{1,0:T(8,128)(2,1)S(1)}, u32[]{:S(2)}, u32[]{:S(2)}) collective-permute-start(bf16[8,1280]{1,0:T(8,128)(2,1)S(1)} %pad_maximum_fusion.refs_2_), channel_id=1, source_target_pairs={{0,24},{1,21},{2,26},{3,23},{4,28},{5,17},{6,30},{7,19},{8,16},{9,... | collective-permute-start | bytes 61448 | tf_op jit(solution)/shard_map/ppermute | solution.py:62
  26.9 0.0 collective-permute-start.9
  26.9 3.2 %collective-permute-start.8 = (bf16[8,1280]{1,0:T(8,128)(2,1)S(1)}, bf16[8,1280]{1,0:T(8,128)(2,1)S(1)}, u32[]{:S(2)}, u32[]{:S(2)}) collective-permute-start(bf16[8,1280]{1,0:T(8,128)(2,1)S(1)} %pad_maximum_fusion.refs_2_), channel_id=1, source_target_pairs={{0,8},{1,5},{2,10},{3,7},{4,12},{5,1},{6,14},{7,3},{8,0},{9,13},{1... | collective-permute-start | bytes 61448 | tf_op jit(solution)/shard_map/ppermute | solution.py:62
  30.1 1.2 %collective-permute-done.10.refs_5_ = bf16[8,1280]{1,0:T(8,128)(2,1)S(1)} collective-permute-done((bf16[8,1280]{1,0:T(8,128)(2,1)S(1)}, bf16[8,1280]{1,0:T(8,128)(2,1)S(1)}, u32[]{:S(2)}, u32[]{:S(2)}) %collective-permute-start.10) | collective-permute-done | bytes 20512 | tf_op jit(solution)/shard_map/ppermute | solution.py:62
  31.3 0.4 %collective-permute-done.9.refs_4_ = bf16[8,1280]{1,0:T(8,128)(2,1)S(1)} collective-permute-done((bf16[8,1280]{1,0:T(8,128)(2,1)S(1)}, bf16[8,1280]{1,0:T(8,128)(2,1)S(1)}, u32[]{:S(2)}, u32[]{:S(2)}) %collective-permute-start.9) | collective-permute-done | bytes 20512 | tf_op jit(solution)/shard_map/ppermute | solution.py:62
  31.8 0.2 collective-permute-done.8.refs_3_
  32.0 0.0 copy-done
  32.0 0.5 %output.1 = (f32[8,640]{1,0:T(8,128)S(1)}, f32[8,640]{1,0:T(8,128)S(1)}, f32[8,640]{1,0:T(8,128)S(1)}, f32[8,640]{1,0:T(8,128)S(1)}) custom-call(bf16[32,32]{1,0:T(8,128)(2,1)S(1)} %get-tuple-element.32.refs_0_, bf16[1280,640]{1,0:T(8,128)(2,1)S(1)} %copy-done, bf16[8,1280]{1,0:T(8,128)(2,1)S(1)} %pad_maximum_fusion.refs_2_, ...), custom_call_target="tpu_custom_call" | custom-call | tf_op jit(solution)/shard_map/output/pallas_call | solution.py:535
  32.5 0.1 collective-permute-start.11
  32.6 1.5 %collective-permute-start.12 = (f32[8,640]{1,0:T(8,128)S(1)}, f32[8,640]{1,0:T(8,128)S(1)}, u32[]{:S(2)}, u32[]{:S(2)}) collective-permute-start(f32[8,640]{1,0:T(8,128)S(1)} %get-tuple-element.57), channel_id=1, source_target_pairs={{0,2},{1,3},{2,0},{3,1},{4,6},{5,7},{6,4},{7,5},{8,10},{9,11},{10,... | collective-permute-start | bytes 61448 | tf_op jit(solution)/shard_map/ppermute | solution.py:66
  34.1 0.3 collective-permute-start.13
  34.4 1.6 %collective-permute-done.11 = f32[8,640]{1,0:T(8,128)S(1)} collective-permute-done((f32[8,640]{1,0:T(8,128)S(1)}, f32[8,640]{1,0:T(8,128)S(1)}, u32[]{:S(2)}, u32[]{:S(2)}) %collective-permute-start.11) | collective-permute-done | bytes 20512 | tf_op jit(solution)/shard_map/ppermute | solution.py:66
  36.0 0.4 %collective-permute-done.12 = f32[8,640]{1,0:T(8,128)S(1)} collective-permute-done((f32[8,640]{1,0:T(8,128)S(1)}, f32[8,640]{1,0:T(8,128)S(1)}, u32[]{:S(2)}, u32[]{:S(2)}) %collective-permute-start.12) | collective-permute-done | bytes 20512 | tf_op jit(solution)/shard_map/ppermute | solution.py:66
  36.4 0.0 collective-permute-done.13
  36.4 0.6 %add_convert_fusion = bf16[8,640]{1,0:T(8,128)(2,1)} fusion(f32[8,640]{1,0:T(8,128)S(1)} %collective-permute-done.13, f32[8,640]{1,0:T(8,128)S(1)} %collective-permute-done.12, f32[8,640]{1,0:T(8,128)S(1)} %get-tuple-element.55, f32[8,640]{1,0:T(8,128)S(1)} %collective-permute-done.11), kind=kLoop, calls=%fused_computation.1 | loop fusion | flops 20480 | bytes 92160 | tf_op jit(solution)/shard_map/convert_element_type | solution.py:546
  (7 shorter events, 0.1 us)
Async XLA Ops:
  0.0 4.8 %collective-permute-start.1 = (bf16[8,640]{1,0:T(8,128)(2,1)}, bf16[8,640]{1,0:T(8,128)(2,1)S(1)}, u32[]{:S(2)}, u32[]{:S(2)}) collective-permute-start(bf16[8,640]{1,0:T(8,128)(2,1)} %refs_5_.1), channel_id=1, source_target_pairs={{0,3},{1,2},{2,1},{3,0},{4,7},{5,6},{6,5},{7,4},{8,11},{9,10},{10,... | collective-permute-start | bytes 30728 | tf_op jit(solution)/shard_map/ppermute | solution.py:66
  2.4 2.5 %collective-permute-start = (bf16[8,640]{1,0:T(8,128)(2,1)}, bf16[8,640]{1,0:T(8,128)(2,1)S(1)}, u32[]{:S(2)}, u32[]{:S(2)}) collective-permute-start(bf16[8,640]{1,0:T(8,128)(2,1)} %refs_5_.1), channel_id=1, source_target_pairs={{0,1},{1,0},{2,3},{3,2},{4,5},{5,4},{6,7},{7,6},{8,9},{9,8},{10,11... | collective-permute-start | bytes 30728 | tf_op jit(solution)/shard_map/ppermute | solution.py:66
  4.8 1.2 %collective-permute-start.2 = (bf16[8,640]{1,0:T(8,128)(2,1)S(1)}, bf16[8,640]{1,0:T(8,128)(2,1)S(1)}, u32[]{:S(2)}, u32[]{:S(2)}) collective-permute-start(bf16[8,640]{1,0:T(8,128)(2,1)S(1)} %collective-permute-done.1.refs_3_), channel_id=1, source_target_pairs={{0,1},{1,0},{2,3},{3,2},{4,5},{5,4},{6,7},{7,6},{8,9},{9,8},{10,11... | collective-permute-start | bytes 30728 | tf_op jit(solution)/shard_map/ppermute | solution.py:66
  6.6 4.9 %collective-permute-start.3 = (f32[16,1920]{1,0:T(8,128)S(1)}, f32[16,1920]{1,0:T(8,128)S(1)}, u32[]{:S(2)}, u32[]{:S(2)}) collective-permute-start(f32[16,1920]{1,0:T(8,128)S(1)} %get-tuple-element.46), channel_id=1, source_target_pairs={{0,4},{1,9},{2,6},{3,11},{4,0},{5,13},{6,2},{7,15},{8,12},{9,1},{1... | collective-permute-start | bytes 368648 | tf_op jit(solution)/shard_map/ppermute | solution.py:62
  11.6 6.9 %collective-permute-start.6 = (f32[4,1920]{1,0:T(4,128)S(1)}, f32[4,1920]{1,0:T(4,128)S(1)}, u32[]{:S(2)}, u32[]{:S(2)}) collective-permute-start(f32[4,1920]{1,0:T(4,128)S(1)} %get-tuple-element.61), channel_id=1, source_target_pairs={{0,24},{1,21},{2,26},{3,23},{4,28},{5,17},{6,30},{7,19},{8,16},{9,... | collective-permute-start | bytes 92168 | tf_op jit(solution)/shard_map/ppermute | solution.py:62
  15.3 4.8 %collective-permute-start.5 = (f32[4,1920]{1,0:T(4,128)S(1)}, f32[4,1920]{1,0:T(4,128)S(1)}, u32[]{:S(2)}, u32[]{:S(2)}) collective-permute-start(f32[4,1920]{1,0:T(4,128)S(1)} %get-tuple-element.62), channel_id=1, source_target_pairs={{0,16},{1,17},{2,18},{3,19},{4,20},{5,21},{6,22},{7,23},{8,24},{9,... | collective-permute-start | bytes 92168 | tf_op jit(solution)/shard_map/ppermute | solution.py:62
  15.3 4.8 %collective-permute-start.4 = (f32[4,1920]{1,0:T(4,128)S(1)}, f32[4,1920]{1,0:T(4,128)S(1)}, u32[]{:S(2)}, u32[]{:S(2)}) collective-permute-start(f32[4,1920]{1,0:T(4,128)S(1)} %get-tuple-element.63), channel_id=1, source_target_pairs={{0,8},{1,5},{2,10},{3,7},{4,12},{5,1},{6,14},{7,3},{8,0},{9,13},{1... | collective-permute-start | bytes 92168 | tf_op jit(solution)/shard_map/ppermute | solution.py:62
  20.1 11.9 %copy-start = (bf16[1280,640]{1,0:T(8,128)(2,1)S(1)}, bf16[1280,640]{1,0:T(8,128)(2,1)}, u32[]{:S(2)}) copy-start(bf16[1280,640]{1,0:T(8,128)(2,1)} %refs_1_.3) | copy-start | bytes 4915204
  21.9 3.7 %collective-permute-start.7 = (bf16[4,1280]{1,0:T(4,128)(2,1)S(1)}, bf16[4,1280]{1,0:T(4,128)(2,1)S(1)}, u32[]{:S(2)}, u32[]{:S(2)}) collective-permute-start(bf16[4,1280]{1,0:T(4,128)(2,1)S(1)} %attend.1), channel_id=1, source_target_pairs={{0,4},{1,9},{2,6},{3,11},{4,0},{5,13},{6,2},{7,15},{8,12},{9,1},{1... | collective-permute-start | bytes 30728 | tf_op jit(solution)/shard_map/ppermute | solution.py:62
  25.7 5.6 %collective-permute-start.10 = (bf16[8,1280]{1,0:T(8,128)(2,1)S(1)}, bf16[8,1280]{1,0:T(8,128)(2,1)S(1)}, u32[]{:S(2)}, u32[]{:S(2)}) collective-permute-start(bf16[8,1280]{1,0:T(8,128)(2,1)S(1)} %pad_maximum_fusion.refs_2_), channel_id=1, source_target_pairs={{0,24},{1,21},{2,26},{3,23},{4,28},{5,17},{6,30},{7,19},{8,16},{9,... | collective-permute-start | bytes 61448 | tf_op jit(solution)/shard_map/ppermute | solution.py:62
  26.9 4.8 %collective-permute-start.9 = (bf16[8,1280]{1,0:T(8,128)(2,1)S(1)}, bf16[8,1280]{1,0:T(8,128)(2,1)S(1)}, u32[]{:S(2)}, u32[]{:S(2)}) collective-permute-start(bf16[8,1280]{1,0:T(8,128)(2,1)S(1)} %pad_maximum_fusion.refs_2_), channel_id=1, source_target_pairs={{0,16},{1,17},{2,18},{3,19},{4,20},{5,21},{6,22},{7,23},{8,24},{9,... | collective-permute-start | bytes 61448 | tf_op jit(solution)/shard_map/ppermute | solution.py:62
  26.9 5.1 %collective-permute-start.8 = (bf16[8,1280]{1,0:T(8,128)(2,1)S(1)}, bf16[8,1280]{1,0:T(8,128)(2,1)S(1)}, u32[]{:S(2)}, u32[]{:S(2)}) collective-permute-start(bf16[8,1280]{1,0:T(8,128)(2,1)S(1)} %pad_maximum_fusion.refs_2_), channel_id=1, source_target_pairs={{0,8},{1,5},{2,10},{3,7},{4,12},{5,1},{6,14},{7,3},{8,0},{9,13},{1... | collective-permute-start | bytes 61448 | tf_op jit(solution)/shard_map/ppermute | solution.py:62
  32.5 3.5 %collective-permute-start.11 = (f32[8,640]{1,0:T(8,128)S(1)}, f32[8,640]{1,0:T(8,128)S(1)}, u32[]{:S(2)}, u32[]{:S(2)}) collective-permute-start(f32[8,640]{1,0:T(8,128)S(1)} %get-tuple-element.56), channel_id=1, source_target_pairs={{0,3},{1,2},{2,1},{3,0},{4,7},{5,6},{6,5},{7,4},{8,11},{9,10},{10,... | collective-permute-start | bytes 61448 | tf_op jit(solution)/shard_map/ppermute | solution.py:66
  32.6 3.8 %collective-permute-start.12 = (f32[8,640]{1,0:T(8,128)S(1)}, f32[8,640]{1,0:T(8,128)S(1)}, u32[]{:S(2)}, u32[]{:S(2)}) collective-permute-start(f32[8,640]{1,0:T(8,128)S(1)} %get-tuple-element.57), channel_id=1, source_target_pairs={{0,2},{1,3},{2,0},{3,1},{4,6},{5,7},{6,4},{7,5},{8,10},{9,11},{10,... | collective-permute-start | bytes 61448 | tf_op jit(solution)/shard_map/ppermute | solution.py:66
  34.1 2.3 %collective-permute-start.13 = (f32[8,640]{1,0:T(8,128)S(1)}, f32[8,640]{1,0:T(8,128)S(1)}, u32[]{:S(2)}, u32[]{:S(2)}) collective-permute-start(f32[8,640]{1,0:T(8,128)S(1)} %get-tuple-element.58), channel_id=1, source_target_pairs={{0,1},{1,0},{2,3},{3,2},{4,5},{5,4},{6,7},{7,6},{8,9},{9,8},{10,11... | collective-permute-start | bytes 61448 | tf_op jit(solution)/shard_map/ppermute | solution.py:66
